TPU v7x, 128 devices: a whole 4x4x4 slice. The times are simulated.
128 devices in a mesh: tower: 2 (over core), tm: 8 (over z, y_hi), tensor: 8 (over y_lo, x).
Axes of the slice: x: 4, y: 4 (y_hi: 2, y_lo: 2; y = y_hi * 2 + y_lo), z: 4, core: 2. Of those that a mesh axis runs over, the one named last changes fastest.
Arguments:
- video_tokens: bfloat16 [24576, 3072], P(('tower', 'tm'), 'tensor')
- audio_tokens: bfloat16 [512, 3072], P(('tower', 'tm'), 'tensor')
- w_query: bfloat16 [2, 3072, 3072], P(None, None, 'tensor'), may hold values from -0.109375 to 0.109375
- w_key: bfloat16 [2, 3072, 3072], P(None, None, 'tensor'), may hold values from -0.109375 to 0.109375
- w_value: bfloat16 [2, 3072, 3072], P(None, None, 'tensor'), may hold values from -0.109375 to 0.109375
- w_out: bfloat16 [2, 3072, 3072], P(None, 'tensor'), may hold values from -2.5 to 2.5
- video_counts: int32 [16], replicated, may hold values from 1440 to 1536, as said below
- audio_counts: int32 [16], replicated, may hold values from 28 to 32, as said below
- video_windows: int32 [16, 2], replicated, may hold values from 4 to 8
- audio_windows: int32 [16, 2], replicated, may hold values from 192 to 384
Outputs:
- video_update: bfloat16 [24576, 3072], P(('tower', 'tm'), 'tensor')
- audio_update: bfloat16 [512, 3072], P(('tower', 'tm'), 'tensor')
Inputs may be any that keep to these rules, and one draw needn't show every extreme that they name: `video_counts`: valid video tokens lie at the start of their time shard. `audio_counts`: valid audio tokens lie at the start of their time shard.
All inputs are finite; a program needn't handle non-finite values.
Results may differ from a plain program's by a relative error of at most 0.019.
Values may be sent and summed in bfloat16 or wider, within the bound.
No kernel may reach another device: no remote copies, remote signals or barrier semaphores. Data moves between devices by JAX's collectives and lax.ppermute only.
A program may use at most 128 MiB of HBM per device.

v0:
```python
import math

import jax
import jax.numpy as jnp
from jax import lax
from jax.sharding import PartitionSpec as P

HEAD = 128


epsilon = 1e-06


def padded(array, sides, width):
    for axis, dim in sides:
        count, length = (lax.axis_size(axis), array.shape[dim])
        up = [(i, (i + 1) % count) for i in range(count - 1)]
        down = [(j, i) for i, j in up]
        last = lax.slice_in_dim(array, length - width, length, axis=dim)
        initial = lax.slice_in_dim(array, 0, width, axis=dim)
        before = lax.ppermute(last, axis, up)
        after = lax.ppermute(initial, axis, down)
        array = jnp.concatenate([before, array, after], axis=dim)
    return array


def layer_norm(row_block):
    values = row_block.astype(jnp.float32)
    centred = values - jnp.mean(values, axis=-1, keepdims=True)
    spread = jnp.mean(centred * centred, axis=-1, keepdims=True)
    return (centred * lax.rsqrt(spread + epsilon)).astype(jnp.bfloat16)


def head_norm(product, head_size):
    shaped = product.reshape(product.shape[0], -1, head_size)
    mean_square = jnp.mean(shaped * shaped, axis=-1, keepdims=True)
    return (shaped * lax.rsqrt(mean_square + epsilon)).reshape(product.shape).astype(jnp.bfloat16)


def lookup(table, position):
    return lax.dynamic_index_in_dim(table, position, 0, keepdims=False)


def key_mask(shard_index, shard_count, key_dev, key_reach, key_counts, reaches):
    span_rows = key_dev + 2 * key_reach
    first_slot = shard_index * key_dev
    position = first_slot - key_reach + jnp.arange(span_rows, dtype=jnp.int32)
    total_rows = key_dev * shard_count
    clipped = jnp.clip(position, 0, total_rows - 1)
    owner_shard = clipped // key_dev
    local_slot = clipped % key_dev
    shard_ids = jnp.arange(shard_count, dtype=jnp.int32)
    count_limit = jnp.sum(
        jnp.where(owner_shard[:, None] == shard_ids[None, :], key_counts[None, :], 0), axis=1
    )
    used_keys = (position >= 0) & (position < total_rows) & (local_slot < count_limit)
    return (
        used_keys
        & (position >= first_slot - reaches[0])
        & (position < first_slot + key_dev + reaches[1])
    )


def shards(
    video_tokens,
    audio_tokens,
    w_query,
    w_key,
    w_value,
    w_out,
    video_counts,
    audio_counts,
    video_windows,
    audio_windows,
):
    shard_index = lax.axis_index(("tower", "tm"))
    shard_count = lax.axis_size(("tower", "tm"))
    video_rows, audio_rows = (
        lax.all_gather(video_tokens, "tensor", axis=1, tiled=True),
        lax.all_gather(audio_tokens, "tensor", axis=1, tiled=True),
    )
    video_normed = layer_norm(video_rows)
    audio_normed = layer_norm(audio_rows)
    vid_rows = video_rows.shape[0]
    aud_rows = audio_rows.shape[0]
    heads_here = w_query.shape[2] // HEAD
    score_scale = 1.0 / math.sqrt(HEAD)
    video_queries = head_norm(
        jnp.dot(video_normed, w_query[0], preferred_element_type=jnp.float32), HEAD
    )
    audio_queries = head_norm(
        jnp.dot(audio_normed, w_query[1], preferred_element_type=jnp.float32), HEAD
    )

    def project_pair(row_block, tower_pos):
        key_part = head_norm(
            jnp.dot(row_block, w_key[tower_pos], preferred_element_type=jnp.float32), HEAD
        )
        value_part = jnp.dot(
            row_block, w_value[tower_pos], preferred_element_type=jnp.float32
        ).astype(jnp.bfloat16)
        return jnp.stack([key_part, value_part], axis=1)

    aud_reach = aud_rows // 4
    vid_reach = vid_rows // 4
    audio_pairs = padded(project_pair(audio_normed, 0), ((("tower", "tm"), 0),), aud_reach)
    video_pairs = padded(project_pair(video_normed, 1), ((("tower", "tm"), 0),), vid_reach)
    audio_span = aud_rows + 2 * aud_reach
    video_span = vid_rows + 2 * vid_reach
    audio_key_heads = audio_pairs[:, 0].reshape(audio_span, heads_here, HEAD)
    audio_value_heads = audio_pairs[:, 1].reshape(audio_span, heads_here, HEAD)
    video_key_heads = video_pairs[:, 0].reshape(video_span, heads_here, HEAD)
    video_value_heads = video_pairs[:, 1].reshape(video_span, heads_here, HEAD)
    audio_used = key_mask(
        shard_index,
        shard_count,
        aud_rows,
        aud_reach,
        audio_counts,
        lookup(video_windows, shard_index),
    )
    video_used = key_mask(
        shard_index,
        shard_count,
        vid_rows,
        vid_reach,
        video_counts,
        lookup(audio_windows, shard_index),
    )
    block_rows = min(512, vid_rows)

    def attend_video(query_block):
        shaped = query_block.reshape(block_rows, heads_here, HEAD)
        scores = (
            jnp.einsum("qhd,khd->hkq", shaped, audio_key_heads, preferred_element_type=jnp.float32)
            * score_scale
        )
        weights = jnp.where(audio_used[None, :, None], jnp.exp(scores), 0.0)
        denominator = jnp.sum(weights, axis=1, keepdims=True)
        probabilities = (weights / denominator).astype(jnp.bfloat16)
        mixed_heads = jnp.einsum(
            "hkq,khd->qhd", probabilities, audio_value_heads, preferred_element_type=jnp.float32
        )
        return mixed_heads.astype(jnp.bfloat16).reshape(block_rows, heads_here * HEAD)

    video_attended = lax.map(
        attend_video, video_queries.reshape(vid_rows // block_rows, block_rows, -1)
    ).reshape(vid_rows, -1)
    audio_shaped = audio_queries.reshape(aud_rows, heads_here, HEAD)
    audio_scores = (
        jnp.einsum(
            "qhd,khd->hqk", audio_shaped, video_key_heads, preferred_element_type=jnp.float32
        )
        * score_scale
    )
    audio_weights = jnp.where(video_used[None, None, :], jnp.exp(audio_scores), 0.0)
    audio_total = jnp.sum(audio_weights, axis=-1, keepdims=True)
    audio_probabilities = (audio_weights / audio_total).astype(jnp.bfloat16)
    audio_mixed = jnp.einsum(
        "hqk,khd->qhd", audio_probabilities, video_value_heads, preferred_element_type=jnp.float32
    )
    audio_attended = audio_mixed.astype(jnp.bfloat16).reshape(aud_rows, heads_here * HEAD)
    video_partial = jnp.dot(video_attended, w_out[0], preferred_element_type=jnp.float32)
    audio_partial = jnp.dot(audio_attended, w_out[1], preferred_element_type=jnp.float32)
    video_summed, audio_summed = (
        lax.psum_scatter(
            video_partial.astype(jnp.bfloat16), "tensor", scatter_dimension=1, tiled=True
        ).astype(jnp.float32),
        lax.psum_scatter(
            audio_partial.astype(jnp.bfloat16), "tensor", scatter_dimension=1, tiled=True
        ).astype(jnp.float32),
    )
    video_limit = lookup(video_counts, shard_index)
    audio_limit = lookup(audio_counts, shard_index)
    video_valid = jnp.arange(vid_rows, dtype=jnp.int32) < video_limit
    audio_valid = jnp.arange(aud_rows, dtype=jnp.int32) < audio_limit
    video_update = jnp.where(video_valid[:, None], video_summed, 0.0).astype(jnp.bfloat16)
    audio_update = jnp.where(audio_valid[:, None], audio_summed, 0.0).astype(jnp.bfloat16)
    return (video_update, audio_update)


def solution(mesh):
    in_specs = (
        P(("tower", "tm"), "tensor"),
        P(("tower", "tm"), "tensor"),
        P(None, None, "tensor"),
        P(None, None, "tensor"),
        P(None, None, "tensor"),
        P(None, "tensor", None),
        P(),
        P(),
        P(),
        P(),
    )
    out_specs = (P(("tower", "tm"), "tensor"), P(("tower", "tm"), "tensor"))
    return jax.shard_map(shards, mesh=mesh, in_specs=in_specs, out_specs=out_specs, check_vma=False)
```

profile of v0, /device:TPU:0, one launch (start us, length us, event | category | flops | bytes accessed | tf_op | source)
XLA Modules:
  0.0 364.7 jit_solution(17164299229992713921)
XLA Ops:
  7.9 5.1 %slice_bitcast_fusion.1 = (bf16[384,3072]{0,1:T(8,128)(2,1)}, bf16[384,3072]{0,1:T(8,128)(2,1)}) fusion(bf16[2,3072,384]{2,1,0:T(8,128)(2,1)} %param.15), kind=kLoop, calls=%fused_computation.38 | loop fusion | bytes 9437184 | tf_op jit(solution)/shard_map/dot_general | solution.py:97
  13.0 2.8 copy.59
  15.9 29.3 %all_gather.7 = bf16[32,3072]{1,0:T(8,128)(2,1)S(1)} all-gather(bf16[32,384]{1,0:T(8,128)(2,1)S(1)} %copy-done.7), channel_id=1, replica_groups=mesh['tower'=2,'tm'=8,'tensor'=8] {'tensor'}, dimensions={1}, use_global_device_ids=true | all-gather | bytes 221184 | tf_op jit(solution)/shard_map/all_gather | solution.py:80
  46.7 2.2 fusion.30
  48.9 4.8 %collective-permute-start = (bf16[8,2,384]{2,0,1:T(8,128)(2,1)S(1)}, bf16[8,2,384]{2,0,1:T(8,128)(2,1)S(1)}, u32[]{:S(2)}, u32[]{:S(2)}) collective-permute-start(bf16[8,2,384]{2,0,1:T(8,128)(2,1)S(1)} %get-tuple-element.81), channel_id=1, source_target_pairs={{0,8},{8,16},{16,24},{24,32},{32,40},{40,48},{48,56},{56,64},{64,7... | collective-permute-start | bytes 36872 | tf_op jit(solution)/shard_map/ppermute | solution.py:21
  57.5 5.2 %slice_bitcast_fusion = (bf16[384,3072]{0,1:T(8,128)(2,1)}, bf16[384,3072]{0,1:T(8,128)(2,1)}) fusion(bf16[2,3072,384]{2,1,0:T(8,128)(2,1)} %param.14), kind=kLoop, calls=%fused_computation.34 | loop fusion | bytes 9437184 | tf_op jit(solution)/shard_map/dot_general | solution.py:92
  62.7 2.9 copy.68
  68.5 4.4 %copy.57 = bf16[384,3072]{1,0:T(8,128)(2,1)} copy(bf16[384,3072]{0,1:T(8,128)(2,1)} %get-tuple-element.72) | data formatting | bytes 4718592 | tf_op jit(solution)/shard_map/dot_general | solution.py:89
  73.0 2.6 copy.65
  75.6 41.8 %collective-permute-done.1 = bf16[8,2,384]{2,0,1:T(8,128)(2,1)S(1)} collective-permute-done((bf16[8,2,384]{2,0,1:T(8,128)(2,1)S(1)}, bf16[8,2,384]{2,0,1:T(8,128)(2,1)S(1)}, u32[]{:S(2)}, u32[]{:S(2)}) %collective-permute-start.1) | collective-permute-done | bytes 12320 | tf_op jit(solution)/shard_map/ppermute | solution.py:22
  117.5 5.1 %convert_reduce_fusion = f32[1536]{0:T(1024)S(1)} fusion(bf16[1536,3072]{1,0:T(8,128)(2,1)} %all-gather.2.cloned.1.call-done), kind=kLoop, calls=%fused_computation.11 | loop fusion | flops 9435648 | bytes 9443328 | tf_op jit(solution)/shard_map/reduce_sum | solution.py:29
  123.9 2.6 fusion.8
  126.5 12.0 %fusion.9 = bf16[1536,3072]{1,0:T(8,128)(2,1)} fusion(bf16[1536,3072]{1,0:T(8,128)(2,1)} %all-gather.2.cloned.1.call-done, f32[1536]{0:T(1024)S(1)} %add_rsqrt_fusion.2, f32[1536]{0:T(1024)S(1)} %broadcast_multiply_fusion), kind=kLoop, calls=%fused_computation.15 | loop fusion | flops 18874368 | bytes 18886656 | tf_op jit(solution)/shard_map/convert_element_type | solution.py:31
  138.5 9.5 %fusion.16 = bf16[1536,1,384]{2,0,1:T(8,128)(2,1)} fusion(bf16[1536,3072]{1,0:T(8,128)(2,1)} %fusion.9, bf16[2,3072,384]{2,1,0:T(8,128)(2,1)} %param.16), kind=kOutput, calls=%fused_computation.27 | convolution fusion | flops 3624468480 | bytes 12976128 | tf_op jit(solution)/shard_map/dot_general | solution.py:99
  148.0 3.9 %multiply_reduce_fusion.1 = (f32[1536,3]{0,1:T(4,128)S(1)}, f32[1536,3,128]{0,2,1:T(8,128)S(1)}) fusion(bf16[3,128,3072]{2,1,0:T(8,128)(2,1)S(1)} %bitcast.126, bf16[1536,3072]{1,0:T(8,128)(2,1)S(1)} %copy-done.1), kind=kOutput, calls=%fused_computation.44 | convolution fusion | flops 3625053696 | bytes 14174208 | tf_op jit(solution)/shard_map/dot_general | solution.py:89
  154.7 6.4 %multiply_reduce_fusion = (f32[1536,3]{0,1:T(4,128)S(1)}, f32[1536,3,128]{0,2,1:T(8,128)S(1)}) fusion(bf16[3,128,3072]{2,1,0:T(8,128)(2,1)S(1)} %bitcast.125, bf16[1536,3072]{1,0:T(8,128)(2,1)} %fusion.9), kind=kOutput, calls=%fused_computation.37 | convolution fusion | flops 3625053696 | bytes 14174208 | tf_op jit(solution)/shard_map/dot_general | solution.py:97
  162.4 1.7 copy.66
  164.1 2.2 pad_maximum_fusion.2
  166.3 4.2 %collective-permute-start.2 = (bf16[384,2,384]{2,0,1:T(8,128)(2,1)}, bf16[384,2,384]{2,0,1:T(8,128)(2,1)}, u32[]{:S(2)}, u32[]{:S(2)}) collective-permute-start(bf16[384,2,384]{2,0,1:T(8,128)(2,1)} %get-tuple-element.77), channel_id=1, source_target_pairs={{0,8},{8,16},{16,24},{24,32},{32,40},{40,48},{48,56},{56,64},{64,7... | collective-permute-start | bytes 1769480 | tf_op jit(solution)/shard_map/ppermute | solution.py:21
  171.9 4.7 %while.10 = (s32[]{:T(128)}, bf16[3,512,384]{2,1,0:T(8,128)(2,1)}, pred[48]{0:T(512)(128)(4,1)S(1)}, bf16[3,512,384]{1,2,0:T(8,128)(2,1)S(1)}, bf16[48,3,128]{2,...) while((s32[]{:T(128)}, bf16[3,512,384]{2,1,0:T(8,128)(2,1)}, pred[48]{0:T(512)(128)(4,1)S(1)}, ...), condition=%wide.region_9.10_spmd, body=%wide.region_7.9_spmd.sunk | while | flops 38241840 | bytes 3809421 | solution.py:146
  176.6 7.2 %collective-permute-done.2 = bf16[384,2,384]{2,0,1:T(8,128)(2,1)} collective-permute-done((bf16[384,2,384]{2,0,1:T(8,128)(2,1)}, bf16[384,2,384]{2,0,1:T(8,128)(2,1)}, u32[]{:S(2)}, u32[]{:S(2)}) %collective-permute-start.2) | collective-permute-done | bytes 589856 | tf_op jit(solution)/shard_map/ppermute | solution.py:21
  183.8 15.2 %collective-permute-done.3 = bf16[384,2,384]{2,0,1:T(8,128)(2,1)} collective-permute-done((bf16[384,2,384]{2,0,1:T(8,128)(2,1)}, bf16[384,2,384]{2,0,1:T(8,128)(2,1)}, u32[]{:S(2)}, u32[]{:S(2)}) %collective-permute-start.3) | collective-permute-done | bytes 589856 | tf_op jit(solution)/shard_map/ppermute | solution.py:22
  198.9 4.1 %pad_maximum_fusion = bf16[2304,2,384]{2,0,1:T(8,128)(2,1)S(1)} fusion(bf16[384,2,384]{2,0,1:T(8,128)(2,1)} %collective-permute-done.3, bf16[1536,1,384]{2,0,1:T(8,128)(2,1)} %fusion.16, bf16[1536,1,384]{2,0,1:T(8,128)(2,1)S(1)} %copy.66, bf16[384,2,384]{2,0,1:T(8,128)(2,1)} %collective-permute-done.2), kind=kLoop, calls=%fused_computation.24 | loop fusion | flops 14155776 | bytes 7077888 | tf_op jit(solution)/shard_map/concatenate | solution.py:23
  203.4 2.4 copy.69
  205.7 2.4 copy.67
  208.1 2.3 fusion.15
  210.4 2.2 fusion.29
  212.5 2.3 convolution_convert_fusion.2
  216.1 9.3 %convolution_convert_fusion.1 = bf16[1536,3072]{1,0:T(8,128)(2,1)} fusion(bf16[1536,384]{1,0:T(8,128)(2,1)S(1)} %bitcast.130, bf16[2,384,3072]{2,1,0:T(8,128)(2,1)} %param.17), kind=kOutput, calls=%fused_computation.16 | convolution fusion | flops 3628597248 | bytes 12976128 | tf_op jit(solution)/shard_map/dot_general | solution.py:163
  225.4 12.7 %copy.78 = bf16[1536,3072]{0,1:T(8,128)(2,1)} copy(bf16[1536,3072]{1,0:T(8,128)(2,1)} %convolution_convert_fusion.1) | data formatting | bytes 18874368
  240.7 10.3 %reduce-scatter.9.cloned.1.call-done = bf16[384,32]{1,0:T(8,128)(2,1)} async-done(((bf16[3072,32]{1,0:T(8,128)(2,1)}), bf16[384,32]{1,0:T(8,128)(2,1)}) %reduce-scatter.9.cloned.1.call-update) | async-done | bytes 24592
  252.7 102.3 %reduce-scatter.7.cloned.1.call-done = bf16[384,1536]{1,0:T(8,128)(2,1)} async-done(((bf16[3072,1536]{1,0:T(8,128)(2,1)}), bf16[384,1536]{1,0:T(8,128)(2,1)}) %reduce-scatter.7.cloned.1.call-update) | async-done | bytes 1179664
  (97 shorter events, 26.6 us)
Async XLA Ops:
  7.2 110.4 %all-gather.2.cloned.1.call-start = ((), (), s32[]{:S(2)}) async-start(), calls=%async_computation.2 | async-start | bytes 10616832 | tf_op jit(solution)/shard_map/all_gather | solution.py:79
  7.9 243.1 %reduce-scatter.9.cloned.1.call-start = ((), (), s32[]{:S(2)}) async-start(), calls=%async_computation.4 | async-start | bytes 884736
  13.0 2.9 copy-start.7
  45.6 9.4 %copy-start.8 = (s32[16,2]{0,1:T(2,128)S(1)}, s32[16,2]{0,1:T(2,128)}, u32[]{:S(2)}) copy-start(s32[16,2]{0,1:T(2,128)} %param.21) | copy-start | bytes 388
  45.6 9.4 %copy-start.9 = (s32[16,2]{0,1:T(2,128)S(1)}, s32[16,2]{0,1:T(2,128)}, u32[]{:S(2)}) copy-start(s32[16,2]{0,1:T(2,128)} %param.20) | copy-start | bytes 388
  48.9 26.7 %collective-permute-start = (bf16[8,2,384]{2,0,1:T(8,128)(2,1)S(1)}, bf16[8,2,384]{2,0,1:T(8,128)(2,1)S(1)}, u32[]{:S(2)}, u32[]{:S(2)}) collective-permute-start(bf16[8,2,384]{2,0,1:T(8,128)(2,1)S(1)} %get-tuple-element.81), channel_id=1, source_target_pairs={{0,8},{8,16},{16,24},{24,32},{32,40},{40,48},{48,56},{56,64},{64,7... | collective-permute-start | bytes 36872 | tf_op jit(solution)/shard_map/ppermute | solution.py:21
  53.7 63.7 %collective-permute-start.1 = (bf16[8,2,384]{2,0,1:T(8,128)(2,1)S(1)}, bf16[8,2,384]{2,0,1:T(8,128)(2,1)S(1)}, u32[]{:S(2)}, u32[]{:S(2)}) collective-permute-start(bf16[8,2,384]{2,0,1:T(8,128)(2,1)S(1)} %get-tuple-element.82), channel_id=1, source_target_pairs={{8,0},{16,8},{24,16},{32,24},{40,32},{48,40},{56,48},{64,56},{72,6... | collective-permute-start | bytes 36872 | tf_op jit(solution)/shard_map/ppermute | solution.py:22
  62.7 4.1 %copy-start.12 = (s32[16]{0:T(128)S(1)}, s32[16]{0:T(128)}, u32[]{:S(2)}) copy-start(s32[16]{0:T(128)} %param.19) | copy-start | bytes 196
  62.7 4.2 %copy-start.10 = (s32[16]{0:T(128)S(1)}, s32[16]{0:T(128)}, u32[]{:S(2)}) copy-start(s32[16]{0:T(128)} %param.18) | copy-start | bytes 196
  68.5 4.4 %copy-start.2 = (bf16[384,3072]{0,1:T(8,128)(2,1)S(1)}, bf16[384,3072]{0,1:T(8,128)(2,1)}, u32[]{:S(2)}) copy-start(bf16[384,3072]{0,1:T(8,128)(2,1)} %get-tuple-element.73) | copy-start | bytes 7077892
  117.5 6.4 %copy-start = (bf16[1536,3072]{1,0:T(8,128)(2,1)S(1)}, bf16[1536,3072]{1,0:T(8,128)(2,1)}, u32[]{:S(2)}) copy-start(bf16[1536,3072]{1,0:T(8,128)(2,1)} %all-gather.2.cloned.1.call-done) | copy-start | bytes 28311556
  138.5 9.5 %copy-start.1 = (bf16[1536,3072]{1,0:T(8,128)(2,1)S(1)}, bf16[1536,3072]{1,0:T(8,128)(2,1)}, u32[]{:S(2)}) copy-start(bf16[1536,3072]{1,0:T(8,128)(2,1)} %fusion.9) | copy-start | bytes 28311556
  138.5 9.5 %copy-start.5 = (bf16[384,3072]{1,0:T(8,128)(2,1)S(1)}, bf16[384,3072]{1,0:T(8,128)(2,1)}, u32[]{:S(2)}) copy-start(bf16[384,3072]{1,0:T(8,128)(2,1)} %copy.57) | copy-start | bytes 7077892
  153.0 1.7 copy-start.4
  166.3 17.4 %collective-permute-start.2 = (bf16[384,2,384]{2,0,1:T(8,128)(2,1)}, bf16[384,2,384]{2,0,1:T(8,128)(2,1)}, u32[]{:S(2)}, u32[]{:S(2)}) collective-permute-start(bf16[384,2,384]{2,0,1:T(8,128)(2,1)} %get-tuple-element.77), channel_id=1, source_target_pairs={{0,8},{8,16},{16,24},{24,32},{32,40},{40,48},{48,56},{56,64},{64,7... | collective-permute-start | bytes 1769480 | tf_op jit(solution)/shard_map/ppermute | solution.py:21
  170.6 28.3 %collective-permute-start.3 = (bf16[384,2,384]{2,0,1:T(8,128)(2,1)}, bf16[384,2,384]{2,0,1:T(8,128)(2,1)}, u32[]{:S(2)}, u32[]{:S(2)}) collective-permute-start(bf16[384,2,384]{2,0,1:T(8,128)(2,1)} %get-tuple-element.78), channel_id=1, source_target_pairs={{8,0},{16,8},{24,16},{32,24},{40,32},{48,40},{56,48},{64,56},{72,6... | collective-permute-start | bytes 1769480 | tf_op jit(solution)/shard_map/ppermute | solution.py:22
  205.7 2.4 copy-start.3
  208.1 2.3 copy-start.6
  212.5 3.6 copy-start.11
  216.1 138.9 %reduce-scatter.7.cloned.1.call-start = ((), (), s32[]{:S(2)}) async-start(), calls=%async_computation.3 | async-start | bytes 10616832
Sparse Core Ops, SparseCore 0:
  9.7 106.3 all-gather.1
  216.2 34.7 reduce-scatter.8
  253.6 101.4 reduce-scatter.6
where the time goes:
time: 367 us; the launch traced here: 365 us
  waiting for transfers between devices  178 us (49%)
  local copies, waits for them, and re-layouts  55.7 us (15%)
  matrix products  41.9 us (11%)
  other arithmetic  31.8 us (9%)
  blocking collectives  29.3 us (8%)
  between operations  16.6 us (5%)
  starting transfers between devices  11.8 us (3%)
    unnamed x5, waiting for transfers between devices  113 us
    ppermute x2, waiting for transfers between devices, padded(): after = lax.ppermute(initial, axis, down)  57 us
    all_gather x1, blocking collectives, shards(): lax.all_gather(audio_tokens, 'tensor', axis=1, tiled=True)  29.3 us
    unnamed x30, local copies, waits for them, and re-layouts  19.2 us
    convert_element_type x1, other arithmetic, layer_norm(): return (centred * lax.rsqrt(spread + epsilon)).astype(jnp.bfloat16)  12 us
    dot_general x2, matrix products, project_pair(): jnp.dot(row_block, w_value[tower_pos], preferred_element_type=jnp.float32)  11.6 us
    dot_general x3, local copies, waits for them, and re-layouts, project_pair(): jnp.dot(row_block, w_key[tower_pos], preferred_element_type=jnp.float32)  10.6 us
    dot_general x1, matrix products, shards(): jnp.dot(video_attended, w_out[0], preferred_element_type=jnp.float32)  9.31 us
  transfers between devices with their start and end apart: 7, of which 5 were waited for; matrix products, arithmetic and copies ran while one was open for 17% of the time, Pallas kernels for 0%

commit v1 on v0

v1 whole, which is shorter than its diff:
```python
import math

import jax
import jax.numpy as jnp
from jax import lax
from jax.experimental import pallas as pl
from jax.experimental.pallas import tpu as pltpu
from jax.sharding import PartitionSpec as P

D = 3072
HEAD = 128
HEADS_DEV = 3
GROUP = HEADS_DEV * HEAD
N_TENSOR = 8
VID = 1536
AUD = 32
REACH = 8
SPAN = AUD + 2 * REACH
KEYS = HEADS_DEV * SPAN
SHARDS = 16
TILE = 256
TILES = VID // TILE
HALF = VID // 2
THIRD = VID // 3
EPS = 1e-6
SCALE = math.log2(math.e) / math.sqrt(HEAD)
F32 = jnp.float32
BF16 = jnp.bfloat16


def params(mib, semantics=1):
    return pltpu.CompilerParams(
        dimension_semantics=("arbitrary",) * semantics, vmem_limit_bytes=mib * 2**20
    )


def dot(a, b):
    return jnp.dot(a, b, preferred_element_type=F32)


def dot_nt(a, b):
    return lax.dot_general(a, b, (((1,), (1,)), ((), ())), preferred_element_type=F32)


def dot_tn(a, b):
    return lax.dot_general(a, b, (((0,), (0,)), ((), ())), preferred_element_type=F32)


def full(shape):
    return pl.BlockSpec(shape, lambda *_: (0,) * len(shape))


def moved(index, dy, dx):
    return (index // 4 + dy) % 2 * 4 + (index % 4 + dx) % 4


def send(array, dy, dx):
    pairs = [(i, moved(i, dy, dx)) for i in range(N_TENSOR)]
    return lax.ppermute(array, "tensor", pairs)


def right(array):
    return send(array, 0, 1)


def left(array):
    return send(array, 0, 3)


def across(array):
    return send(array, 1, 0)


def cat(*arrays):
    return jnp.concatenate(arrays, axis=0)


def audio_in_kernel(a_ref, wq_ref, wk_ref, wv_ref, qkv_ref, prev_ref, next_ref, stat, acc):
    step = pl.program_id(0)

    @pl.when(step == 0)
    def _():
        values = a_ref[...].astype(F32)
        mean = jnp.sum(jnp.sum(values, axis=0), axis=-1, keepdims=True) / D
        centred = values - mean[None]
        var = jnp.sum(jnp.sum(centred * centred, axis=0), axis=-1, keepdims=True) / D
        stat[0] = jnp.broadcast_to(mean, (AUD, HEAD))
        stat[1] = jnp.broadcast_to(lax.rsqrt(var + EPS), (AUD, HEAD))
        acc[...] = jnp.zeros_like(acc)

    block = a_ref[step].astype(F32)
    normed = ((block - stat[0][:, :1]) * stat[1][:, :1]).astype(BF16)
    weights = jnp.concatenate([wq_ref[0], wk_ref[0], wv_ref[0]], axis=1)
    acc[...] += dot(normed, weights)

    @pl.when(step == N_TENSOR - 1)
    def _():
        total = acc[...]
        heads = []
        for h in range(2 * HEADS_DEV):
            part = total[:, h * HEAD : (h + 1) * HEAD]
            mean_square = jnp.mean(part * part, axis=-1, keepdims=True)
            heads.append(part * lax.rsqrt(mean_square + EPS))
        q = jnp.concatenate(heads[:HEADS_DEV], axis=1)
        k = jnp.concatenate(heads[HEADS_DEV:], axis=1)
        v = total[:, 2 * GROUP :]
        qkv_ref[...] = cat(q, k, v).astype(BF16)
        prev_ref[...] = cat(q, k[:REACH], v[:REACH]).astype(BF16)
        next_ref[...] = cat(q, k[AUD - REACH :], v[AUD - REACH :]).astype(BF16)


def audio_in(gathered, w_query, w_key, w_value):
    def weight(tower):
        return pl.BlockSpec((1, GROUP, GROUP), lambda j: (tower, j, 0))

    packed = AUD + 2 * REACH
    return pl.pallas_call(
        audio_in_kernel,
        grid=(N_TENSOR,),
        in_specs=[full((N_TENSOR, AUD, GROUP)), weight(1), weight(0), weight(0)],
        out_specs=[full((3 * AUD, GROUP)), full((packed, GROUP)), full((packed, GROUP))],
        out_shape=[
            jax.ShapeDtypeStruct((3 * AUD, GROUP), BF16),
            jax.ShapeDtypeStruct((packed, GROUP), BF16),
            jax.ShapeDtypeStruct((packed, GROUP), BF16),
        ],
        scratch_shapes=[pltpu.VMEM((2, AUD, HEAD), F32), pltpu.VMEM((AUD, 3 * GROUP), F32)],
        compiler_params=params(32),
        cost_estimate=pl.CostEstimate(
            flops=2 * AUD * D * 3 * GROUP, bytes_accessed=3 * D * GROUP * 2, transcendentals=0
        ),
        name="audio_in",
    )(gathered, w_query, w_key, w_value)


def value_out_kernel(dest_ref, qkv_ref, prev_ref, next_ref, w_ref, out_ref):
    before = prev_ref[...].astype(F32)[AUD + REACH :]
    own = qkv_ref[...].astype(F32)[2 * AUD :]
    after = next_ref[...].astype(F32)[AUD + REACH :]
    values = cat(before, own, after).astype(BF16)
    for h in range(HEADS_DEV):
        cols = slice(h * HEAD, (h + 1) * HEAD)
        out_ref[0, h * SPAN : (h + 1) * SPAN, :] = dot(values[:, cols], w_ref[0, cols, :]).astype(
            BF16
        )


def value_out(dest, qkv, from_prev, from_next, w_out):
    packed = AUD + 2 * REACH
    return pl.pallas_call(
        value_out_kernel,
        grid_spec=pltpu.PrefetchScalarGridSpec(
            num_scalar_prefetch=1,
            grid=(N_TENSOR,),
            in_specs=[
                full((3 * AUD, GROUP)),
                full((packed, GROUP)),
                full((packed, GROUP)),
                pl.BlockSpec((1, GROUP, GROUP), lambda j, dest: (0, 0, dest[j])),
            ],
            out_specs=pl.BlockSpec((1, KEYS, GROUP), lambda j, dest: (j, 0, 0)),
        ),
        out_shape=jax.ShapeDtypeStruct((N_TENSOR, KEYS, GROUP), BF16),
        compiler_params=params(32),
        cost_estimate=pl.CostEstimate(
            flops=2 * KEYS * HEAD * D, bytes_accessed=GROUP * D * 2 + KEYS * D * 2, transcendentals=0
        ),
        name="value_out",
    )(dest, qkv, from_prev, from_next, w_out)


def row_stats(block):
    values = block.astype(F32)
    mean = jnp.mean(values, axis=-1, keepdims=True)
    centred = values - mean
    return mean, jnp.sum(centred * centred, axis=-1, keepdims=True)


def fill_weights(w_refs, wcat, sums):
    for part in range(3):
        for j in range(4):
            wcat[j * GROUP : (j + 1) * GROUP, part * GROUP : (part + 1) * GROUP] = w_refs[
                part * 4 + j
            ][0]
    sums[...] = dot(jnp.ones((8, 4 * GROUP), BF16), wcat[...])


def first_kernel(order_ref, *refs):
    x_refs, w_refs = refs[:4], refs[4:16]
    acc_ref, stat_ref, sums_ref, wcat = refs[16:]

    @pl.when(pl.program_id(0) == 0)
    def _():
        fill_weights(w_refs, wcat, sums_ref)

    block = jnp.concatenate([ref[...] for ref in x_refs], axis=1)
    acc_ref[...] = dot(block, wcat[...])
    mean, square = row_stats(block)
    lane = lax.broadcasted_iota(jnp.int32, (TILE, HEAD), 1)
    stat_ref[...] = jnp.where(lane == 0, mean, square)


def weight_specs(first):
    specs = []
    for tower in (0, 1, 1):
        for j in range(first, first + 4):
            specs.append(
                pl.BlockSpec(
                    (1, GROUP, GROUP), lambda i, order, *_, t=tower, j=j: (t, order[j], 0)
                )
            )
    return specs


def weight_args(w_query, w_key, w_value):
    return [w_query] * 4 + [w_key] * 4 + [w_value] * 4


def first_half(order, blocks, w_query, w_key, w_value):
    rows = pl.BlockSpec((TILE, GROUP), lambda i, order: (i, 0))
    return pl.pallas_call(
        first_kernel,
        grid_spec=pltpu.PrefetchScalarGridSpec(
            num_scalar_prefetch=1,
            grid=(TILES,),
            in_specs=[rows] * 4 + weight_specs(0),
            out_specs=[
                pl.BlockSpec((TILE, 3 * GROUP), lambda i, order: (i, 0)),
                pl.BlockSpec((TILE, HEAD), lambda i, order: (i, 0)),
                full((8, 3 * GROUP)),
            ],
            scratch_shapes=[pltpu.VMEM((4 * GROUP, 3 * GROUP), BF16)],
        ),
        out_shape=[
            jax.ShapeDtypeStruct((VID, 3 * GROUP), F32),
            jax.ShapeDtypeStruct((VID, HEAD), F32),
            jax.ShapeDtypeStruct((8, 3 * GROUP), F32),
        ],
        compiler_params=params(40),
        cost_estimate=pl.CostEstimate(
            flops=2 * VID * 4 * GROUP * 3 * GROUP,
            bytes_accessed=4 * VID * GROUP * 2 + VID * 3 * GROUP * 4 + 12 * GROUP * GROUP * 2,
            transcendentals=0,
        ),
        name="first_half",
    )(order, *blocks, *weight_args(w_query, w_key, w_value))


def second_kernel(
    order_ref, vc_ref, ac_ref, vw_ref, aw_ref, *refs
):
    x_refs, w_refs = refs[:10], refs[10:22]
    acc_ref, stat_ref, sums1_ref, qkv_ref, prev_ref, next_ref = refs[22:28]
    pt_ref, part_p, part_o, part_n, wcat, sums, xcat, keys, queries = refs[28:]
    i = pl.program_id(0)
    shard = order_ref[N_TENSOR]

    @pl.when(i == 0)
    def _():
        fill_weights(w_refs, wcat, sums)
        before = prev_ref[...].astype(F32)
        own = qkv_ref[...].astype(F32)
        after = next_ref[...].astype(F32)
        keys[...] = cat(
            before[AUD : AUD + REACH], own[AUD : 2 * AUD], after[AUD : AUD + REACH]
        ).astype(BF16)
        queries[...] = cat(before[:AUD], own[:AUD], after[:AUD]).astype(BF16)
        for ref in (part_p, part_o, part_n):
            ref[...] = jnp.zeros_like(ref)

    places = (
        (0, 0, 0, 3), (0, 1, 3, 6),
        (1, 2, 0, 2), (1, 3, 2, 4), (1, 4, 4, 6),
        (2, 5, 0, 2), (2, 6, 2, 4), (2, 7, 4, 6),
        (3, 8, 0, 3), (3, 9, 3, 6),
    )
    for col, source, low, high in places:

        @pl.when((i >= low) & (i < high))
        def _(col=col, source=source):
            xcat[:, col * GROUP : (col + 1) * GROUP] = x_refs[source][...]

    block = xcat[...]
    mean2, square2 = row_stats(block)
    mean1, square1 = stat_ref[:, :1], stat_ref[:, 1:2]
    gap = mean1 - mean2
    mean = 0.5 * (mean1 + mean2)
    var = (square1 + square2 + gap * gap * (D / 4)) / D
    total = acc_ref[...] + dot(block, wcat[...])
    total = total - mean * (sums1_ref[:1, :] + sums[:1, :])
    floor = EPS * (var + EPS)

    prev_at, next_at = jnp.maximum(shard - 1, 0), jnp.minimum(shard + 1, SHARDS - 1)
    has_prev, has_next = shard > 0, shard < SHARDS - 1
    slot = lax.broadcasted_iota(jnp.int32, (SPAN, 1), 0)
    end_prev = jnp.where(has_prev, ac_ref[prev_at] - (AUD - REACH), 0)
    end_own = REACH + ac_ref[shard]
    end_next = jnp.where(
        has_next, REACH + AUD + jnp.minimum(ac_ref[next_at], vw_ref[shard, 1]), 0
    )
    used = (slot >= REACH - vw_ref[shard, 0]) & (slot < jnp.minimum(end_prev, REACH))
    used |= (slot >= REACH) & (slot < end_own)
    used |= (slot >= REACH + AUD) & (slot < end_next)

    count = vc_ref[shard]
    row = lax.broadcasted_iota(jnp.int32, (3 * AUD, 1), 0)
    high_prev = jnp.where(has_prev, jnp.minimum(count, aw_ref[prev_at, 1]), 0)
    high_next = jnp.where(has_next, count, 0)
    low = jnp.where(row < 2 * AUD, 0, VID - aw_ref[next_at, 0])
    high = jnp.where(row < AUD, high_prev, jnp.where(row < 2 * AUD, count, high_next))
    place = i * TILE + lax.broadcasted_iota(jnp.int32, (3 * AUD, TILE), 1)
    seen = (place >= low) & (place < high)
    spread = lax.rsqrt(var + EPS)

    for h in range(HEADS_DEV):
        cols = slice(h * HEAD, (h + 1) * HEAD)

        def normed(first):
            part = total[:, first + h * HEAD : first + (h + 1) * HEAD]
            mean_square = jnp.mean(part * part, axis=-1, keepdims=True)
            return (part * lax.rsqrt(mean_square + floor)).astype(BF16)

        scores = dot_nt(keys[:, cols], normed(0))
        weights = jnp.where(used, jnp.exp2(scores * SCALE), 0.0)
        sums_h = jnp.sum(weights, axis=0, keepdims=True)
        pt_ref[0, h * SPAN : (h + 1) * SPAN, :] = (weights * (1.0 / sums_h)).astype(BF16)

        value = (total[:, 2 * GROUP + h * HEAD : 2 * GROUP + (h + 1) * HEAD] * spread).astype(BF16)
        scores = dot_nt(queries[:, cols], normed(GROUP))
        weights = jnp.where(seen, jnp.exp2(scores * SCALE), 0.0)
        bottom = jnp.broadcast_to(jnp.sum(weights, axis=1, keepdims=True), (3 * AUD, HEAD))
        top = dot(weights.astype(BF16), value)
        for g, ref in enumerate((part_p, part_o, part_n)):
            ref[0, :, cols] += top[g * AUD : (g + 1) * AUD]
            ref[1, :, cols] += bottom[g * AUD : (g + 1) * AUD]


def second_half(order, tables, pieces, w_query, w_key, w_value, acc, stat, sums, qkv, prev, after):
    def rows(low, count, base=0):
        return pl.BlockSpec(
            (TILE, GROUP), lambda i, *_: (base + jnp.clip(i - low, 0, count - 1), 0)
        )

    packed = AUD + 2 * REACH
    part = jax.ShapeDtypeStruct((2, AUD, GROUP), F32)
    piece_specs = [
        rows(0, 3), rows(3, 3),
        rows(0, 2), rows(2, 2), rows(4, 2),
        rows(0, 2, 2), rows(2, 2, 2), rows(4, 2),
        rows(0, 3), rows(3, 3),
    ]
    return pl.pallas_call(
        second_kernel,
        grid_spec=pltpu.PrefetchScalarGridSpec(
            num_scalar_prefetch=5,
            grid=(TILES,),
            in_specs=piece_specs
            + weight_specs(4)
            + [
                pl.BlockSpec((TILE, 3 * GROUP), lambda i, *_: (i, 0)),
                pl.BlockSpec((TILE, HEAD), lambda i, *_: (i, 0)),
                full((8, 3 * GROUP)),
                full((3 * AUD, GROUP)),
                full((packed, GROUP)),
                full((packed, GROUP)),
            ],
            out_specs=[
                pl.BlockSpec((1, KEYS, TILE), lambda i, *_: (i // 3, 0, i % 3)),
                full((2, AUD, GROUP)),
                full((2, AUD, GROUP)),
                full((2, AUD, GROUP)),
            ],
            scratch_shapes=[
                pltpu.VMEM((4 * GROUP, 3 * GROUP), BF16),
                pltpu.VMEM((8, 3 * GROUP), F32),
                pltpu.VMEM((TILE, 4 * GROUP), BF16),
                pltpu.VMEM((SPAN, GROUP), BF16),
                pltpu.VMEM((3 * AUD, GROUP), BF16),
            ],
        ),
        out_shape=[jax.ShapeDtypeStruct((2, KEYS, HALF), BF16), part, part, part],
        compiler_params=params(44),
        cost_estimate=pl.CostEstimate(
            flops=2 * VID * 4 * GROUP * 3 * GROUP,
            bytes_accessed=4 * VID * GROUP * 2 + VID * 3 * GROUP * 4 + 12 * GROUP * GROUP * 2,
            transcendentals=VID * HEADS_DEV * (SPAN + 3 * AUD),
        ),
        name="second_half",
    )(
        order, *tables, *pieces, *weight_args(w_query, w_key, w_value),
        acc, stat, sums, qkv, prev, after,
    )


def audio_out_kernel(own_ref, prev_ref, next_ref, w_ref, out_ref, attended):
    @pl.when(pl.program_id(0) == 0)
    def _():
        total = own_ref[...] + prev_ref[...] + next_ref[...]
        attended[...] = (total[0] / total[1]).astype(BF16)

    out_ref[0] = dot(attended[...], w_ref[0]).astype(BF16)


def audio_out(own, from_prev, from_next, w_out):
    return pl.pallas_call(
        audio_out_kernel,
        grid=(N_TENSOR,),
        in_specs=[full((2, AUD, GROUP))] * 3
        + [pl.BlockSpec((1, GROUP, GROUP), lambda j: (1, 0, j))],
        out_specs=pl.BlockSpec((1, AUD, GROUP), lambda j: (j, 0, 0)),
        out_shape=jax.ShapeDtypeStruct((N_TENSOR, AUD, GROUP), BF16),
        scratch_shapes=[pltpu.VMEM((AUD, GROUP), BF16)],
        compiler_params=params(32),
        cost_estimate=pl.CostEstimate(
            flops=2 * AUD * GROUP * D, bytes_accessed=GROUP * D * 2, transcendentals=0
        ),
        name="audio_out",
    )(own, from_prev, from_next, w_out)


def video_out_kernel(meta_ref, vc_ref, *refs):
    p_refs, a_refs, v_refs = refs[:6], refs[6:8], refs[8:16]
    out_ref, projected, probs = refs[16:]
    i = pl.program_id(0)

    @pl.when(i == 0)
    def _():
        for j, ref in enumerate(v_refs):
            projected[j * KEYS : (j + 1) * KEYS, :] = ref[0] if j == 0 else ref[...]

    for j, ref in enumerate(p_refs):
        probs[j * KEYS : (j + 1) * KEYS, :] = ref[0]

    for half in range(2):

        @pl.when(i // 3 == half)
        def _(half=half):
            for j in range(2):
                probs[(6 + j) * KEYS : (7 + j) * KEYS, :] = a_refs[half][j]

    result = dot_tn(probs[...], projected[...])
    row = i * TILE + lax.broadcasted_iota(jnp.int32, (TILE, 1), 0)
    valid = row < vc_ref[meta_ref[N_TENSOR]]
    out_ref[...] = jnp.where(valid, result, 0.0).astype(BF16)


def video_out(meta, video_counts, probs, fars, own_values, values):
    tile = pl.BlockSpec((1, KEYS, TILE), lambda i, *_: (i // 3, 0, i % 3))
    low = pl.BlockSpec((2, KEYS, TILE), lambda i, *_: (0, 0, jnp.minimum(i, 2)))
    high = pl.BlockSpec((2, KEYS, TILE), lambda i, *_: (0, 0, jnp.maximum(i - 3, 0)))
    return pl.pallas_call(
        video_out_kernel,
        grid_spec=pltpu.PrefetchScalarGridSpec(
            num_scalar_prefetch=2,
            grid=(TILES,),
            in_specs=[tile] * 6
            + [low, high]
            + [full((1, KEYS, GROUP))]
            + [full((KEYS, GROUP))] * 7,
            out_specs=pl.BlockSpec((TILE, GROUP), lambda i, *_: (i, 0)),
            scratch_shapes=[
                pltpu.VMEM((N_TENSOR * KEYS, GROUP), BF16),
                pltpu.VMEM((N_TENSOR * KEYS, TILE), BF16),
            ],
        ),
        out_shape=jax.ShapeDtypeStruct((VID, GROUP), BF16),
        compiler_params=params(40),
        cost_estimate=pl.CostEstimate(
            flops=2 * VID * N_TENSOR * KEYS * GROUP,
            bytes_accessed=VID * N_TENSOR * KEYS * 2 + N_TENSOR * KEYS * GROUP * 2,
            transcendentals=0,
        ),
        name="video_out",
    )(meta, video_counts, *probs, *fars, own_values, *values)


def shards(
    video_tokens,
    audio_tokens,
    w_query,
    w_key,
    w_value,
    w_out,
    video_counts,
    audio_counts,
    video_windows,
    audio_windows,
):
    me = lax.axis_index("tensor")
    shard = lax.axis_index(("tower", "tm"))
    up = [(i, i + 1) for i in range(SHARDS - 1)]
    down = [(i + 1, i) for i in range(SHARDS - 1)]

    def to_next(array):
        return lax.ppermute(array, ("tower", "tm"), up)

    def to_prev(array):
        return lax.ppermute(array, ("tower", "tm"), down)

    offsets = ((0, 0), (0, 3), (0, 1), (1, 0), (0, 2), (1, 3), (1, 1), (1, 2))
    order = jnp.stack([moved(me, dy, dx) for dy, dx in offsets] + [shard]).astype(jnp.int32)
    dest = jnp.stack([moved(me, dy, -dx) for dy, dx in offsets]).astype(jnp.int32)

    own = video_tokens
    xl, xr, xy = right(own), left(own), across(own)
    audio_blocks = lax.all_to_all(
        jnp.broadcast_to(audio_tokens[None], (N_TENSOR, AUD, GROUP)), "tensor", 0, 0
    )
    qkv, for_prev, for_next = audio_in(audio_blocks, w_query, w_key, w_value)
    from_next, from_prev = to_prev(for_prev), to_next(for_next)

    q_top, q_bot = right(xl[:HALF]), left(xr[HALF:])
    yl_a, yr_c = right(xy[:THIRD]), left(xy[2 * THIRD :])
    middle = across(cat(xl[THIRD : 2 * THIRD], xr[THIRD : 2 * THIRD]))
    edge = across(cat(xl[2 * THIRD :], xr[:THIRD]))
    yq_top = right(cat(yl_a, middle[: HALF - THIRD]))
    yq_bot = left(cat(middle[THIRD + HALF - THIRD :], yr_c))

    acc, stat, sums = first_half(order, (own, xl, xr, xy), w_query, w_key, w_value)
    projected = value_out(dest, qkv, from_prev, from_next, w_out)
    values = [send(projected[j], dy, -dx) for j, (dy, dx) in enumerate(offsets) if j]

    pieces = (q_top, q_bot, yl_a, middle, edge, edge, middle, yr_c, yq_top, yq_bot)
    probs, part_prev, part_own, part_next = second_half(
        order,
        (video_counts, audio_counts, video_windows, audio_windows),
        pieces,
        w_query,
        w_key,
        w_value,
        acc,
        stat,
        sums,
        qkv,
        from_prev,
        from_next,
    )

    pl_, pr_, py_ = right(probs), left(probs), across(probs)
    pyl, pyr = right(py_), left(py_)
    far_low = right(jnp.stack([pl_[0], pyl[0]]))
    far_high = left(jnp.stack([pr_[1], pyr[1]]))

    audio_from_next, audio_from_prev = to_prev(part_prev), to_next(part_next)
    audio_parts = audio_out(part_own, audio_from_prev, audio_from_next, w_out)
    audio_sums = jnp.sum(
        lax.all_to_all(audio_parts, "tensor", 0, 0).astype(F32), axis=0
    )
    audio_limit = lax.dynamic_index_in_dim(audio_counts, shard, 0, keepdims=False)
    audio_valid = jnp.arange(AUD, dtype=jnp.int32) < audio_limit
    audio_update = jnp.where(audio_valid[:, None], audio_sums, 0.0).astype(BF16)

    arranged = [values[k - 1] for k in (1, 2, 3, 5, 6, 4, 7)]
    video_update = video_out(
        order,
        video_counts,
        (probs, pl_, pr_, py_, pyl, pyr),
        (far_low, far_high),
        projected[:1],
        arranged,
    )
    return (video_update, audio_update)


def solution(mesh):
    in_specs = (
        P(("tower", "tm"), "tensor"),
        P(("tower", "tm"), "tensor"),
        P(None, None, "tensor"),
        P(None, None, "tensor"),
        P(None, None, "tensor"),
        P(None, "tensor", None),
        P(),
        P(),
        P(),
        P(),
    )
    out_specs = (P(("tower", "tm"), "tensor"), P(("tower", "tm"), "tensor"))
    return jax.shard_map(shards, mesh=mesh, in_specs=in_specs, out_specs=out_specs, check_vma=False)
```

time: 367 us -> 207 us (0.56)
  waiting for transfers between devices: 178 us -> 58.7 us
  starting transfers between devices: 11.8 us -> 60.8 us
  Pallas kernels: 0 us -> 46.1 us
  matrix products: 41.9 us -> 0 us
  blocking collectives: 29.3 us -> 0 us
  local copies, waits for them, and re-layouts: 55.7 us -> 30 us
  other arithmetic: 31.8 us -> 7.5 us
  between operations: 16.6 us -> 1.06 us
    unnamed x5 -> x0, waiting for transfers between devices: 113 us -> none
    pallas_call x0 -> x6, Pallas kernels: none -> 46.1 us  [the longest x1 17.6 us: second_half(): pl.pallas_call(second_kernel, grid_spec=pltpu.PrefetchScalarGridSpec(num_...]
    dot_general x16 -> x0, matrix products: 41.9 us -> none  [the longest x2 11.6 us: project_pair(): jnp.dot(row_block, w_value[tower_pos], preferred_element_type=jnp.float32)]
    ppermute x4 -> x29, starting transfers between devices: 11.6 us -> 51.3 us  [the longest x25 35.6 us: send(): return lax.ppermute(array, 'tensor', pairs)]
    all_gather x1 -> x0, blocking collectives: 29.3 us -> none  [shards(): lax.all_gather(audio_tokens, 'tensor', axis=1, tiled=True)]
    dot_general x6 -> x0, local copies, waits for them, and re-layouts: 23.1 us -> none  [the longest x3 10.6 us: project_pair(): jnp.dot(row_block, w_key[tower_pos], preferred_element_type=jnp.float32)]
    convert_element_type x6 -> x1, other arithmetic: 15.8 us -> 0.68 us  [shards(): audio_update = jnp.where(audio_valid[:, None], audio_sums, 0.0).astype(BF16)]
    ppermute x4 -> x29, waiting for transfers between devices: 64.1 us -> 49.5 us  [the longest x25 43.7 us: send(): return lax.ppermute(array, 'tensor', pairs)]
  transfers between devices with their start and end apart: 7 -> 31, of which waited for: 5 -> 10; matrix products, arithmetic and copies ran while one was open for 17% -> 9% of each run, Pallas kernels for 0% -> 11%
where the time goes in v1:
time: 207 us; the launch traced here: 204 us
  starting transfers between devices  60.8 us (29%)
  waiting for transfers between devices  58.7 us (28%)
  Pallas kernels  46.1 us (22%)
  local copies, waits for them, and re-layouts  30 us (14%)
  other arithmetic  7.5 us (4%)
    ppermute x25, waiting for transfers between devices, send(): return lax.ppermute(array, 'tensor', pairs)  43.7 us
    ppermute x25, starting transfers between devices, send(): return lax.ppermute(array, 'tensor', pairs)  35.6 us
    unnamed x68, local copies, waits for them, and re-layouts  20.8 us
    pallas_call x1, Pallas kernels, second_half(): pl.pallas_call(second_kernel, grid_spec=pltpu.PrefetchScalarGridSpec(num_...  17.6 us
    ppermute x2, starting transfers between devices, to_next(): return lax.ppermute(array, ('tower', 'tm'), up)  12.9 us
    pallas_call x1, Pallas kernels, first_half(): pl.pallas_call(first_kernel, grid_spec=pltpu.PrefetchScalarGridSpec(num_s...  12.2 us
    all_to_all x1, waiting for transfers between devices, shards(): lax.all_to_all(jnp.broadcast_to(audio_tokens[None], (N_TENSOR, AUD, GROUP...  9.17 us
    pallas_call x1, Pallas kernels, video_out(): pl.pallas_call(video_out_kernel, grid_spec=pltpu.PrefetchScalarGridSpec(n...  6.57 us
  transfers between devices with their start and end apart: 31, of which 10 were waited for; matrix products, arithmetic and copies ran while one was open for 9% of the time, Pallas kernels for 11%

profile of v1, /device:TPU:0, one launch (start us, length us, event | category | flops | bytes accessed | tf_op | source)
XLA Modules:
  0.0 204.2 jit_solution(15910743402754128572)
XLA Ops:
  2.3 1.7 collective-permute-start.2
  3.9 1.7 collective-permute-start.4
  5.6 24.1 %collective-permute-done.refs_1_ = bf16[1536,384]{1,0:T(8,128)(2,1)S(1)} collective-permute-done((bf16[1536,384]{1,0:T(8,128)(2,1)}, bf16[1536,384]{1,0:T(8,128)(2,1)S(1)}, u32[]{:S(2)}, u32[]{:S(2)}) %collective-permute-start) | collective-permute-done | bytes 1179680 | tf_op jit(solution)/shard_map/ppermute | solution.py:59
  32.3 1.8 collective-permute-start.6
  34.8 4.0 %all-to-all-start = ((bf16[8,32,384]{2,1,0:T(8,128)(2,1)}), bf16[8,32,384]{2,1,0:T(8,128)(2,1)}, u32[]{:S(2)}, u32[]{:S(2)}) async-start(bf16[8,32,384]{2,1,0:T(8,128)(2,1)} %broadcast_in_dim.19), calls=%async_computation | async-start | bytes 393216 | tf_op jit(solution)/shard_map/all_to_all | solution.py:506
  38.8 2.1 %fusion = (bf16[512,384]{1,0:T(8,128)(2,1)}, bf16[512,384]{1,0:T(8,128)(2,1)}) fusion(bf16[1536,384]{1,0:T(8,128)(2,1)} %collective-permute-done.4.refs_3_), kind=kLoop, calls=%fused_computation.16 | loop fusion | bytes 1572864 | tf_op jit(solution)/shard_map/slice | solution.py:513
  40.9 3.1 %collective-permute-start.8 = (bf16[512,384]{1,0:T(8,128)(2,1)}, bf16[512,384]{1,0:T(8,128)(2,1)S(1)}, u32[]{:S(2)}, u32[]{:S(2)}) collective-permute-start(bf16[512,384]{1,0:T(8,128)(2,1)} %get-tuple-element.22), channel_id=1, source_target_pairs={{0,3},{1,0},{2,1},{3,2},{4,7},{5,4},{6,5},{7,6},{8,11},{9,8},{10,9... | collective-permute-start | bytes 1179656 | tf_op jit(solution)/shard_map/ppermute | solution.py:59
  44.0 9.2 %all-to-all-done.a_ref = bf16[8,32,384]{2,1,0:T(8,128)(2,1)} async-done(((bf16[8,32,384]{2,1,0:T(8,128)(2,1)}), bf16[8,32,384]{2,1,0:T(8,128)(2,1)}, u32[]{:S(2)}, u32[]{:S(2)}) %all-to-all-start) | async-done | bytes 196640 | tf_op jit(solution)/shard_map/all_to_all | solution.py:506
  53.2 2.3 %copy-done = bf16[2,3072,384]{2,1,0:T(8,128)(2,1)S(1)} copy-done((bf16[2,3072,384]{2,1,0:T(8,128)(2,1)S(1)}, bf16[2,3072,384]{2,1,0:T(8,128)(2,1)}, u32[]{:S(2)}) %copy-start) | copy-done | bytes 4718616
  55.5 2.3 %copy-done.2 = bf16[2,3072,384]{2,1,0:T(8,128)(2,1)S(1)} copy-done((bf16[2,3072,384]{2,1,0:T(8,128)(2,1)S(1)}, bf16[2,3072,384]{2,1,0:T(8,128)(2,1)}, u32[]{:S(2)}) %copy-start.2) | copy-done | bytes 4718616
  57.9 2.3 %copy-done.3 = bf16[2,3072,384]{2,1,0:T(8,128)(2,1)S(1)} copy-done((bf16[2,3072,384]{2,1,0:T(8,128)(2,1)S(1)}, bf16[2,3072,384]{2,1,0:T(8,128)(2,1)}, u32[]{:S(2)}) %copy-start.3) | copy-done | bytes 4718616
  60.2 3.9 %audio_in.1 = (bf16[96,384]{1,0:T(8,128)(2,1)S(1)}, bf16[48,384]{1,0:T(8,128)(2,1)S(1)}, bf16[48,384]{1,0:T(8,128)(2,1)S(1)}) custom-call(bf16[8,32,384]{2,1,0:T(8,128)(2,1)} %all-to-all-done.a_ref, bf16[2,3072,384]{2,1,0:T(8,128)(2,1)S(1)} %copy-done, bf16[2,3072,384]{2,1,0:T(8,128)(2,1)S(1)} %copy-done.2, bf16[2,3072,384]{2,1,0:T(8,128)(2,1)S(1)} %copy-done.3), custom_call_target="tpu_custom_call" | custom-call | flops 226492416 | bytes 7077888 | tf_op jit(solution)/shard_map/audio_in/pallas_call | solution.py:117
  64.1 5.3 %collective-permute-start.11 = (bf16[48,384]{1,0:T(8,128)(2,1)S(1)}, bf16[48,384]{1,0:T(8,128)(2,1)S(1)}, u32[]{:S(2)}, u32[]{:S(2)}) collective-permute-start(bf16[48,384]{1,0:T(8,128)(2,1)S(1)} %get-tuple-element.16), channel_id=1, source_target_pairs={{0,8},{8,16},{16,24},{24,32},{32,40},{40,48},{48,56},{56,64},{64,7... | collective-permute-start | bytes 110600 | tf_op jit(solution)/shard_map/ppermute | solution.py:495
  77.1 3.5 %collective-permute-done.5.refs_2_ = bf16[512,384]{1,0:T(8,128)(2,1)S(1)} collective-permute-done((bf16[512,384]{1,0:T(8,128)(2,1)S(1)}, bf16[512,384]{1,0:T(8,128)(2,1)S(1)}, u32[]{:S(2)}, u32[]{:S(2)}) %collective-permute-start.5) | collective-permute-done | bytes 393248 | tf_op jit(solution)/shard_map/ppermute | solution.py:59
  87.6 2.3 %copy-done.1 = bf16[2,3072,384]{2,1,0:T(8,128)(2,1)S(1)} copy-done((bf16[2,3072,384]{2,1,0:T(8,128)(2,1)S(1)}, bf16[2,3072,384]{2,1,0:T(8,128)(2,1)}, u32[]{:S(2)}) %copy-start.1) | copy-done | bytes 4718616
  91.9 12.2 %first_half.1 = (f32[1536,1152]{1,0:T(8,128)}, f32[1536,128]{1,0:T(8,128)S(1)}, f32[8,1152]{1,0:T(8,128)S(1)}) custom-call(s32[9]{0:T(128)S(1)} %copy-done.20, bf16[1536,384]{1,0:T(8,128)(2,1)S(1)} %copy-done.8, bf16[1536,384]{1,0:T(8,128)(2,1)S(1)} %collective-permute-done.refs_1_, bf16[1536,384]{1,0:T(8,128)(2,1)S(1)} %collective-permute-done.2.refs_2_, ...), custom_call_target="tpu_custom_call" | custom-call | flops 5435817984 | bytes 15335424 | tf_op jit(solution)/shard_map/first_half/pallas_call | solution.py:221
  104.1 2.0 collective-permute-done.9.refs_8_
  106.1 17.6 %second_half.1 = (bf16[2,144,768]{2,1,0:T(8,128)(2,1)S(1)}, f32[2,32,384]{2,1,0:T(8,128)S(1)}, f32[2,32,384]{2,1,0:T(8,128)S(1)}, f32[2,32,384]{2,1,0:T(8,128)}) custom-call(s32[9]{0:T(128)S(1)} %copy-done.21, s32[16]{0:T(128)S(1)} %copy-done.23, s32[16]{0:T(128)S(1)} %copy-done.25, s32[16,2]{1,0:T(8,128)S(1)} %copy.12.vw_ref, s32[16,2]{1,0:T(8,128)S(1)} %copy.13.aw_ref, ...), custom_call_target="tpu_custom_call" | custom-call | flops 5435817984 | bytes 15335424 | tf_op jit(solution)/shard_map/second_half/pallas_call | solution.py:352
  127.7 7.3 %collective-permute-done.15.refs_3_ = bf16[2,144,768]{2,1,0:T(8,128)(2,1)S(1)} collective-permute-done((bf16[2,144,768]{2,1,0:T(8,128)(2,1)S(1)}, bf16[2,144,768]{2,1,0:T(8,128)(2,1)S(1)}, u32[]{:S(2)}, u32[]{:S(2)}) %collective-permute-start.15) | collective-permute-done | bytes 442400 | tf_op jit(solution)/shard_map/ppermute | solution.py:59
  135.0 7.7 %collective-permute-start.27 = (f32[2,32,384]{2,1,0:T(8,128)}, f32[2,32,384]{2,1,0:T(8,128)S(1)}, u32[]{:S(2)}, u32[]{:S(2)}) collective-permute-start(f32[2,32,384]{2,1,0:T(8,128)} %get-tuple-element.20), channel_id=1, source_target_pairs={{0,8},{8,16},{16,24},{24,32},{32,40},{40,48},{48,56},{56,64},{64,7... | collective-permute-start | bytes 294920 | tf_op jit(solution)/shard_map/ppermute | solution.py:495
  144.4 2.3 %copy-done.4 = bf16[2,384,3072]{2,1,0:T(8,128)(2,1)S(1)} copy-done((bf16[2,384,3072]{2,1,0:T(8,128)(2,1)S(1)}, bf16[2,384,3072]{2,1,0:T(8,128)(2,1)}, u32[]{:S(2)}) %copy-start.4) | copy-done | bytes 4718616
  147.5 2.4 %value_out.1 = bf16[8,144,384]{2,1,0:T(8,128)(2,1)S(1)} custom-call(s32[8]{0:T(128)S(1)} %stack.77.dest_ref, bf16[96,384]{1,0:T(8,128)(2,1)S(1)} %copy-done.11, bf16[48,384]{1,0:T(8,128)(2,1)S(1)} %copy-done.14, bf16[48,384]{1,0:T(8,128)(2,1)S(1)} %copy-done.17, bf16[2,384,3072]{2,1,0:T(8,128)(2,1)S(1)} %copy-done.4), custom_call_target="tpu_custom_call" | custom-call | flops 113246208 | bytes 3244032 | tf_op jit(solution)/shard_map/value_out/pallas_call | solution.py:150
  152.2 5.8 %collective-permute-done.28.next_ref = f32[2,32,384]{2,1,0:T(8,128)S(1)} collective-permute-done((f32[2,32,384]{2,1,0:T(8,128)S(1)}, f32[2,32,384]{2,1,0:T(8,128)S(1)}, u32[]{:S(2)}, u32[]{:S(2)}) %collective-permute-start.28) | collective-permute-done | bytes 98336 | tf_op jit(solution)/shard_map/ppermute | solution.py:498
  159.6 2.3 %copy-done.5 = bf16[2,384,3072]{2,1,0:T(8,128)(2,1)S(1)} copy-done((bf16[2,384,3072]{2,1,0:T(8,128)(2,1)S(1)}, bf16[2,384,3072]{2,1,0:T(8,128)(2,1)}, u32[]{:S(2)}) %copy-start.5) | copy-done | bytes 4718616
  161.9 3.4 %audio_out.1 = bf16[8,32,384]{2,1,0:T(8,128)(2,1)} custom-call(f32[2,32,384]{2,1,0:T(8,128)S(1)} %copy-done.19, f32[2,32,384]{2,1,0:T(8,128)S(1)} %collective-permute-done.27.prev_ref, f32[2,32,384]{2,1,0:T(8,128)S(1)} %collective-permute-done.28.next_ref, bf16[2,384,3072]{2,1,0:T(8,128)(2,1)S(1)} %copy-done.5), custom_call_target="tpu_custom_call" | custom-call | flops 75497472 | bytes 2359296 | tf_op jit(solution)/shard_map/audio_out/pallas_call | solution.py:405
  165.3 5.5 %all-to-all-start.1 = ((bf16[8,32,384]{2,1,0:T(8,128)(2,1)}), bf16[8,32,384]{2,1,0:T(8,128)(2,1)}, u32[]{:S(2)}, u32[]{:S(2)}) async-start(bf16[8,32,384]{2,1,0:T(8,128)(2,1)} %audio_out.1), calls=%async_computation.1 | async-start | bytes 393216 | tf_op jit(solution)/shard_map/all_to_all | solution.py:547
  171.8 3.2 %collective-permute-start.19 = (bf16[2,144,768]{2,1,0:T(8,128)(2,1)}, bf16[2,144,768]{2,1,0:T(8,128)(2,1)S(1)}, u32[]{:S(2)}, u32[]{:S(2)}) collective-permute-start(bf16[2,144,768]{2,1,0:T(8,128)(2,1)} %pad_maximum_fusion.5), channel_id=1, source_target_pairs={{0,3},{1,0},{2,1},{3,2},{4,7},{5,4},{6,5},{7,6},{8,11},{9,8},{10,9... | collective-permute-start | bytes 1327112 | tf_op jit(solution)/shard_map/ppermute | solution.py:59
  176.4 3.3 %collective-permute-start.21 = (bf16[144,384]{1,0:T(8,128)(2,1)}, bf16[144,384]{1,0:T(8,128)(2,1)S(1)}, u32[]{:S(2)}, u32[]{:S(2)}) collective-permute-start(bf16[144,384]{1,0:T(8,128)(2,1)} %get-tuple-element.33), channel_id=1, source_target_pairs={{0,3},{1,0},{2,1},{3,2},{4,7},{5,4},{6,5},{7,6},{8,11},{9,8},{10,9... | collective-permute-start | bytes 331784 | tf_op jit(solution)/shard_map/ppermute | solution.py:59
  182.2 3.0 %collective-permute-done.21.refs_10_ = bf16[144,384]{1,0:T(8,128)(2,1)S(1)} collective-permute-done((bf16[144,384]{1,0:T(8,128)(2,1)}, bf16[144,384]{1,0:T(8,128)(2,1)S(1)}, u32[]{:S(2)}, u32[]{:S(2)}) %collective-permute-start.21) | collective-permute-done | bytes 110624 | tf_op jit(solution)/shard_map/ppermute | solution.py:59
  185.2 5.0 %collective-permute-start.24 = (bf16[144,384]{1,0:T(8,128)(2,1)}, bf16[144,384]{1,0:T(8,128)(2,1)S(1)}, u32[]{:S(2)}, u32[]{:S(2)}) collective-permute-start(bf16[144,384]{1,0:T(8,128)(2,1)} %get-tuple-element.30), channel_id=1, source_target_pairs={{0,7},{1,4},{2,5},{3,6},{4,3},{5,0},{6,1},{7,2},{8,15},{9,12},{10,... | collective-permute-start | bytes 331784 | tf_op jit(solution)/shard_map/ppermute | solution.py:59
  190.2 3.0 %collective-permute-start.26 = (bf16[144,384]{1,0:T(8,128)(2,1)}, bf16[144,384]{1,0:T(8,128)(2,1)S(1)}, u32[]{:S(2)}, u32[]{:S(2)}) collective-permute-start(bf16[144,384]{1,0:T(8,128)(2,1)} %get-tuple-element.28), channel_id=1, source_target_pairs={{0,6},{1,7},{2,4},{3,5},{4,2},{5,3},{6,0},{7,1},{8,14},{9,15},{10,... | collective-permute-start | bytes 331784 | tf_op jit(solution)/shard_map/ppermute | solution.py:59
  197.6 6.6 %video_out.1 = bf16[1536,384]{1,0:T(8,128)(2,1)} custom-call(s32[9]{0:T(128)S(1)} %copy-done.22, s32[16]{0:T(128)S(1)} %copy-done.24, bf16[2,144,768]{2,1,0:T(8,128)(2,1)S(1)} %get-tuple-element.18.refs_0_, bf16[2,144,768]{2,1,0:T(8,128)(2,1)S(1)} %collective-permute-done.13.refs_1_, bf16[2,144,768]{2,1,0:T(8,128)(2,1)S(1)} %collective-permute-done.14.refs_2_, ...), custom_call_target="tpu_custom_call" | custom-call | flops 1358954496 | bytes 4423680 | tf_op jit(solution)/shard_map/video_out/pallas_call | solution.py:451
  (128 shorter events, 40.9 us)
Async XLA Ops:
  0.6 29.1 %collective-permute-start = (bf16[1536,384]{1,0:T(8,128)(2,1)}, bf16[1536,384]{1,0:T(8,128)(2,1)S(1)}, u32[]{:S(2)}, u32[]{:S(2)}) collective-permute-start(bf16[1536,384]{1,0:T(8,128)(2,1)} %refs_0_.1), channel_id=1, source_target_pairs={{0,1},{1,2},{2,3},{3,0},{4,5},{5,6},{6,7},{7,4},{8,9},{9,10},{10,1... | collective-permute-start | bytes 3538952 | tf_op jit(solution)/shard_map/ppermute | solution.py:59
  2.3 28.3 %collective-permute-start.2 = (bf16[1536,384]{1,0:T(8,128)(2,1)}, bf16[1536,384]{1,0:T(8,128)(2,1)S(1)}, u32[]{:S(2)}, u32[]{:S(2)}) collective-permute-start(bf16[1536,384]{1,0:T(8,128)(2,1)} %refs_0_.1), channel_id=1, source_target_pairs={{0,3},{1,0},{2,1},{3,2},{4,7},{5,4},{6,5},{7,6},{8,11},{9,8},{10,9... | collective-permute-start | bytes 3538952 | tf_op jit(solution)/shard_map/ppermute | solution.py:59
  3.9 34.9 %collective-permute-start.4 = (bf16[1536,384]{1,0:T(8,128)(2,1)}, bf16[1536,384]{1,0:T(8,128)(2,1)}, u32[]{:S(2)}, u32[]{:S(2)}) collective-permute-start(bf16[1536,384]{1,0:T(8,128)(2,1)} %refs_0_.1), channel_id=1, source_target_pairs={{0,4},{1,5},{2,6},{3,7},{4,0},{5,1},{6,2},{7,3},{8,12},{9,13},{10,... | collective-permute-start | bytes 3538952 | tf_op jit(solution)/shard_map/ppermute | solution.py:59
  32.3 41.6 %collective-permute-start.6 = (bf16[1024,384]{1,0:T(8,128)(2,1)}, bf16[1024,384]{1,0:T(8,128)(2,1)S(1)}, u32[]{:S(2)}, u32[]{:S(2)}) collective-permute-start(bf16[1024,384]{1,0:T(8,128)(2,1)} %pad_maximum_fusion), channel_id=1, source_target_pairs={{0,4},{1,5},{2,6},{3,7},{4,0},{5,1},{6,2},{7,3},{8,12},{9,13},{10,... | collective-permute-start | bytes 2359304 | tf_op jit(solution)/shard_map/ppermute | solution.py:59
  34.8 18.4 %all-to-all-start = ((bf16[8,32,384]{2,1,0:T(8,128)(2,1)}), bf16[8,32,384]{2,1,0:T(8,128)(2,1)}, u32[]{:S(2)}, u32[]{:S(2)}) async-start(bf16[8,32,384]{2,1,0:T(8,128)(2,1)} %broadcast_in_dim.19), calls=%async_computation | async-start | bytes 393216 | tf_op jit(solution)/shard_map/all_to_all | solution.py:506
  40.9 33.8 %collective-permute-start.8 = (bf16[512,384]{1,0:T(8,128)(2,1)}, bf16[512,384]{1,0:T(8,128)(2,1)S(1)}, u32[]{:S(2)}, u32[]{:S(2)}) collective-permute-start(bf16[512,384]{1,0:T(8,128)(2,1)} %get-tuple-element.22), channel_id=1, source_target_pairs={{0,3},{1,0},{2,1},{3,2},{4,7},{5,4},{6,5},{7,6},{8,11},{9,8},{10,9... | collective-permute-start | bytes 1179656 | tf_op jit(solution)/shard_map/ppermute | solution.py:59
  64.1 18.7 %collective-permute-start.11 = (bf16[48,384]{1,0:T(8,128)(2,1)S(1)}, bf16[48,384]{1,0:T(8,128)(2,1)S(1)}, u32[]{:S(2)}, u32[]{:S(2)}) collective-permute-start(bf16[48,384]{1,0:T(8,128)(2,1)S(1)} %get-tuple-element.16), channel_id=1, source_target_pairs={{0,8},{8,16},{16,24},{24,32},{32,40},{40,48},{48,56},{56,64},{64,7... | collective-permute-start | bytes 110600 | tf_op jit(solution)/shard_map/ppermute | solution.py:495
  69.4 14.8 %collective-permute-start.12 = (bf16[48,384]{1,0:T(8,128)(2,1)S(1)}, bf16[48,384]{1,0:T(8,128)(2,1)S(1)}, u32[]{:S(2)}, u32[]{:S(2)}) collective-permute-start(bf16[48,384]{1,0:T(8,128)(2,1)S(1)} %get-tuple-element.17), channel_id=1, source_target_pairs={{8,0},{16,8},{24,16},{32,24},{40,32},{48,40},{56,48},{64,56},{72,6... | collective-permute-start | bytes 110600 | tf_op jit(solution)/shard_map/ppermute | solution.py:498
  70.7 9.9 %collective-permute-start.5 = (bf16[512,384]{1,0:T(8,128)(2,1)S(1)}, bf16[512,384]{1,0:T(8,128)(2,1)S(1)}, u32[]{:S(2)}, u32[]{:S(2)}) collective-permute-start(bf16[512,384]{1,0:T(8,128)(2,1)S(1)} %copy-done.30), channel_id=1, source_target_pairs={{0,1},{1,2},{2,3},{3,0},{4,5},{5,6},{6,7},{7,4},{8,9},{9,10},{10,1... | collective-permute-start | bytes 1179656 | tf_op jit(solution)/shard_map/ppermute | solution.py:59
  74.0 30.1 %collective-permute-start.7 = (bf16[1024,384]{1,0:T(8,128)(2,1)}, bf16[1024,384]{1,0:T(8,128)(2,1)}, u32[]{:S(2)}, u32[]{:S(2)}) collective-permute-start(bf16[1024,384]{1,0:T(8,128)(2,1)} %pad_maximum_fusion.1), channel_id=1, source_target_pairs={{0,4},{1,5},{2,6},{3,7},{4,0},{5,1},{6,2},{7,3},{8,12},{9,13},{10,... | collective-permute-start | bytes 2359304 | tf_op jit(solution)/shard_map/ppermute | solution.py:59
  74.7 29.3 %collective-permute-start.1 = (bf16[768,384]{1,0:T(8,128)(2,1)}, bf16[768,384]{1,0:T(8,128)(2,1)}, u32[]{:S(2)}, u32[]{:S(2)}) collective-permute-start(bf16[768,384]{1,0:T(8,128)(2,1)} %slice.88), channel_id=1, source_target_pairs={{0,1},{1,2},{2,3},{3,0},{4,5},{5,6},{6,7},{7,4},{8,9},{9,10},{10,1... | collective-permute-start | bytes 1769480 | tf_op jit(solution)/shard_map/ppermute | solution.py:59
  80.6 23.4 %collective-permute-start.3 = (bf16[768,384]{1,0:T(8,128)(2,1)}, bf16[768,384]{1,0:T(8,128)(2,1)}, u32[]{:S(2)}, u32[]{:S(2)}) collective-permute-start(bf16[768,384]{1,0:T(8,128)(2,1)} %slice.89), channel_id=1, source_target_pairs={{0,3},{1,0},{2,1},{3,2},{4,7},{5,4},{6,5},{7,6},{8,11},{9,8},{10,9... | collective-permute-start | bytes 1769480 | tf_op jit(solution)/shard_map/ppermute | solution.py:59
  83.5 20.6 %collective-permute-start.10 = (bf16[768,384]{1,0:T(8,128)(2,1)}, bf16[768,384]{1,0:T(8,128)(2,1)}, u32[]{:S(2)}, u32[]{:S(2)}) collective-permute-start(bf16[768,384]{1,0:T(8,128)(2,1)} %pad_maximum_fusion.3), channel_id=1, source_target_pairs={{0,3},{1,0},{2,1},{3,2},{4,7},{5,4},{6,5},{7,6},{8,11},{9,8},{10,9... | collective-permute-start | bytes 1769480 | tf_op jit(solution)/shard_map/ppermute | solution.py:59
  84.8 21.3 %collective-permute-start.9 = (bf16[768,384]{1,0:T(8,128)(2,1)}, bf16[768,384]{1,0:T(8,128)(2,1)}, u32[]{:S(2)}, u32[]{:S(2)}) collective-permute-start(bf16[768,384]{1,0:T(8,128)(2,1)} %pad_maximum_fusion.2), channel_id=1, source_target_pairs={{0,1},{1,2},{2,3},{3,0},{4,5},{5,6},{6,7},{7,4},{8,9},{9,10},{10,1... | collective-permute-start | bytes 1769480 | tf_op jit(solution)/shard_map/ppermute | solution.py:59
  106.1 38.3 %copy-start.11 = (bf16[96,384]{1,0:T(8,128)(2,1)S(1)}, bf16[96,384]{1,0:T(8,128)(2,1)}, u32[]{:S(2)}) copy-start(bf16[96,384]{1,0:T(8,128)(2,1)} %copy-done.9) | copy-start | bytes 221188
  125.0 10.0 %collective-permute-start.15 = (bf16[2,144,768]{2,1,0:T(8,128)(2,1)S(1)}, bf16[2,144,768]{2,1,0:T(8,128)(2,1)S(1)}, u32[]{:S(2)}, u32[]{:S(2)}) collective-permute-start(bf16[2,144,768]{2,1,0:T(8,128)(2,1)S(1)} %get-tuple-element.18.refs_0_), channel_id=1, source_target_pairs={{0,4},{1,5},{2,6},{3,7},{4,0},{5,1},{6,2},{7,3},{8,12},{9,13},{10,... | collective-permute-start | bytes 1327112 | tf_op jit(solution)/shard_map/ppermute | solution.py:59
  125.7 45.2 %collective-permute-start.14 = (bf16[2,144,768]{2,1,0:T(8,128)(2,1)S(1)}, bf16[2,144,768]{2,1,0:T(8,128)(2,1)S(1)}, u32[]{:S(2)}, u32[]{:S(2)}) collective-permute-start(bf16[2,144,768]{2,1,0:T(8,128)(2,1)S(1)} %get-tuple-element.18.refs_0_), channel_id=1, source_target_pairs={{0,3},{1,0},{2,1},{3,2},{4,7},{5,4},{6,5},{7,6},{8,11},{9,8},{10,9... | collective-permute-start | bytes 1327112 | tf_op jit(solution)/shard_map/ppermute | solution.py:59
  127.1 43.8 %collective-permute-start.13 = (bf16[2,144,768]{2,1,0:T(8,128)(2,1)S(1)}, bf16[2,144,768]{2,1,0:T(8,128)(2,1)S(1)}, u32[]{:S(2)}, u32[]{:S(2)}) collective-permute-start(bf16[2,144,768]{2,1,0:T(8,128)(2,1)S(1)} %get-tuple-element.18.refs_0_), channel_id=1, source_target_pairs={{0,1},{1,2},{2,3},{3,0},{4,5},{5,6},{6,7},{7,4},{8,9},{9,10},{10,1... | collective-permute-start | bytes 1327112 | tf_op jit(solution)/shard_map/ppermute | solution.py:59
  135.0 35.9 %collective-permute-start.17 = (bf16[2,144,768]{2,1,0:T(8,128)(2,1)S(1)}, bf16[2,144,768]{2,1,0:T(8,128)(2,1)S(1)}, u32[]{:S(2)}, u32[]{:S(2)}) collective-permute-start(bf16[2,144,768]{2,1,0:T(8,128)(2,1)S(1)} %collective-permute-done.15.refs_3_), channel_id=1, source_target_pairs={{0,3},{1,0},{2,1},{3,2},{4,7},{5,4},{6,5},{7,6},{8,11},{9,8},{10,9... | collective-permute-start | bytes 1327112 | tf_op jit(solution)/shard_map/ppermute | solution.py:59
  135.0 14.9 %collective-permute-start.27 = (f32[2,32,384]{2,1,0:T(8,128)}, f32[2,32,384]{2,1,0:T(8,128)S(1)}, u32[]{:S(2)}, u32[]{:S(2)}) collective-permute-start(f32[2,32,384]{2,1,0:T(8,128)} %get-tuple-element.20), channel_id=1, source_target_pairs={{0,8},{8,16},{16,24},{24,32},{32,40},{40,48},{48,56},{56,64},{64,7... | collective-permute-start | bytes 294920 | tf_op jit(solution)/shard_map/ppermute | solution.py:495
  142.7 32.3 %collective-permute-start.16 = (bf16[2,144,768]{2,1,0:T(8,128)(2,1)S(1)}, bf16[2,144,768]{2,1,0:T(8,128)(2,1)S(1)}, u32[]{:S(2)}, u32[]{:S(2)}) collective-permute-start(bf16[2,144,768]{2,1,0:T(8,128)(2,1)S(1)} %collective-permute-done.15.refs_3_), channel_id=1, source_target_pairs={{0,1},{1,2},{2,3},{3,0},{4,5},{5,6},{6,7},{7,4},{8,9},{9,10},{10,1... | collective-permute-start | bytes 1327112 | tf_op jit(solution)/shard_map/ppermute | solution.py:59
  149.9 8.1 %collective-permute-start.28 = (f32[2,32,384]{2,1,0:T(8,128)S(1)}, f32[2,32,384]{2,1,0:T(8,128)S(1)}, u32[]{:S(2)}, u32[]{:S(2)}) collective-permute-start(f32[2,32,384]{2,1,0:T(8,128)S(1)} %copy-done.27), channel_id=1, source_target_pairs={{8,0},{16,8},{24,16},{32,24},{40,32},{48,40},{56,48},{64,56},{72,6... | collective-permute-start | bytes 294920 | tf_op jit(solution)/shard_map/ppermute | solution.py:498
  158.0 23.2 %collective-permute-start.20 = (bf16[144,384]{1,0:T(8,128)(2,1)}, bf16[144,384]{1,0:T(8,128)(2,1)S(1)}, u32[]{:S(2)}, u32[]{:S(2)}) collective-permute-start(bf16[144,384]{1,0:T(8,128)(2,1)} %get-tuple-element.34), channel_id=1, source_target_pairs={{0,1},{1,2},{2,3},{3,0},{4,5},{5,6},{6,7},{7,4},{8,9},{9,10},{10,1... | collective-permute-start | bytes 331784 | tf_op jit(solution)/shard_map/ppermute | solution.py:59
  165.3 15.9 %all-to-all-start.1 = ((bf16[8,32,384]{2,1,0:T(8,128)(2,1)}), bf16[8,32,384]{2,1,0:T(8,128)(2,1)}, u32[]{:S(2)}, u32[]{:S(2)}) async-start(bf16[8,32,384]{2,1,0:T(8,128)(2,1)} %audio_out.1), calls=%async_computation.1 | async-start | bytes 393216 | tf_op jit(solution)/shard_map/all_to_all | solution.py:547
  171.8 25.8 %collective-permute-start.19 = (bf16[2,144,768]{2,1,0:T(8,128)(2,1)}, bf16[2,144,768]{2,1,0:T(8,128)(2,1)S(1)}, u32[]{:S(2)}, u32[]{:S(2)}) collective-permute-start(bf16[2,144,768]{2,1,0:T(8,128)(2,1)} %pad_maximum_fusion.5), channel_id=1, source_target_pairs={{0,3},{1,0},{2,1},{3,2},{4,7},{5,4},{6,5},{7,6},{8,11},{9,8},{10,9... | collective-permute-start | bytes 1327112 | tf_op jit(solution)/shard_map/ppermute | solution.py:59
  175.9 21.7 %collective-permute-start.18 = (bf16[2,144,768]{2,1,0:T(8,128)(2,1)}, bf16[2,144,768]{2,1,0:T(8,128)(2,1)}, u32[]{:S(2)}, u32[]{:S(2)}) collective-permute-start(bf16[2,144,768]{2,1,0:T(8,128)(2,1)} %pad_maximum_fusion.4), channel_id=1, source_target_pairs={{0,1},{1,2},{2,3},{3,0},{4,5},{5,6},{6,7},{7,4},{8,9},{9,10},{10,1... | collective-permute-start | bytes 1327112 | tf_op jit(solution)/shard_map/ppermute | solution.py:59
  176.4 8.7 %collective-permute-start.21 = (bf16[144,384]{1,0:T(8,128)(2,1)}, bf16[144,384]{1,0:T(8,128)(2,1)S(1)}, u32[]{:S(2)}, u32[]{:S(2)}) collective-permute-start(bf16[144,384]{1,0:T(8,128)(2,1)} %get-tuple-element.33), channel_id=1, source_target_pairs={{0,3},{1,0},{2,1},{3,2},{4,7},{5,4},{6,5},{7,6},{8,11},{9,8},{10,9... | collective-permute-start | bytes 331784 | tf_op jit(solution)/shard_map/ppermute | solution.py:59
  179.7 10.4 %collective-permute-start.22 = (bf16[144,384]{1,0:T(8,128)(2,1)}, bf16[144,384]{1,0:T(8,128)(2,1)S(1)}, u32[]{:S(2)}, u32[]{:S(2)}) collective-permute-start(bf16[144,384]{1,0:T(8,128)(2,1)} %get-tuple-element.32), channel_id=1, source_target_pairs={{0,4},{1,5},{2,6},{3,7},{4,0},{5,1},{6,2},{7,3},{8,12},{9,13},{10,... | collective-permute-start | bytes 331784 | tf_op jit(solution)/shard_map/ppermute | solution.py:59
  181.2 9.0 %collective-permute-start.23 = (bf16[144,384]{1,0:T(8,128)(2,1)}, bf16[144,384]{1,0:T(8,128)(2,1)}, u32[]{:S(2)}, u32[]{:S(2)}) collective-permute-start(bf16[144,384]{1,0:T(8,128)(2,1)} %get-tuple-element.31), channel_id=1, source_target_pairs={{0,5},{1,6},{2,7},{3,4},{4,1},{5,2},{6,3},{7,0},{8,13},{9,14},{10,... | collective-permute-start | bytes 331784 | tf_op jit(solution)/shard_map/ppermute | solution.py:59
  185.2 9.9 %collective-permute-start.24 = (bf16[144,384]{1,0:T(8,128)(2,1)}, bf16[144,384]{1,0:T(8,128)(2,1)S(1)}, u32[]{:S(2)}, u32[]{:S(2)}) collective-permute-start(bf16[144,384]{1,0:T(8,128)(2,1)} %get-tuple-element.30), channel_id=1, source_target_pairs={{0,7},{1,4},{2,5},{3,6},{4,3},{5,0},{6,1},{7,2},{8,15},{9,12},{10,... | collective-permute-start | bytes 331784 | tf_op jit(solution)/shard_map/ppermute | solution.py:59
  190.1 6.5 %collective-permute-start.25 = (bf16[144,384]{1,0:T(8,128)(2,1)}, bf16[144,384]{1,0:T(8,128)(2,1)S(1)}, u32[]{:S(2)}, u32[]{:S(2)}) collective-permute-start(bf16[144,384]{1,0:T(8,128)(2,1)} %get-tuple-element.29), channel_id=1, source_target_pairs={{0,2},{1,3},{2,0},{3,1},{4,6},{5,7},{6,4},{7,5},{8,10},{9,11},{10,... | collective-permute-start | bytes 331784 | tf_op jit(solution)/shard_map/ppermute | solution.py:59
  190.2 7.4 %collective-permute-start.26 = (bf16[144,384]{1,0:T(8,128)(2,1)}, bf16[144,384]{1,0:T(8,128)(2,1)S(1)}, u32[]{:S(2)}, u32[]{:S(2)}) collective-permute-start(bf16[144,384]{1,0:T(8,128)(2,1)} %get-tuple-element.28), channel_id=1, source_target_pairs={{0,6},{1,7},{2,4},{3,5},{4,2},{5,3},{6,0},{7,1},{8,14},{9,15},{10,... | collective-permute-start | bytes 331784 | tf_op jit(solution)/shard_map/ppermute | solution.py:59
  (32 other events, 277.0 us)

commit v2 on v0

v2 whole, which is shorter than its diff:
```python
import functools
import math

import jax
import jax.numpy as jnp
import numpy as np
from jax import lax
from jax.experimental import pallas as pl
from jax.experimental.pallas import tpu as pltpu
from jax.sharding import PartitionSpec as P

D = 3072
HEAD = 128
HEADS_DEV = 3
GROUP = HEADS_DEV * HEAD
N_TENSOR = 8
VID = 1536
AUD = 32
REACH = 8
SPAN = AUD + 2 * REACH
KEYS = HEADS_DEV * SPAN
PACKED = AUD + 2 * REACH
SHARDS = 16
TILE = 256
TILES = VID // TILE
THIRD = VID // 3
AT_SHARD = 8
AT_VIDEO = 9
AT_AUDIO = 25
AT_VWIN = 41
AT_AWIN = 73
EPS = 1e-6
SCALE = math.log2(math.e) / math.sqrt(HEAD)
F32 = jnp.float32
BF16 = jnp.bfloat16


def cost(microseconds):
    return pl.CostEstimate(
        flops=int(microseconds * 1e9), bytes_accessed=0, transcendentals=0
    )


def dot(a, b):
    return jnp.dot(a, b, preferred_element_type=F32)


def dot_nt(a, b):
    return lax.dot_general(a, b, (((1,), (1,)), ((), ())), preferred_element_type=F32)


def dot_tn(a, b):
    return lax.dot_general(a, b, (((0,), (0,)), ((), ())), preferred_element_type=F32)


ANY = pl.BlockSpec(memory_space=pl.ANY)


def after(kernel, scalars, inputs, extra):
    def run(*refs):
        kernel(*refs[: scalars + inputs], *refs[scalars + inputs + extra :])

    return run


def gate(arrays, *extra):
    count = len(arrays)
    return pl.pallas_call(
        lambda *refs: None,
        in_specs=[ANY] * (count + len(extra)),
        out_specs=[ANY] * count,
        out_shape=[jax.ShapeDtypeStruct(a.shape, a.dtype) for a in arrays],
        input_output_aliases={i: i for i in range(count)},
        compiler_params=pltpu.CompilerParams(vmem_limit_bytes=2**20),
        cost_estimate=cost(0),
        name="gate",
    )(*arrays, *extra)


def moved(index, dy, dx):
    return (index // 4 + dy) % 2 * 4 + (index % 4 + dx) % 4


def send(array, dy, dx):
    pairs = [(i, moved(i, dy, dx)) for i in range(N_TENSOR)]
    return lax.ppermute(array, "tensor", pairs)


def right(array):
    return send(array, 0, 1)


def left(array):
    return send(array, 0, 3)


def across(array):
    return send(array, 1, 0)


def cat(*arrays):
    return jnp.concatenate(arrays, axis=0)


VMEM = pl.BlockSpec(memory_space=pltpu.VMEM)
SMEM = pl.BlockSpec(memory_space=pltpu.SMEM)


def rows_of(t):
    return pl.ds(pl.multiple_of(t * TILE, TILE), TILE)


def call(kernel, name, micros, inputs, extra, outputs, scratch):
    return pl.pallas_call(
        after(kernel, 0, len(inputs), len(extra)),
        in_specs=[spec for spec, _ in inputs] + [ANY] * len(extra),
        out_specs=[spec for spec, _ in outputs],
        out_shape=[shape for _, shape in outputs],
        scratch_shapes=scratch,
        compiler_params=pltpu.CompilerParams(vmem_limit_bytes=60 * 2**20),
        cost_estimate=cost(micros),
        name=name,
    )(*[array for _, array in inputs], *extra)


def sds(shape, dtype):
    return jax.ShapeDtypeStruct(shape, dtype)


def audio_in_kernel(a_ref, wq, wk, wv, qkv_ref, prev_ref, next_ref, wcat, normed, sems):
    def weight(part, j):
        ref, tower = ((wq, 1), (wk, 0), (wv, 0))[part]
        rows = pl.ds(j * GROUP, GROUP)
        cols = pl.ds(part * GROUP, GROUP)
        return pltpu.make_async_copy(
            ref.at[tower, rows, :], wcat.at[rows, cols], sems.at[3 * j + part]
        )

    for j in range(N_TENSOR):
        for part in range(3):
            weight(part, j).start()

    values = a_ref[...].astype(F32)
    mean = jnp.sum(jnp.sum(values, axis=0), axis=-1, keepdims=True) / D
    centred = values - mean[None]
    var = jnp.sum(jnp.sum(centred * centred, axis=0), axis=-1, keepdims=True) / D
    normed[...] = (centred * lax.rsqrt(var + EPS)[None]).astype(BF16)

    total = jnp.zeros((AUD, 3 * GROUP), F32)
    for j in range(N_TENSOR):
        for part in range(3):
            weight(part, j).wait()
        total = total + dot(normed[j], wcat[j * GROUP : (j + 1) * GROUP, :])

    heads = []
    for h in range(2 * HEADS_DEV):
        part = total[:, h * HEAD : (h + 1) * HEAD]
        mean_square = jnp.mean(part * part, axis=-1, keepdims=True)
        heads.append(part * lax.rsqrt(mean_square + EPS))
    q = jnp.concatenate(heads[:HEADS_DEV], axis=1)
    k = jnp.concatenate(heads[HEADS_DEV:], axis=1)
    v = total[:, 2 * GROUP :]
    qkv_ref[...] = cat(q, k, v).astype(BF16)
    prev_ref[...] = cat(q, k[:REACH], v[:REACH]).astype(BF16)
    next_ref[...] = cat(q, k[AUD - REACH :], v[AUD - REACH :]).astype(BF16)


def audio_in(gathered, w_query, w_key, w_value, *extra):
    return call(
        audio_in_kernel,
        "audio_in",
        2,
        [(VMEM, gathered), (ANY, w_query), (ANY, w_key), (ANY, w_value)],
        extra,
        [
            (VMEM, sds((3 * AUD, GROUP), BF16)),
            (VMEM, sds((PACKED, GROUP), BF16)),
            (VMEM, sds((PACKED, GROUP), BF16)),
        ],
        [
            pltpu.VMEM((D, 3 * GROUP), BF16),
            pltpu.VMEM((N_TENSOR, AUD, GROUP), BF16),
            pltpu.SemaphoreType.DMA((3 * N_TENSOR,)),
        ],
    )


def head_rows(w_ref, tower, wbuf, sems):
    return [
        pltpu.make_async_copy(
            w_ref.at[tower, h * HEAD : (h + 1) * HEAD, :],
            wbuf.at[h * HEAD : (h + 1) * HEAD, :],
            sems.at[h],
        )
        for h in range(HEADS_DEV)
    ]


def value_out_kernel(qkv_ref, prev_ref, next_ref, w_ref, out_ref, wbuf, sems):
    copies = head_rows(w_ref, 0, wbuf, sems)
    for copy in copies:
        copy.start()
    before = prev_ref[...].astype(F32)[AUD + REACH :]
    own = qkv_ref[...].astype(F32)[2 * AUD :]
    behind = next_ref[...].astype(F32)[AUD + REACH :]
    values = cat(before, own, behind).astype(BF16)
    for h in range(HEADS_DEV):
        copies[h].wait()
        product = dot(values[:, h * HEAD : (h + 1) * HEAD], wbuf[h * HEAD : (h + 1) * HEAD, :])
        product = product.astype(BF16)
        for j in range(N_TENSOR):
            out_ref[j, h * SPAN : (h + 1) * SPAN, :] = product[:, j * GROUP : (j + 1) * GROUP]


def value_out(qkv, from_prev, from_next, w_out, *extra):
    (out,) = call(
        value_out_kernel,
        "value_out",
        1,
        [(VMEM, qkv), (VMEM, from_prev), (VMEM, from_next), (ANY, w_out)],
        extra,
        [(VMEM, sds((N_TENSOR, KEYS, GROUP), BF16))],
        [pltpu.VMEM((GROUP, D), BF16), pltpu.SemaphoreType.DMA((HEADS_DEV,))],
    )
    return out


def row_stats(block):
    values = block.astype(F32)
    mean = jnp.mean(values, axis=-1, keepdims=True)
    centred = values - mean
    return mean, jnp.sum(centred * centred, axis=-1, keepdims=True)


def merged_stats(stat, count1, block):
    count2 = block.shape[1]
    mean1, square1 = stat[:, :1], stat[:, 1:2]
    mean2, square2 = row_stats(block)
    gap = mean2 - mean1
    total = count1 + count2
    mean = mean1 + gap * (count2 / total)
    return mean, square1 + square2 + gap * gap * (count1 * count2 / total)


def packed_stats(mean, square):
    lane = lax.broadcasted_iota(jnp.int32, (TILE, HEAD), 1)
    return jnp.where(lane == 0, mean, square)


def weight_copies(meta_ref, weights, first, count, wcat, sems):
    copies = []
    for part, (ref, tower) in enumerate(weights):
        for j in range(count):
            row = pl.multiple_of(meta_ref[first + j] * GROUP, GROUP)
            copies.append(
                pltpu.make_async_copy(
                    ref.at[tower, pl.ds(row, GROUP), :],
                    wcat.at[j * GROUP : (j + 1) * GROUP, part * GROUP : (part + 1) * GROUP],
                    sems.at[part * count + j],
                )
            )
    return copies


def column_sums(wcat):
    return dot(jnp.ones((8, wcat.shape[0]), BF16), wcat[...])


def stage_kernel(first, count, start, meta_ref, *refs):
    x_refs, weights, refs = refs[:count], refs[count : count + 3], refs[count + 3 :]
    if not start:
        acc_in, stat_in, sums_in = refs[:3]
        refs = refs[3:]
    acc_ref, stat_ref, sums_ref, wcat, xbuf, acc, stat, wsem, xsem, insem, outsem = refs

    def x_copy(t, j):
        return pltpu.make_async_copy(
            x_refs[j].at[rows_of(t), :],
            xbuf.at[rows_of(t), pl.ds(j * GROUP, GROUP)],
            xsem.at[t * count + j],
        )

    def in_copies(t):
        if start:
            return []
        return [
            pltpu.make_async_copy(acc_in.at[rows_of(t), :], acc.at[rows_of(t), :], insem.at[t]),
            pltpu.make_async_copy(
                stat_in.at[rows_of(t), :], stat.at[rows_of(t), :], insem.at[TILES + t]
            ),
        ]

    def out_copies(t):
        return [
            pltpu.make_async_copy(acc.at[rows_of(t), :], acc_ref.at[rows_of(t), :], outsem.at[t]),
            pltpu.make_async_copy(
                stat.at[rows_of(t), :], stat_ref.at[rows_of(t), :], outsem.at[TILES + t]
            ),
        ]

    wq, wk, wv = weights
    w_copies = weight_copies(meta_ref, ((wq, 0), (wk, 1), (wv, 1)), first, count, wcat, wsem)
    for copy in w_copies:
        copy.start()

    def fetch(t):
        for j in range(count):
            x_copy(t, j).start()
        for copy in in_copies(t):
            copy.start()

    fetch(0)
    for copy in w_copies:
        copy.wait()
    for t in range(1, TILES):
        fetch(t)
    here = column_sums(wcat)
    sums_ref[...] = here if start else sums_in[...] + here

    @pl.loop(0, TILES)
    def _(t):
        for j in range(count):
            x_copy(t, j).wait()
        for copy in in_copies(t):
            copy.wait()
        rows = rows_of(t)
        block = xbuf[rows, :]
        total = dot(block, wcat[...])
        if start:
            acc[rows, :] = total
            stat[rows, :] = packed_stats(*row_stats(block))
        else:
            acc[rows, :] += total
            stat[rows, :] = packed_stats(*merged_stats(stat[rows, :], first * GROUP, block))
        for copy in out_copies(t):
            copy.start()

    for t in range(TILES):
        for copy in out_copies(t):
            copy.wait()


def stage(meta, blocks, w_query, w_key, w_value, first, before=(), extra=()):
    count, start = len(blocks), not before
    state = [(ANY, a) for a in before[:2]] + [(VMEM, a) for a in before[2:]]
    return call(
        functools.partial(stage_kernel, first, count, start),
        f"stage_{first}",
        4,
        [(SMEM, meta)]
        + [(ANY, a) for a in blocks]
        + [(ANY, w_query), (ANY, w_key), (ANY, w_value)]
        + state,
        extra,
        [
            (ANY, sds((VID, 3 * GROUP), F32)),
            (ANY, sds((VID, HEAD), F32)),
            (VMEM, sds((8, 3 * GROUP), F32)),
        ],
        [
            pltpu.VMEM((count * GROUP, 3 * GROUP), BF16),
            pltpu.VMEM((VID, count * GROUP), BF16),
            pltpu.VMEM((VID, 3 * GROUP), F32),
            pltpu.VMEM((VID, HEAD), F32),
            pltpu.SemaphoreType.DMA((3 * count,)),
            pltpu.SemaphoreType.DMA((TILES * count,)),
            pltpu.SemaphoreType.DMA((2 * TILES,)),
            pltpu.SemaphoreType.DMA((2 * TILES,)),
        ],
    )


def head_norm(part, floor):
    mean_square = jnp.mean(part * part, axis=-1, keepdims=True)
    return (part * lax.rsqrt(mean_square + floor)).astype(BF16)


def last_fetch(pieces, acc_ref, cols, stat_ref, xbuf, acc, stat, sems):
    def copies(t, piece=None):
        place = pl.ds((t % 2) * TILE, TILE) if isinstance(t, int) else pl.ds(0, TILE)
        source = pieces[0 if piece is None else piece]
        return [
            pltpu.make_async_copy(source.at[place, :], xbuf.at[rows_of(t), :], sems.at[t]),
            pltpu.make_async_copy(
                acc_ref.at[rows_of(t), cols], acc.at[rows_of(t), :], sems.at[TILES + t]
            ),
            pltpu.make_async_copy(
                stat_ref.at[rows_of(t), :], stat.at[rows_of(t), :], sems.at[2 * TILES + t]
            ),
        ]

    for t in range(TILES):
        for copy in copies(t, t // 2):
            copy.start()

    def wait(t):
        for copy in copies(t):
            copy.wait()

    return wait


def query_kernel(
    meta_ref, xa, xb, xc, wq, acc_ref, stat_ref, sums_ref, qkv_ref, prev_ref, next_ref,
    pt_ref, stat_out, wcat, xbuf, acc, stat, ptbuf, wsem, insem, outsem,
):
    (w_copy,) = weight_copies(meta_ref, ((wq, 0),), 7, 1, wcat, wsem)
    w_copy.start()
    wait = last_fetch((xa, xb, xc), acc_ref, pl.ds(0, GROUP), stat_ref, xbuf, acc, stat, insem)

    shard = meta_ref[AT_SHARD]
    before = prev_ref[...].astype(F32)
    own = qkv_ref[...].astype(F32)
    behind = next_ref[...].astype(F32)
    keys = cat(
        before[AUD : AUD + REACH], own[AUD : 2 * AUD], behind[AUD : AUD + REACH]
    ).astype(BF16)

    prev_at, next_at = jnp.maximum(shard - 1, 0), jnp.minimum(shard + 1, SHARDS - 1)
    slot = lax.broadcasted_iota(jnp.int32, (SPAN, 1), 0)
    end_prev = jnp.where(shard > 0, meta_ref[AT_AUDIO + prev_at] - (AUD - REACH), 0)
    reach = jnp.minimum(meta_ref[AT_AUDIO + next_at], meta_ref[AT_VWIN + 2 * shard + 1])
    end_next = jnp.where(shard < SHARDS - 1, REACH + AUD + reach, 0)
    used = (slot >= REACH - meta_ref[AT_VWIN + 2 * shard]) & (slot < jnp.minimum(end_prev, REACH))
    used |= (slot >= REACH) & (slot < REACH + meta_ref[AT_AUDIO + shard])
    used |= (slot >= REACH + AUD) & (slot < end_next)

    w_copy.wait()
    sums = sums_ref[:1, :GROUP] + column_sums(wcat)[:1]

    def out_copies(t):
        return [
            pltpu.make_async_copy(ptbuf.at[t], pt_ref.at[t], outsem.at[t]),
            pltpu.make_async_copy(
                stat.at[rows_of(t), :], stat_out.at[rows_of(t), :], outsem.at[TILES + t]
            ),
        ]

    @pl.loop(0, TILES)
    def _(t):
        wait(t)
        rows = rows_of(t)
        block = xbuf[rows, :]
        mean, square = merged_stats(stat[rows, :], 7 * GROUP, block)
        var = square / D
        stat[rows, :] = packed_stats(mean, var)
        total = acc[rows, :] + dot(block, wcat[...]) - mean * sums
        floor = EPS * (var + EPS)
        for h in range(HEADS_DEV):
            cols = slice(h * HEAD, (h + 1) * HEAD)
            scores = dot_nt(keys[:, cols], head_norm(total[:, cols], floor))
            weights = jnp.where(used, jnp.exp2(scores * SCALE), 0.0)
            below = jnp.sum(weights, axis=0, keepdims=True)
            ptbuf[t, h * SPAN : (h + 1) * SPAN, :] = (weights * (1.0 / below)).astype(BF16)
        for copy in out_copies(t):
            copy.start()

    for t in range(TILES):
        for copy in out_copies(t):
            copy.wait()


def queries_out(meta, pieces, w_query, acc, stat, sums, qkv, from_prev, from_next, *extra):
    return call(
        query_kernel,
        "queries_out",
        2,
        [(SMEM, meta)]
        + [(ANY, a) for a in pieces]
        + [(ANY, w_query), (ANY, acc), (ANY, stat)]
        + [(VMEM, sums), (VMEM, qkv), (VMEM, from_prev), (VMEM, from_next)],
        extra,
        [(ANY, sds((TILES, KEYS, TILE), BF16)), (ANY, sds((VID, HEAD), F32))],
        [
            pltpu.VMEM((GROUP, GROUP), BF16),
            pltpu.VMEM((VID, GROUP), BF16),
            pltpu.VMEM((VID, GROUP), F32),
            pltpu.VMEM((VID, HEAD), F32),
            pltpu.VMEM((TILES, KEYS, TILE), BF16),
            pltpu.SemaphoreType.DMA((1,)),
            pltpu.SemaphoreType.DMA((3 * TILES,)),
            pltpu.SemaphoreType.DMA((2 * TILES,)),
        ],
    )


def audio_part_kernel(
    meta_ref, xa, xb, xc, wk, wv, acc_ref, stat_ref, sums_ref, qkv_ref, prev_ref, next_ref,
    part_p, part_o, part_n, wcat, xbuf, acc, stat, wsem, insem,
):
    w_copies = weight_copies(meta_ref, ((wk, 1), (wv, 1)), 7, 1, wcat, wsem)
    for copy in w_copies:
        copy.start()
    cols = pl.ds(GROUP, 2 * GROUP)
    wait = last_fetch((xa, xb, xc), acc_ref, cols, stat_ref, xbuf, acc, stat, insem)

    shard = meta_ref[AT_SHARD]
    queries = cat(prev_ref[:AUD], qkv_ref[:AUD], next_ref[:AUD])
    for ref in (part_p, part_o, part_n):
        ref[...] = jnp.zeros_like(ref)

    prev_at, next_at = jnp.maximum(shard - 1, 0), jnp.minimum(shard + 1, SHARDS - 1)
    count = meta_ref[AT_VIDEO + shard]
    row = lax.broadcasted_iota(jnp.int32, (3 * AUD, 1), 0)
    high_prev = jnp.where(shard > 0, jnp.minimum(count, meta_ref[AT_AWIN + 2 * prev_at + 1]), 0)
    high_next = jnp.where(shard < SHARDS - 1, count, 0)
    low = jnp.where(row < 2 * AUD, 0, VID - meta_ref[AT_AWIN + 2 * next_at])
    high = jnp.where(row < AUD, high_prev, jnp.where(row < 2 * AUD, count, high_next))

    for copy in w_copies:
        copy.wait()
    sums = sums_ref[:1, GROUP:] + column_sums(wcat)[:1]

    @pl.loop(0, TILES)
    def _(t):
        wait(t)
        rows = rows_of(t)
        block = xbuf[rows, :]
        mean, var = stat[rows, :1], stat[rows, 1:2]
        total = acc[rows, :] + dot(block, wcat[...]) - mean * sums
        floor = EPS * (var + EPS)
        spread = lax.rsqrt(var + EPS)
        place = t * TILE + lax.broadcasted_iota(jnp.int32, (3 * AUD, TILE), 1)
        seen = (place >= low) & (place < high)
        for h in range(HEADS_DEV):
            cols = slice(h * HEAD, (h + 1) * HEAD)
            value = (total[:, GROUP + h * HEAD : GROUP + (h + 1) * HEAD] * spread).astype(BF16)
            scores = dot_nt(queries[:, cols], head_norm(total[:, cols], floor))
            weights = jnp.where(seen, jnp.exp2(scores * SCALE), 0.0)
            bottom = jnp.broadcast_to(jnp.sum(weights, axis=1, keepdims=True), (3 * AUD, HEAD))
            top = dot(weights.astype(BF16), value)
            for g, ref in enumerate((part_p, part_o, part_n)):
                ref[0, :, cols] += top[g * AUD : (g + 1) * AUD]
                ref[1, :, cols] += bottom[g * AUD : (g + 1) * AUD]


def audio_part(meta, pieces, w_key, w_value, acc, stat, sums, qkv, from_prev, from_next):
    return call(
        audio_part_kernel,
        "audio_part",
        0,
        [(SMEM, meta)]
        + [(ANY, a) for a in pieces]
        + [(ANY, w_key), (ANY, w_value), (ANY, acc), (ANY, stat)]
        + [(VMEM, sums), (VMEM, qkv), (VMEM, from_prev), (VMEM, from_next)],
        (),
        [(VMEM, sds((2, AUD, GROUP), F32))] * 3,
        [
            pltpu.VMEM((GROUP, 2 * GROUP), BF16),
            pltpu.VMEM((VID, GROUP), BF16),
            pltpu.VMEM((VID, 2 * GROUP), F32),
            pltpu.VMEM((VID, HEAD), F32),
            pltpu.SemaphoreType.DMA((2,)),
            pltpu.SemaphoreType.DMA((3 * TILES,)),
        ],
    )


def audio_out_kernel(own_ref, prev_ref, next_ref, w_ref, out_ref, wbuf, sems):
    copies = head_rows(w_ref, 1, wbuf, sems)
    for copy in copies:
        copy.start()
    total = own_ref[...] + prev_ref[...] + next_ref[...]
    attended = (total[0] / total[1]).astype(BF16)
    for copy in copies:
        copy.wait()
    for j in range(N_TENSOR):
        out_ref[j] = dot(attended, wbuf[:, j * GROUP : (j + 1) * GROUP]).astype(BF16)


def audio_out(own, from_prev, from_next, w_out, *extra):
    (out,) = call(
        audio_out_kernel,
        "audio_out",
        0,
        [(VMEM, own), (VMEM, from_prev), (VMEM, from_next), (ANY, w_out)],
        extra,
        [(VMEM, sds((N_TENSOR, AUD, GROUP), BF16))],
        [pltpu.VMEM((GROUP, D), BF16), pltpu.SemaphoreType.DMA((HEADS_DEV,))],
    )
    return out


def value_copy(meta_ref, v_ref, j, at, projected, sem):
    return pltpu.make_async_copy(
        v_ref.at[meta_ref[j]], projected.at[at * KEYS : (at + 1) * KEYS, :], sem
    )


def output_first_kernel(meta_ref, *refs):
    p_refs, v_ref = refs[:7], refs[7]
    out_ref, projected, probs, out, vsem, psem, outsem = refs[8:]

    def p_copy(t, j):
        return pltpu.make_async_copy(
            p_refs[j].at[t], probs.at[t, pl.ds(j * KEYS, KEYS), :], psem.at[t * 7 + j]
        )

    def out_copy(t):
        return pltpu.make_async_copy(out.at[rows_of(t), :], out_ref.at[rows_of(t), :], outsem.at[t])

    v_copies = [value_copy(meta_ref, v_ref, j, j, projected, vsem.at[j]) for j in range(7)]
    for copy in v_copies:
        copy.start()
    for t in range(TILES):
        for j in range(7):
            p_copy(t, j).start()
    for copy in v_copies:
        copy.wait()

    @pl.loop(0, TILES)
    def _(t):
        for j in range(7):
            p_copy(t, j).wait()
        out[rows_of(t), :] = dot_tn(probs[t], projected[...])
        out_copy(t).start()

    for t in range(TILES):
        out_copy(t).wait()


def output_first(meta, probs, values, *extra):
    (out,) = call(
        output_first_kernel,
        "output_first",
        0,
        [(SMEM, meta)] + [(ANY, p) for p in probs] + [(ANY, values)],
        extra,
        [(ANY, sds((VID, GROUP), F32))],
        [
            pltpu.VMEM((7 * KEYS, GROUP), BF16),
            pltpu.VMEM((TILES, 7 * KEYS, TILE), BF16),
            pltpu.VMEM((VID, GROUP), F32),
            pltpu.SemaphoreType.DMA((7,)),
            pltpu.SemaphoreType.DMA((7 * TILES,)),
            pltpu.SemaphoreType.DMA((TILES,)),
        ],
    )
    return out


def output_last_kernel(
    meta_ref, low_ref, high_ref, v_ref, sum_ref, out_ref,
    projected, probs, sums, out, vsem, psem, outsem,
):
    def p_copy(t, source):
        return pltpu.make_async_copy(source, probs.at[t], psem.at[t])

    def s_copy(t):
        return pltpu.make_async_copy(
            sum_ref.at[rows_of(t), :], sums.at[rows_of(t), :], psem.at[TILES + t]
        )

    def out_copy(t):
        return pltpu.make_async_copy(out.at[rows_of(t), :], out_ref.at[rows_of(t), :], outsem.at[t])

    v_copy = value_copy(meta_ref, v_ref, 7, 0, projected, vsem.at[0])
    v_copy.start()
    for t in range(TILES):
        p_copy(t, low_ref.at[t] if t < 3 else high_ref.at[t - 3]).start()
        s_copy(t).start()
    v_copy.wait()
    limit = meta_ref[AT_VIDEO + meta_ref[AT_SHARD]]

    @pl.loop(0, TILES)
    def _(t):
        p_copy(t, low_ref.at[0]).wait()
        s_copy(t).wait()
        result = sums[rows_of(t), :] + dot_tn(probs[t], projected[...])
        row = t * TILE + lax.broadcasted_iota(jnp.int32, (TILE, 1), 0)
        out[rows_of(t), :] = jnp.where(row < limit, result, 0.0).astype(BF16)
        out_copy(t).start()

    for t in range(TILES):
        out_copy(t).wait()


def output_last(meta, low, high, values, sums):
    (out,) = call(
        output_last_kernel,
        "output_last",
        1,
        [(SMEM, meta), (ANY, low), (ANY, high), (ANY, values), (ANY, sums)],
        (),
        [(ANY, sds((VID, GROUP), BF16))],
        [
            pltpu.VMEM((KEYS, GROUP), BF16),
            pltpu.VMEM((TILES, KEYS, TILE), BF16),
            pltpu.VMEM((VID, GROUP), F32),
            pltpu.VMEM((VID, GROUP), BF16),
            pltpu.SemaphoreType.DMA((1,)),
            pltpu.SemaphoreType.DMA((2 * TILES,)),
            pltpu.SemaphoreType.DMA((TILES,)),
        ],
    )
    return out


def shards(
    video_tokens,
    audio_tokens,
    w_query,
    w_key,
    w_value,
    w_out,
    video_counts,
    audio_counts,
    video_windows,
    audio_windows,
):
    me = lax.axis_index("tensor")
    shard = lax.axis_index(("tower", "tm"))
    up = [(i, i + 1) for i in range(SHARDS - 1)]
    down = [(i + 1, i) for i in range(SHARDS - 1)]

    def to_next(array):
        return lax.ppermute(array, ("tower", "tm"), up)

    def to_prev(array):
        return lax.ppermute(array, ("tower", "tm"), down)

    offsets = ((0, 0), (0, 3), (0, 1), (1, 0), (1, 3), (0, 2), (1, 1), (1, 2))
    places = np.array([[moved(i, dy, dx) for dy, dx in offsets] for i in range(N_TENSOR)])
    order = lax.dynamic_index_in_dim(jnp.asarray(places, jnp.int32), me, 0, keepdims=False)
    meta = jnp.concatenate(
        [
            order,
            shard.reshape(1).astype(jnp.int32),
            video_counts,
            audio_counts,
            video_windows.reshape(-1),
            audio_windows.reshape(-1),
        ]
    )

    audio_blocks = lax.all_to_all(
        jnp.broadcast_to(audio_tokens[None], (N_TENSOR, AUD, GROUP)), "tensor", 0, 0
    )
    weights = (w_query, w_key, w_value)
    (own,) = gate((video_tokens,), audio_blocks)
    xl, xr, xy = right(own), left(own), across(own)
    qkv, for_prev, for_next = audio_in(audio_blocks, w_query, w_key, w_value, own)
    from_next, from_prev = to_prev(for_prev), to_next(for_next)
    projected = value_out(qkv, from_prev, from_next, w_out)
    xl, xr, xy = gate((xl, xr, xy), projected)
    yl, xq, yr = right(xy), left(xr), across(xr)
    state = stage(meta, (own, xl, xr, xy), *weights, 0)
    yl, xq, yr = gate((yl, xq, yr), state[0])
    pieces = right(yl[:THIRD]), across(xq[THIRD : 2 * THIRD]), left(yr[2 * THIRD :])
    acc, stat, sums = stage(meta, (yl, xq, yr), *weights, 4, state)
    values = lax.all_to_all(projected, "tensor", 0, 0)

    probs, stat = queries_out(
        meta, pieces, w_query, acc, stat, sums, qkv, from_prev, from_next, values
    )
    pl_, pr_, py_ = right(probs), left(probs), across(probs)
    part_prev, part_own, part_next = audio_part(
        meta, pieces, w_key, w_value, acc, stat, sums, qkv, from_prev, from_next
    )
    pl_, pr_, py_ = gate((pl_, pr_, py_), part_prev)
    pyl, pq, pyr = right(py_), left(pr_), across(pr_)
    audio_from_next, audio_from_prev = to_prev(part_prev), to_next(part_next)
    pyl, pq, pyr = gate((pyl, pq, pyr))
    low, high = right(pyl[: TILES // 2]), left(pyr[TILES // 2 :])
    audio_parts = audio_out(part_own, audio_from_prev, audio_from_next, w_out, pyl)
    video_sums = output_first(meta, (probs, pl_, pr_, py_, pyl, pq, pyr), values, audio_parts)

    audio_sums = jnp.sum(lax.all_to_all(audio_parts, "tensor", 0, 0).astype(F32), axis=0)
    audio_limit = lax.dynamic_index_in_dim(audio_counts, shard, 0, keepdims=False)
    audio_valid = jnp.arange(AUD, dtype=jnp.int32) < audio_limit
    audio_update = jnp.where(audio_valid[:, None], audio_sums, 0.0).astype(BF16)

    video_update = output_last(meta, low, high, values, video_sums)
    return (video_update, audio_update)


def solution(mesh):
    in_specs = (
        P(("tower", "tm"), "tensor"),
        P(("tower", "tm"), "tensor"),
        P(None, None, "tensor"),
        P(None, None, "tensor"),
        P(None, None, "tensor"),
        P(None, "tensor", None),
        P(),
        P(),
        P(),
        P(),
    )
    out_specs = (P(("tower", "tm"), "tensor"), P(("tower", "tm"), "tensor"))
    return jax.shard_map(shards, mesh=mesh, in_specs=in_specs, out_specs=out_specs, check_vma=False)
```

time: 367 us -> 177 us (0.48)
  waiting for transfers between devices: 178 us -> 27 us
  Pallas kernels: 0 us -> 70.4 us
  matrix products: 41.9 us -> 0 us
  local copies, waits for them, and re-layouts: 55.7 us -> 17.6 us
  starting transfers between devices: 11.8 us -> 46.2 us
  other arithmetic: 31.8 us -> 1.36 us
  blocking collectives: 29.3 us -> 12.1 us
  between operations: 16.6 us -> 1.25 us
    unnamed x5 -> x0, waiting for transfers between devices: 113 us -> none
    pallas_call x0 -> x14, Pallas kernels: none -> 70.4 us  [the longest x9 70.4 us: call(): pl.pallas_call(after(kernel, 0, len(inputs), len(extra)), in_specs=[spec...]
    dot_general x16 -> x0, matrix products: 41.9 us -> none  [the longest x2 11.6 us: project_pair(): jnp.dot(row_block, w_value[tower_pos], preferred_element_type=jnp.float32)]
    ppermute x4 -> x21, waiting for transfers between devices: 64.1 us -> 27 us  [the longest x2 12 us: to_next(): return lax.ppermute(array, ('tower', 'tm'), up)]
    all_gather x1 -> x0, blocking collectives: 29.3 us -> none  [shards(): lax.all_gather(audio_tokens, 'tensor', axis=1, tiled=True)]
    ppermute x4 -> x21, starting transfers between devices: 11.6 us -> 38.6 us  [the longest x17 22.5 us: send(): return lax.ppermute(array, 'tensor', pairs)]
    dot_general x6 -> x0, local copies, waits for them, and re-layouts: 23.1 us -> none  [the longest x3 10.6 us: project_pair(): jnp.dot(row_block, w_key[tower_pos], preferred_element_type=jnp.float32)]
    convert_element_type x6 -> x1, other arithmetic: 15.8 us -> 0.68 us  [shards(): audio_update = jnp.where(audio_valid[:, None], audio_sums, 0.0).astype(BF16)]
  transfers between devices with their start and end apart: 7 -> 23, of which waited for: 5 -> 6; matrix products, arithmetic and copies ran while one was open for 17% -> 4% of each run, Pallas kernels for 0% -> 30%
where the time goes in v2:
time: 177 us; the launch traced here: 176 us
  Pallas kernels  70.4 us (40%)
  starting transfers between devices  46.2 us (26%)
  waiting for transfers between devices  27 us (15%)
  local copies, waits for them, and re-layouts  17.6 us (10%)
  blocking collectives  12.1 us (7%)
    pallas_call x9, Pallas kernels, call(): pl.pallas_call(after(kernel, 0, len(inputs), len(extra)), in_specs=[spec...  70.4 us
    ppermute x17, starting transfers between devices, send(): return lax.ppermute(array, 'tensor', pairs)  22.5 us
    ppermute x2, starting transfers between devices, to_next(): return lax.ppermute(array, ('tower', 'tm'), up)  13.5 us
    all_to_all x1, blocking collectives, shards(): lax.all_to_all(jnp.broadcast_to(audio_tokens[None], (N_TENSOR, AUD, GROUP...  12.1 us
    ppermute x2, waiting for transfers between devices, to_next(): return lax.ppermute(array, ('tower', 'tm'), up)  12 us
    unnamed x61, local copies, waits for them, and re-layouts  11.4 us
    ppermute x2, waiting for transfers between devices, to_prev(): return lax.ppermute(array, ('tower', 'tm'), down)  9.47 us
    ppermute x17, waiting for transfers between devices, send(): return lax.ppermute(array, 'tensor', pairs)  5.57 us
  transfers between devices with their start and end apart: 23, of which 6 were waited for; matrix products, arithmetic and copies ran while one was open for 4% of the time, Pallas kernels for 30%

profile of v2, /device:TPU:0, one launch (start us, length us, event | category | flops | bytes accessed | tf_op | source)
XLA Modules:
  0.0 175.9 jit_solution(5826667453620853641)
XLA Ops:
  0.6 1.3 copy.44.refs_0_
  1.9 12.1 %all_to_all.15.refs_1_.refs_0_ = bf16[8,32,384]{2,1,0:T(8,128)(2,1)S(1)} all-to-all(bf16[8,32,384]{2,1,0:T(8,128)(2,1)S(1)} %broadcast_in_dim.19), channel_id=1, replica_groups=mesh['tower'=2,'tm'=8,'tensor'=8] {'tensor'}, dimensions={0} | all-to-all | bytes 393216 | tf_op jit(solution)/shard_map/all_to_all | solution.py:736
  15.3 1.5 collective-permute-start.1
  17.4 5.1 %audio_in.1 = (bf16[96,384]{1,0:T(8,128)(2,1)}, bf16[48,384]{1,0:T(8,128)(2,1)}, bf16[48,384]{1,0:T(8,128)(2,1)}) custom-call(bf16[8,32,384]{2,1,0:T(8,128)(2,1)} %copy-done.9, bf16[2,3072,384]{2,1,0:T(8,128)(2,1)} %refs_4_.4, bf16[2,3072,384]{2,1,0:T(8,128)(2,1)} %refs_4_.5, bf16[2,3072,384]{2,1,0:T(8,128)(2,1)} %refs_5_.5, bf16[1536,384]{1,0:T(8,128)(2,1)} %copy-done.1), custom_call_target="tpu_custom_call" | custom-call | flops 2000000000 | tf_op jit(solution)/shard_map/audio_in/pallas_call | solution.py:114
  22.5 4.8 %collective-permute-start.3 = (bf16[48,384]{1,0:T(8,128)(2,1)}, bf16[48,384]{1,0:T(8,128)(2,1)S(1)}, u32[]{:S(2)}, u32[]{:S(2)}) collective-permute-start(bf16[48,384]{1,0:T(8,128)(2,1)} %get-tuple-element.29), channel_id=1, source_target_pairs={{0,8},{8,16},{16,24},{24,32},{32,40},{40,48},{48,56},{56,64},{64,7... | collective-permute-start | bytes 110600 | tf_op jit(solution)/shard_map/ppermute | solution.py:717
  27.3 1.3 collective-permute-start.4
  28.6 11.9 %collective-permute-done.3.refs_1_.refs_9_.refs_10_ = bf16[48,384]{1,0:T(8,128)(2,1)S(1)} collective-permute-done((bf16[48,384]{1,0:T(8,128)(2,1)}, bf16[48,384]{1,0:T(8,128)(2,1)S(1)}, u32[]{:S(2)}, u32[]{:S(2)}) %collective-permute-start.3) | collective-permute-done | bytes 36896 | tf_op jit(solution)/shard_map/ppermute | solution.py:717
  40.5 3.6 %collective-permute-done.4.refs_2_.refs_10_.refs_11_ = bf16[48,384]{1,0:T(8,128)(2,1)S(1)} collective-permute-done((bf16[48,384]{1,0:T(8,128)(2,1)}, bf16[48,384]{1,0:T(8,128)(2,1)S(1)}, u32[]{:S(2)}, u32[]{:S(2)}) %collective-permute-start.4) | collective-permute-done | bytes 36896 | tf_op jit(solution)/shard_map/ppermute | solution.py:720
  44.7 3.7 %value_out.1.refs_3_ = bf16[8,144,384]{2,1,0:T(8,128)(2,1)} custom-call(bf16[96,384]{1,0:T(8,128)(2,1)} %get-tuple-element.28.refs_0_.refs_8_.refs_9_, bf16[48,384]{1,0:T(8,128)(2,1)} %copy-done.18, bf16[48,384]{1,0:T(8,128)(2,1)} %copy-done.19, bf16[2,384,3072]{2,1,0:T(8,128)(2,1)} %refs_3_.5), custom_call_target="tpu_custom_call" | custom-call | flops 1000000000 | tf_op jit(solution)/shard_map/value_out/pallas_call | solution.py:114
  51.2 2.7 %collective-permute-start.6 = (bf16[1536,384]{1,0:T(8,128)(2,1)}, bf16[1536,384]{1,0:T(8,128)(2,1)S(1)}, u32[]{:S(2)}, u32[]{:S(2)}) collective-permute-start(bf16[1536,384]{1,0:T(8,128)(2,1)} %get-tuple-element.32.refs_3_), channel_id=1, source_target_pairs={{0,3},{1,0},{2,1},{3,2},{4,7},{5,4},{6,5},{7,6},{8,11},{9,8},{10,9... | collective-permute-start | bytes 3538952 | tf_op jit(solution)/shard_map/ppermute | solution.py:86
  53.9 4.2 %all-to-all-start.1 = ((bf16[8,144,384]{2,1,0:T(8,128)(2,1)}), bf16[8,144,384]{2,1,0:T(8,128)(2,1)}, u32[]{:S(2)}, u32[]{:S(2)}) async-start(bf16[8,144,384]{2,1,0:T(8,128)(2,1)} %value_out.1.refs_3_), calls=%async_computation.1 | async-start | bytes 1769472 | tf_op jit(solution)/shard_map/all_to_all | solution.py:751
  59.7 1.3 concatenate.3.refs_0_
  61.0 13.0 %stage_0.1 = (f32[1536,1152]{1,0:T(8,128)}, f32[1536,128]{1,0:T(8,128)}, f32[8,1152]{1,0:T(8,128)}) custom-call(s32[105]{0:T(128)} %concatenate.3.refs_0_, bf16[1536,384]{1,0:T(8,128)(2,1)} %copy-done.1, bf16[1536,384]{1,0:T(8,128)(2,1)} %copy-done.7, bf16[1536,384]{1,0:T(8,128)(2,1)} %get-tuple-element.32.refs_3_, ...), custom_call_target="tpu_custom_call" | custom-call | flops 4000000000 | tf_op jit(solution)/shard_map/stage_0/pallas_call | solution.py:114
  74.0 4.4 %collective-permute-done.5.refs_0_ = bf16[1536,384]{1,0:T(8,128)(2,1)S(1)} collective-permute-done((bf16[1536,384]{1,0:T(8,128)(2,1)}, bf16[1536,384]{1,0:T(8,128)(2,1)S(1)}, u32[]{:S(2)}, u32[]{:S(2)}) %collective-permute-start.5) | collective-permute-done | bytes 1179680 | tf_op jit(solution)/shard_map/ppermute | solution.py:86
  79.6 3.0 %copy-done = f32[1536,1152]{1,0:T(8,128)S(1)} copy-done((f32[1536,1152]{1,0:T(8,128)S(1)}, f32[1536,1152]{1,0:T(8,128)}, u32[]{:S(2)}) %copy-start) | copy-done | bytes 7077912
  83.4 1.2 slice.16
  86.5 3.5 %collective-permute-start.10 = (bf16[512,384]{1,0:T(8,128)(2,1)}, bf16[512,384]{1,0:T(8,128)(2,1)S(1)}, u32[]{:S(2)}, u32[]{:S(2)}) collective-permute-start(bf16[512,384]{1,0:T(8,128)(2,1)} %slice.17), channel_id=1, source_target_pairs={{0,3},{1,0},{2,1},{3,2},{4,7},{5,4},{6,5},{7,6},{8,11},{9,8},{10,9... | collective-permute-start | bytes 1179656 | tf_op jit(solution)/shard_map/ppermute | solution.py:86
  90.1 11.9 %stage_4.1 = (f32[1536,1152]{1,0:T(8,128)}, f32[1536,128]{1,0:T(8,128)}, f32[8,1152]{1,0:T(8,128)}) custom-call(s32[105]{0:T(128)} %concatenate.3.refs_0_, bf16[1536,384]{1,0:T(8,128)(2,1)} %copy-done.2, bf16[1536,384]{1,0:T(8,128)(2,1)} %copy-done.4, bf16[1536,384]{1,0:T(8,128)(2,1)} %copy-done.3, bf16[2,3072,384]{2,1,0:T(8,128)(2,1)} %refs_4_.4, ...), custom_call_target="tpu_custom_call" | custom-call | flops 4000000000 | tf_op jit(solution)/shard_map/stage_4/pallas_call | solution.py:114
  102.9 9.2 %queries_out.1 = (bf16[6,144,256]{2,1,0:T(8,128)(2,1)}, f32[1536,128]{1,0:T(8,128)}) custom-call(s32[105]{0:T(128)} %concatenate.3.refs_0_, bf16[512,384]{1,0:T(8,128)(2,1)} %collective-permute-done.8.refs_1_, bf16[512,384]{1,0:T(8,128)(2,1)} %copy-done.16, bf16[512,384]{1,0:T(8,128)(2,1)} %copy-done.17, bf16[2,3072,384]{2,1,0:T(8,128)(2,1)} %refs_4_.4, ...), custom_call_target="tpu_custom_call" | custom-call | flops 2000000000 | tf_op jit(solution)/shard_map/queries_out/pallas_call | solution.py:114
  112.2 1.2 collective-permute-start.13
  113.4 1.9 %collective-permute-start.12 = (bf16[6,144,256]{2,1,0:T(8,128)(2,1)}, bf16[6,144,256]{2,1,0:T(8,128)(2,1)S(1)}, u32[]{:S(2)}, u32[]{:S(2)}) collective-permute-start(bf16[6,144,256]{2,1,0:T(8,128)(2,1)} %get-tuple-element.43.refs_1_), channel_id=1, source_target_pairs={{0,3},{1,0},{2,1},{3,2},{4,7},{5,4},{6,5},{7,6},{8,11},{9,8},{10,9... | collective-permute-start | bytes 1327112 | tf_op jit(solution)/shard_map/ppermute | solution.py:86
  115.4 11.7 %audio_part.1 = (f32[2,32,384]{2,1,0:T(8,128)}, f32[2,32,384]{2,1,0:T(8,128)}, f32[2,32,384]{2,1,0:T(8,128)}) custom-call(s32[105]{0:T(128)} %concatenate.3.refs_0_, bf16[512,384]{1,0:T(8,128)(2,1)} %collective-permute-done.8.refs_1_, bf16[512,384]{1,0:T(8,128)(2,1)} %copy-done.16, bf16[512,384]{1,0:T(8,128)(2,1)} %copy-done.17, ...), custom_call_target="tpu_custom_call" | custom-call | tf_op jit(solution)/shard_map/audio_part/pallas_call | solution.py:114
  129.3 3.1 %collective-permute-start.15 = (bf16[6,144,256]{2,1,0:T(8,128)(2,1)S(1)}, bf16[6,144,256]{2,1,0:T(8,128)(2,1)S(1)}, u32[]{:S(2)}, u32[]{:S(2)}) collective-permute-start(bf16[6,144,256]{2,1,0:T(8,128)(2,1)S(1)} %get-tuple-element.47.refs_3_), channel_id=1, source_target_pairs={{0,3},{1,0},{2,1},{3,2},{4,7},{5,4},{6,5},{7,6},{8,11},{9,8},{10,9... | collective-permute-start | bytes 1327112 | tf_op jit(solution)/shard_map/ppermute | solution.py:86
  132.5 8.7 %collective-permute-start.19 = (f32[2,32,384]{2,1,0:T(8,128)S(1)}, f32[2,32,384]{2,1,0:T(8,128)S(1)}, u32[]{:S(2)}, u32[]{:S(2)}) collective-permute-start(f32[2,32,384]{2,1,0:T(8,128)S(1)} %copy-done.28), channel_id=1, source_target_pairs={{0,8},{8,16},{16,24},{24,32},{32,40},{40,48},{48,56},{56,64},{64,7... | collective-permute-start | bytes 294920 | tf_op jit(solution)/shard_map/ppermute | solution.py:717
  141.2 1.3 collective-permute-start.20
  143.4 5.8 %collective-permute-done.20.refs_2_ = f32[2,32,384]{2,1,0:T(8,128)S(1)} collective-permute-done((f32[2,32,384]{2,1,0:T(8,128)S(1)}, f32[2,32,384]{2,1,0:T(8,128)S(1)}, u32[]{:S(2)}, u32[]{:S(2)}) %collective-permute-start.20) | collective-permute-done | bytes 98336 | tf_op jit(solution)/shard_map/ppermute | solution.py:720
  149.8 3.8 %audio_out.1.refs_9_ = bf16[8,32,384]{2,1,0:T(8,128)(2,1)} custom-call(f32[2,32,384]{2,1,0:T(8,128)} %get-tuple-element.52.refs_0_, f32[2,32,384]{2,1,0:T(8,128)} %copy-done.22, f32[2,32,384]{2,1,0:T(8,128)} %copy-done.23, bf16[2,384,3072]{2,1,0:T(8,128)(2,1)} %refs_3_.5, bf16[6,144,256]{2,1,0:T(8,128)(2,1)} %copy-done.5), custom_call_target="tpu_custom_call" | custom-call | tf_op jit(solution)/shard_map/audio_out/pallas_call | solution.py:114
  153.7 3.4 %all-to-all-start.2 = ((bf16[8,32,384]{2,1,0:T(8,128)(2,1)}), bf16[8,32,384]{2,1,0:T(8,128)(2,1)S(1)}, u32[]{:S(2)}, u32[]{:S(2)}) async-start(bf16[8,32,384]{2,1,0:T(8,128)(2,1)} %audio_out.1.refs_9_), calls=%async_computation.2 | async-start | bytes 393216 | tf_op jit(solution)/shard_map/all_to_all | solution.py:768
  158.4 2.0 %collective-permute-start.17 = (bf16[3,144,256]{2,1,0:T(8,128)(2,1)S(1)}, bf16[3,144,256]{2,1,0:T(8,128)(2,1)S(1)}, u32[]{:S(2)}, u32[]{:S(2)}) collective-permute-start(bf16[3,144,256]{2,1,0:T(8,128)(2,1)S(1)} %slice.18), channel_id=1, source_target_pairs={{0,1},{1,2},{2,3},{3,0},{4,5},{5,6},{6,7},{7,4},{8,9},{9,10},{10,1... | collective-permute-start | bytes 663560 | tf_op jit(solution)/shard_map/ppermute | solution.py:86
  160.4 1.3 collective-permute-start.18
  161.7 7.0 %output_first.1.refs_4_ = f32[1536,384]{1,0:T(8,128)} custom-call(s32[105]{0:T(128)} %concatenate.3.refs_0_, bf16[6,144,256]{2,1,0:T(8,128)(2,1)} %get-tuple-element.43.refs_1_, bf16[6,144,256]{2,1,0:T(8,128)(2,1)} %copy-done.12, bf16[6,144,256]{2,1,0:T(8,128)(2,1)} %copy-done.11, bf16[6,144,256]{2,1,0:T(8,128)(2,1)} %copy-done.10, ...), custom_call_target="tpu_custom_call" | custom-call | tf_op jit(solution)/shard_map/output_first/pallas_call | solution.py:114
  170.8 4.9 %output_last.1 = bf16[1536,384]{1,0:T(8,128)(2,1)} custom-call(s32[105]{0:T(128)} %concatenate.3.refs_0_, bf16[3,144,256]{2,1,0:T(8,128)(2,1)} %copy-done.20, bf16[3,144,256]{2,1,0:T(8,128)(2,1)} %copy-done.21, bf16[8,144,384]{2,1,0:T(8,128)(2,1)} %all-to-all-done.1.refs_11_.refs_8_.refs_3_, f32[1536,384]{1,0:T(8,128)} %output_first.1.refs_4_), custom_call_target="tpu_custom_call" | custom-call | flops 1000000000 | tf_op jit(solution)/shard_map/output_last/pallas_call | solution.py:114
  (104 shorter events, 18.6 us)
Async XLA Ops:
  14.8 33.7 %collective-permute-start.2 = (bf16[1536,384]{1,0:T(8,128)(2,1)S(1)}, bf16[1536,384]{1,0:T(8,128)(2,1)}, u32[]{:S(2)}, u32[]{:S(2)}) collective-permute-start(bf16[1536,384]{1,0:T(8,128)(2,1)S(1)} %gate.5.refs_4_.refs_1_), channel_id=1, source_target_pairs={{0,4},{1,5},{2,6},{3,7},{4,0},{5,1},{6,2},{7,3},{8,12},{9,13},{10,... | collective-permute-start | bytes 3538952 | tf_op jit(solution)/shard_map/ppermute | solution.py:86
  15.3 33.2 %collective-permute-start.1 = (bf16[1536,384]{1,0:T(8,128)(2,1)S(1)}, bf16[1536,384]{1,0:T(8,128)(2,1)}, u32[]{:S(2)}, u32[]{:S(2)}) collective-permute-start(bf16[1536,384]{1,0:T(8,128)(2,1)S(1)} %gate.5.refs_4_.refs_1_), channel_id=1, source_target_pairs={{0,3},{1,0},{2,1},{3,2},{4,7},{5,4},{6,5},{7,6},{8,11},{9,8},{10,9... | collective-permute-start | bytes 3538952 | tf_op jit(solution)/shard_map/ppermute | solution.py:86
  16.8 31.7 %collective-permute-start = (bf16[1536,384]{1,0:T(8,128)(2,1)S(1)}, bf16[1536,384]{1,0:T(8,128)(2,1)S(1)}, u32[]{:S(2)}, u32[]{:S(2)}) collective-permute-start(bf16[1536,384]{1,0:T(8,128)(2,1)S(1)} %gate.5.refs_4_.refs_1_), channel_id=1, source_target_pairs={{0,1},{1,2},{2,3},{3,0},{4,5},{5,6},{6,7},{7,4},{8,9},{9,10},{10,1... | collective-permute-start | bytes 3538952 | tf_op jit(solution)/shard_map/ppermute | solution.py:86
  22.5 18.0 %collective-permute-start.3 = (bf16[48,384]{1,0:T(8,128)(2,1)}, bf16[48,384]{1,0:T(8,128)(2,1)S(1)}, u32[]{:S(2)}, u32[]{:S(2)}) collective-permute-start(bf16[48,384]{1,0:T(8,128)(2,1)} %get-tuple-element.29), channel_id=1, source_target_pairs={{0,8},{8,16},{16,24},{24,32},{32,40},{40,48},{48,56},{56,64},{64,7... | collective-permute-start | bytes 110600 | tf_op jit(solution)/shard_map/ppermute | solution.py:717
  27.3 16.8 %collective-permute-start.4 = (bf16[48,384]{1,0:T(8,128)(2,1)}, bf16[48,384]{1,0:T(8,128)(2,1)S(1)}, u32[]{:S(2)}, u32[]{:S(2)}) collective-permute-start(bf16[48,384]{1,0:T(8,128)(2,1)} %get-tuple-element.30), channel_id=1, source_target_pairs={{8,0},{16,8},{24,16},{32,24},{40,32},{48,40},{56,48},{64,56},{72,6... | collective-permute-start | bytes 110600 | tf_op jit(solution)/shard_map/ppermute | solution.py:720
  49.6 9.8 %copy-start.25 = (s32[16,2]{0,1:T(2,128)S(1)}, s32[16,2]{0,1:T(2,128)}, u32[]{:S(2)}) copy-start(s32[16,2]{0,1:T(2,128)} %param.19) | copy-start | bytes 388
  49.6 9.9 %copy-start.26 = (s32[16,2]{0,1:T(2,128)S(1)}, s32[16,2]{0,1:T(2,128)}, u32[]{:S(2)}) copy-start(s32[16,2]{0,1:T(2,128)} %param.20) | copy-start | bytes 388
  49.6 28.9 %collective-permute-start.5 = (bf16[1536,384]{1,0:T(8,128)(2,1)}, bf16[1536,384]{1,0:T(8,128)(2,1)S(1)}, u32[]{:S(2)}, u32[]{:S(2)}) collective-permute-start(bf16[1536,384]{1,0:T(8,128)(2,1)} %get-tuple-element.31.refs_4_), channel_id=1, source_target_pairs={{0,1},{1,2},{2,3},{3,0},{4,5},{5,6},{6,7},{7,4},{8,9},{9,10},{10,1... | collective-permute-start | bytes 3538952 | tf_op jit(solution)/shard_map/ppermute | solution.py:86
  50.4 28.1 %collective-permute-start.7 = (bf16[1536,384]{1,0:T(8,128)(2,1)}, bf16[1536,384]{1,0:T(8,128)(2,1)S(1)}, u32[]{:S(2)}, u32[]{:S(2)}) collective-permute-start(bf16[1536,384]{1,0:T(8,128)(2,1)} %get-tuple-element.32.refs_3_), channel_id=1, source_target_pairs={{0,4},{1,5},{2,6},{3,7},{4,0},{5,1},{6,2},{7,3},{8,12},{9,13},{10,... | collective-permute-start | bytes 3538952 | tf_op jit(solution)/shard_map/ppermute | solution.py:86
  51.2 28.3 %collective-permute-start.6 = (bf16[1536,384]{1,0:T(8,128)(2,1)}, bf16[1536,384]{1,0:T(8,128)(2,1)S(1)}, u32[]{:S(2)}, u32[]{:S(2)}) collective-permute-start(bf16[1536,384]{1,0:T(8,128)(2,1)} %get-tuple-element.32.refs_3_), channel_id=1, source_target_pairs={{0,3},{1,0},{2,1},{3,2},{4,7},{5,4},{6,5},{7,6},{8,11},{9,8},{10,9... | collective-permute-start | bytes 3538952 | tf_op jit(solution)/shard_map/ppermute | solution.py:86
  53.9 48.1 %all-to-all-start.1 = ((bf16[8,144,384]{2,1,0:T(8,128)(2,1)}), bf16[8,144,384]{2,1,0:T(8,128)(2,1)}, u32[]{:S(2)}, u32[]{:S(2)}) async-start(bf16[8,144,384]{2,1,0:T(8,128)(2,1)} %value_out.1.refs_3_), calls=%async_computation.1 | async-start | bytes 1769472 | tf_op jit(solution)/shard_map/all_to_all | solution.py:751
  85.5 16.5 %collective-permute-start.8 = (bf16[512,384]{1,0:T(8,128)(2,1)}, bf16[512,384]{1,0:T(8,128)(2,1)}, u32[]{:S(2)}, u32[]{:S(2)}) collective-permute-start(bf16[512,384]{1,0:T(8,128)(2,1)} %slice.15), channel_id=1, source_target_pairs={{0,1},{1,2},{2,3},{3,0},{4,5},{5,6},{6,7},{7,4},{8,9},{9,10},{10,1... | collective-permute-start | bytes 1179656 | tf_op jit(solution)/shard_map/ppermute | solution.py:86
  85.5 16.6 %collective-permute-start.9 = (bf16[512,384]{1,0:T(8,128)(2,1)}, bf16[512,384]{1,0:T(8,128)(2,1)S(1)}, u32[]{:S(2)}, u32[]{:S(2)}) collective-permute-start(bf16[512,384]{1,0:T(8,128)(2,1)} %slice.16), channel_id=1, source_target_pairs={{0,4},{1,5},{2,6},{3,7},{4,0},{5,1},{6,2},{7,3},{8,12},{9,13},{10,... | collective-permute-start | bytes 1179656 | tf_op jit(solution)/shard_map/ppermute | solution.py:86
  86.5 15.5 %collective-permute-start.10 = (bf16[512,384]{1,0:T(8,128)(2,1)}, bf16[512,384]{1,0:T(8,128)(2,1)S(1)}, u32[]{:S(2)}, u32[]{:S(2)}) collective-permute-start(bf16[512,384]{1,0:T(8,128)(2,1)} %slice.17), channel_id=1, source_target_pairs={{0,3},{1,0},{2,1},{3,2},{4,7},{5,4},{6,5},{7,6},{8,11},{9,8},{10,9... | collective-permute-start | bytes 1179656 | tf_op jit(solution)/shard_map/ppermute | solution.py:86
  112.2 14.9 %collective-permute-start.13 = (bf16[6,144,256]{2,1,0:T(8,128)(2,1)}, bf16[6,144,256]{2,1,0:T(8,128)(2,1)S(1)}, u32[]{:S(2)}, u32[]{:S(2)}) collective-permute-start(bf16[6,144,256]{2,1,0:T(8,128)(2,1)} %get-tuple-element.43.refs_1_), channel_id=1, source_target_pairs={{0,4},{1,5},{2,6},{3,7},{4,0},{5,1},{6,2},{7,3},{8,12},{9,13},{10,... | collective-permute-start | bytes 1327112 | tf_op jit(solution)/shard_map/ppermute | solution.py:86
  113.4 13.7 %collective-permute-start.12 = (bf16[6,144,256]{2,1,0:T(8,128)(2,1)}, bf16[6,144,256]{2,1,0:T(8,128)(2,1)S(1)}, u32[]{:S(2)}, u32[]{:S(2)}) collective-permute-start(bf16[6,144,256]{2,1,0:T(8,128)(2,1)} %get-tuple-element.43.refs_1_), channel_id=1, source_target_pairs={{0,3},{1,0},{2,1},{3,2},{4,7},{5,4},{6,5},{7,6},{8,11},{9,8},{10,9... | collective-permute-start | bytes 1327112 | tf_op jit(solution)/shard_map/ppermute | solution.py:86
  115.3 11.8 %collective-permute-start.11 = (bf16[6,144,256]{2,1,0:T(8,128)(2,1)}, bf16[6,144,256]{2,1,0:T(8,128)(2,1)S(1)}, u32[]{:S(2)}, u32[]{:S(2)}) collective-permute-start(bf16[6,144,256]{2,1,0:T(8,128)(2,1)} %get-tuple-element.43.refs_1_), channel_id=1, source_target_pairs={{0,1},{1,2},{2,3},{3,0},{4,5},{5,6},{6,7},{7,4},{8,9},{9,10},{10,1... | collective-permute-start | bytes 1327112 | tf_op jit(solution)/shard_map/ppermute | solution.py:86
  128.0 13.1 %copy-start.15 = (f32[2,32,384]{2,1,0:T(8,128)S(1)}, f32[2,32,384]{2,1,0:T(8,128)}, u32[]{:S(2)}) copy-start(f32[2,32,384]{2,1,0:T(8,128)} %get-tuple-element.45.refs_3_) | copy-start | bytes 294916
  128.0 25.6 %copy-start.10 = (bf16[6,144,256]{2,1,0:T(8,128)(2,1)}, bf16[6,144,256]{2,1,0:T(8,128)(2,1)S(1)}, u32[]{:S(2)}) copy-start(bf16[6,144,256]{2,1,0:T(8,128)(2,1)S(1)} %get-tuple-element.46.refs_4_) | copy-start | bytes 1327108
  128.0 25.6 %copy-start.11 = (bf16[6,144,256]{2,1,0:T(8,128)(2,1)}, bf16[6,144,256]{2,1,0:T(8,128)(2,1)S(1)}, u32[]{:S(2)}) copy-start(bf16[6,144,256]{2,1,0:T(8,128)(2,1)S(1)} %get-tuple-element.47.refs_3_) | copy-start | bytes 1327108
  128.0 25.6 %copy-start.12 = (bf16[6,144,256]{2,1,0:T(8,128)(2,1)}, bf16[6,144,256]{2,1,0:T(8,128)(2,1)S(1)}, u32[]{:S(2)}) copy-start(bf16[6,144,256]{2,1,0:T(8,128)(2,1)S(1)} %get-tuple-element.50.refs_2_) | copy-start | bytes 1327108
  128.0 14.4 %collective-permute-start.14 = (bf16[6,144,256]{2,1,0:T(8,128)(2,1)S(1)}, bf16[6,144,256]{2,1,0:T(8,128)(2,1)S(1)}, u32[]{:S(2)}, u32[]{:S(2)}) collective-permute-start(bf16[6,144,256]{2,1,0:T(8,128)(2,1)S(1)} %get-tuple-element.46.refs_4_), channel_id=1, source_target_pairs={{0,1},{1,2},{2,3},{3,0},{4,5},{5,6},{6,7},{7,4},{8,9},{9,10},{10,1... | collective-permute-start | bytes 1327112 | tf_op jit(solution)/shard_map/ppermute | solution.py:86
  128.3 14.2 %collective-permute-start.16 = (bf16[6,144,256]{2,1,0:T(8,128)(2,1)S(1)}, bf16[6,144,256]{2,1,0:T(8,128)(2,1)S(1)}, u32[]{:S(2)}, u32[]{:S(2)}) collective-permute-start(bf16[6,144,256]{2,1,0:T(8,128)(2,1)S(1)} %get-tuple-element.47.refs_3_), channel_id=1, source_target_pairs={{0,4},{1,5},{2,6},{3,7},{4,0},{5,1},{6,2},{7,3},{8,12},{9,13},{10,... | collective-permute-start | bytes 1327112 | tf_op jit(solution)/shard_map/ppermute | solution.py:86
  129.3 13.2 %collective-permute-start.15 = (bf16[6,144,256]{2,1,0:T(8,128)(2,1)S(1)}, bf16[6,144,256]{2,1,0:T(8,128)(2,1)S(1)}, u32[]{:S(2)}, u32[]{:S(2)}) collective-permute-start(bf16[6,144,256]{2,1,0:T(8,128)(2,1)S(1)} %get-tuple-element.47.refs_3_), channel_id=1, source_target_pairs={{0,3},{1,0},{2,1},{3,2},{4,7},{5,4},{6,5},{7,6},{8,11},{9,8},{10,9... | collective-permute-start | bytes 1327112 | tf_op jit(solution)/shard_map/ppermute | solution.py:86
  132.5 10.9 %collective-permute-start.19 = (f32[2,32,384]{2,1,0:T(8,128)S(1)}, f32[2,32,384]{2,1,0:T(8,128)S(1)}, u32[]{:S(2)}, u32[]{:S(2)}) collective-permute-start(f32[2,32,384]{2,1,0:T(8,128)S(1)} %copy-done.28), channel_id=1, source_target_pairs={{0,8},{8,16},{16,24},{24,32},{32,40},{40,48},{48,56},{56,64},{64,7... | collective-permute-start | bytes 294920 | tf_op jit(solution)/shard_map/ppermute | solution.py:717
  141.2 8.0 %collective-permute-start.20 = (f32[2,32,384]{2,1,0:T(8,128)S(1)}, f32[2,32,384]{2,1,0:T(8,128)S(1)}, u32[]{:S(2)}, u32[]{:S(2)}) collective-permute-start(f32[2,32,384]{2,1,0:T(8,128)S(1)} %copy-done.15), channel_id=1, source_target_pairs={{8,0},{16,8},{24,16},{32,24},{40,32},{48,40},{56,48},{64,56},{72,6... | collective-permute-start | bytes 294920 | tf_op jit(solution)/shard_map/ppermute | solution.py:720
  143.3 10.4 %copy-start.13 = (bf16[6,144,256]{2,1,0:T(8,128)(2,1)}, bf16[6,144,256]{2,1,0:T(8,128)(2,1)S(1)}, u32[]{:S(2)}) copy-start(bf16[6,144,256]{2,1,0:T(8,128)(2,1)S(1)} %get-tuple-element.51.refs_6_) | copy-start | bytes 1327108
  143.3 15.1 %copy-start.8 = (bf16[6,144,256]{2,1,0:T(8,128)(2,1)}, bf16[6,144,256]{2,1,0:T(8,128)(2,1)S(1)}, u32[]{:S(2)}) copy-start(bf16[6,144,256]{2,1,0:T(8,128)(2,1)S(1)} %get-tuple-element.49.refs_7_) | copy-start | bytes 1327108
  149.8 8.5 %copy-start.6 = (bf16[6,144,256]{2,1,0:T(8,128)(2,1)S(1)}, bf16[6,144,256]{2,1,0:T(8,128)(2,1)}, u32[]{:S(2)}) copy-start(bf16[6,144,256]{2,1,0:T(8,128)(2,1)} %copy-done.5) | copy-start | bytes 1327108
  153.7 15.0 %all-to-all-start.2 = ((bf16[8,32,384]{2,1,0:T(8,128)(2,1)}), bf16[8,32,384]{2,1,0:T(8,128)(2,1)S(1)}, u32[]{:S(2)}, u32[]{:S(2)}) async-start(bf16[8,32,384]{2,1,0:T(8,128)(2,1)} %audio_out.1.refs_9_), calls=%async_computation.2 | async-start | bytes 393216 | tf_op jit(solution)/shard_map/all_to_all | solution.py:768
  158.4 11.0 %collective-permute-start.17 = (bf16[3,144,256]{2,1,0:T(8,128)(2,1)S(1)}, bf16[3,144,256]{2,1,0:T(8,128)(2,1)S(1)}, u32[]{:S(2)}, u32[]{:S(2)}) collective-permute-start(bf16[3,144,256]{2,1,0:T(8,128)(2,1)S(1)} %slice.18), channel_id=1, source_target_pairs={{0,1},{1,2},{2,3},{3,0},{4,5},{5,6},{6,7},{7,4},{8,9},{9,10},{10,1... | collective-permute-start | bytes 663560 | tf_op jit(solution)/shard_map/ppermute | solution.py:86
  160.4 9.1 %collective-permute-start.18 = (bf16[3,144,256]{2,1,0:T(8,128)(2,1)S(1)}, bf16[3,144,256]{2,1,0:T(8,128)(2,1)S(1)}, u32[]{:S(2)}, u32[]{:S(2)}) collective-permute-start(bf16[3,144,256]{2,1,0:T(8,128)(2,1)S(1)} %slice.19), channel_id=1, source_target_pairs={{0,3},{1,0},{2,1},{3,2},{4,7},{5,4},{6,5},{7,6},{8,11},{9,8},{10,9... | collective-permute-start | bytes 663560 | tf_op jit(solution)/shard_map/ppermute | solution.py:86
  (20 other events, 49.0 us)

commit v3 on v2

v3 whole, which is shorter than its diff:
```python
import functools
import math

import jax
import jax.numpy as jnp
import numpy as np
from jax import lax
from jax.experimental import pallas as pl
from jax.experimental.pallas import tpu as pltpu
from jax.sharding import PartitionSpec as P

D = 3072
HEAD = 128
HEADS_DEV = 3
GROUP = HEADS_DEV * HEAD
N_TENSOR = 8
VID = 1536
AUD = 32
REACH = 8
SPAN = AUD + 2 * REACH
KEYS = HEADS_DEV * SPAN
PACKED = AUD + 2 * REACH
SHARDS = 16
TILE = 256
TILES = VID // TILE
THIRD = VID // 3
AT_DEST = 8
AT_SHARD = 16
AT_VIDEO = 17
AT_AUDIO = 33
AT_VWIN = 49
AT_AWIN = 81
EPS = 1e-6
SCALE = math.log2(math.e) / math.sqrt(HEAD)
F32 = jnp.float32
BF16 = jnp.bfloat16


def cost(microseconds):
    return pl.CostEstimate(
        flops=int(microseconds * 1e9), bytes_accessed=0, transcendentals=0
    )


def dot(a, b):
    return jnp.dot(a, b, preferred_element_type=F32)


def dot_nt(a, b):
    return lax.dot_general(a, b, (((1,), (1,)), ((), ())), preferred_element_type=F32)


def dot_tn(a, b):
    return lax.dot_general(a, b, (((0,), (0,)), ((), ())), preferred_element_type=F32)


ANY = pl.BlockSpec(memory_space=pl.ANY)
VMEM = pl.BlockSpec(memory_space=pltpu.VMEM)
SMEM = pl.BlockSpec(memory_space=pltpu.SMEM)
HBM = pl.BlockSpec(memory_space=pltpu.HBM)


def sds(shape, dtype):
    return jax.ShapeDtypeStruct(shape, dtype)


def call(kernel, name, micros, inputs, extra, outputs, scratch=(), aliases=None, mib=16, out_spec=VMEM):
    count = len(inputs)

    def run(*refs):
        kernel(*refs[:count], *refs[count + len(extra) :])

    arrays = [
        pltpu.with_memory_space_constraint(array, spec.memory_space)
        if spec is VMEM or spec is HBM
        else array
        for spec, array in inputs
    ]
    return pl.pallas_call(
        run,
        in_specs=[spec for spec, _ in inputs] + [ANY] * len(extra),
        out_specs=[out_spec] * len(outputs),
        out_shape=list(outputs),
        scratch_shapes=list(scratch),
        input_output_aliases=aliases or {},
        compiler_params=pltpu.CompilerParams(vmem_limit_bytes=mib * 2**20),
        cost_estimate=cost(micros),
        name=name,
    )(*arrays, *extra)


def gate(arrays, *extra, spec=ANY):
    shape = sds if spec is ANY else pltpu.VMEM
    return call(
        lambda *refs: None,
        "gate",
        0,
        [(spec, a) for a in arrays],
        extra,
        [shape(a.shape, a.dtype) for a in arrays],
        aliases={i: i for i in range(len(arrays))},
        mib=4,
        out_spec=spec,
    )


def parts(pieces, *extra):
    def kernel(*refs):
        for (_, first, count), ref, out in zip(pieces, refs, refs[len(pieces) :]):
            out[...] = ref[first : first + count]

    return call(
        kernel,
        "parts",
        0,
        [(VMEM, a) for a, _, _ in pieces],
        extra,
        [pltpu.VMEM((count,) + a.shape[1:], a.dtype) for a, _, count in pieces],
    )


def moved(index, dy, dx):
    return (index // 4 + dy) % 2 * 4 + (index % 4 + dx) % 4


OFFSETS = ((0, 0), (0, 3), (0, 1), (1, 0), (1, 3), (0, 2), (1, 1), (1, 2))


def send(array, dy, dx):
    pairs = [(i, moved(i, dy, dx)) for i in range(N_TENSOR)]
    return lax.ppermute(array, "tensor", pairs)


def right(array):
    return send(array, 0, 1)


def left(array):
    return send(array, 0, 3)


def across(array):
    return send(array, 1, 0)


def cat(*arrays):
    return jnp.concatenate(arrays, axis=0)


def rows_of(t):
    return pl.ds(pl.multiple_of(t * TILE, TILE), TILE)


def prefetch_kernel(
    meta_ref, audio_ref, wq, wk, wv, wo, copies_ref, w_ref, out_w_ref, sums_ref, sems
):
    copies = []
    for part, (ref, tower) in enumerate(((wq, 0), (wk, 1), (wv, 1))):
        for j in range(N_TENSOR):
            row = pl.multiple_of(meta_ref[j] * GROUP, GROUP)
            copies.append(
                pltpu.make_async_copy(
                    ref.at[tower, pl.ds(row, GROUP), :],
                    w_ref.at[pl.ds(j * GROUP, GROUP), pl.ds(part * GROUP, GROUP)],
                    sems.at[part * N_TENSOR + j],
                )
            )
    for tower in range(2):
        copies.append(
            pltpu.make_async_copy(
                wo.at[tower], out_w_ref.at[tower], sems.at[3 * N_TENSOR + tower]
            )
        )
    for copy in copies:
        copy.start()
    copies_ref[...] = jnp.broadcast_to(audio_ref[...][None], (N_TENSOR, AUD, GROUP))
    for copy in copies:
        copy.wait()
    sums_ref[...] = dot(jnp.ones((8, D), BF16), w_ref[...])


def prefetch(meta, audio_tokens, w_query, w_key, w_value, w_out):
    return call(
        prefetch_kernel,
        "prefetch",
        0,
        [(SMEM, meta), (VMEM, audio_tokens)]
        + [(HBM, w) for w in (w_query, w_key, w_value, w_out)],
        (),
        [
            pltpu.VMEM((N_TENSOR, AUD, GROUP), BF16),
            pltpu.VMEM((D, 3 * GROUP), BF16),
            pltpu.VMEM((2, GROUP, D), BF16),
            pltpu.VMEM((8, 3 * GROUP), F32),
        ],
        [pltpu.SemaphoreType.DMA((3 * N_TENSOR + 2,))],
    )


def audio_in_kernel(a_ref, wq, wk, wv, qkv_ref, prev_ref, next_ref, wcat, normed, sems):
    def weight(part, j):
        ref, tower = ((wq, 1), (wk, 0), (wv, 0))[part]
        rows = pl.ds(j * GROUP, GROUP)
        cols = pl.ds(part * GROUP, GROUP)
        return pltpu.make_async_copy(
            ref.at[tower, rows, :], wcat.at[rows, cols], sems.at[3 * j + part]
        )

    for j in range(N_TENSOR):
        for part in range(3):
            weight(part, j).start()

    values = a_ref[...].astype(F32)
    mean = jnp.sum(jnp.sum(values, axis=0), axis=-1, keepdims=True) / D
    centred = values - mean[None]
    var = jnp.sum(jnp.sum(centred * centred, axis=0), axis=-1, keepdims=True) / D
    normed[...] = (centred * lax.rsqrt(var + EPS)[None]).astype(BF16)

    total = jnp.zeros((AUD, 3 * GROUP), F32)
    for j in range(N_TENSOR):
        for part in range(3):
            weight(part, j).wait()
        total = total + dot(normed[j], wcat[j * GROUP : (j + 1) * GROUP, :])

    heads = []
    for h in range(2 * HEADS_DEV):
        part = total[:, h * HEAD : (h + 1) * HEAD]
        mean_square = jnp.mean(part * part, axis=-1, keepdims=True)
        heads.append(part * lax.rsqrt(mean_square + EPS))
    q = jnp.concatenate(heads[:HEADS_DEV], axis=1)
    k = jnp.concatenate(heads[HEADS_DEV:], axis=1)
    v = total[:, 2 * GROUP :]
    qkv_ref[...] = cat(q, k, v).astype(BF16)
    prev_ref[...] = cat(q, k[:REACH], v[:REACH]).astype(BF16)
    next_ref[...] = cat(q, k[AUD - REACH :], v[AUD - REACH :]).astype(BF16)


def audio_in(gathered, w_query, w_key, w_value, *extra):
    return call(
        audio_in_kernel,
        "audio_in",
        2,
        [(VMEM, gathered), (HBM, w_query), (HBM, w_key), (HBM, w_value)],
        extra,
        [
            pltpu.VMEM((3 * AUD, GROUP), BF16),
            pltpu.VMEM((PACKED, GROUP), BF16),
            pltpu.VMEM((PACKED, GROUP), BF16),
        ],
        [
            pltpu.VMEM((D, 3 * GROUP), BF16),
            pltpu.VMEM((N_TENSOR, AUD, GROUP), BF16),
            pltpu.SemaphoreType.DMA((3 * N_TENSOR,)),
        ],
    )


def dest_cols(meta_ref, j):
    return pl.ds(pl.multiple_of(meta_ref[AT_DEST + j] * GROUP, GROUP), GROUP)


def dest_cols(meta_ref, j):
    return pl.ds(pl.multiple_of(meta_ref[AT_DEST + j] * GROUP, GROUP), GROUP)


def value_out_kernel(meta_ref, qkv_ref, prev_ref, next_ref, w_ref, keep_ref, give_ref):
    before = prev_ref[...].astype(F32)[AUD + REACH :]
    own = qkv_ref[...].astype(F32)[2 * AUD :]
    behind = next_ref[...].astype(F32)[AUD + REACH :]
    values = cat(before, own, behind).astype(BF16)
    for h in range(HEADS_DEV):
        cols = slice(h * HEAD, (h + 1) * HEAD)
        for j, (dy, dx) in enumerate(OFFSETS):
            product = dot(values[:, cols], w_ref[0, cols, dest_cols(meta_ref, j)])
            out_ref = give_ref if dy else keep_ref
            out_ref[dx, h * SPAN : (h + 1) * SPAN, :] = product.astype(BF16)


def value_out(meta, qkv, from_prev, from_next, w_out, *extra):
    return call(
        value_out_kernel,
        "value_out",
        0,
        [(SMEM, meta), (VMEM, qkv), (VMEM, from_prev), (VMEM, from_next), (VMEM, w_out)],
        extra,
        [pltpu.VMEM((4, KEYS, GROUP), BF16)] * 2,
    )


def value_pairs_kernel(keep_ref, got_ref, *out_refs):
    for dx in range(1, 4):
        out_refs[dx - 1][0] = keep_ref[dx]
        out_refs[dx - 1][1] = got_ref[dx]


def value_pairs(keep, got, *extra):
    return call(
        value_pairs_kernel,
        "value_pairs",
        0,
        [(VMEM, keep), (VMEM, got)],
        extra,
        [pltpu.VMEM((2, KEYS, GROUP), BF16)] * 3,
    )


def row_stats(block):
    values = block.astype(F32)
    mean = jnp.mean(values, axis=-1, keepdims=True)
    centred = values - mean
    return mean, jnp.sum(centred * centred, axis=-1, keepdims=True)


def merged_stats(stat, count1, block):
    count2 = block.shape[1]
    mean1, square1 = stat[:, :1], stat[:, 1:2]
    mean2, square2 = row_stats(block)
    gap = mean2 - mean1
    total = count1 + count2
    mean = mean1 + gap * (count2 / total)
    return mean, square1 + square2 + gap * gap * (count1 * count2 / total)


def packed_stats(mean, square):
    lane = lax.broadcasted_iota(jnp.int32, (TILE, HEAD), 1)
    return jnp.where(lane == 0, mean, square)


def stage_kernel(first, count, start, *refs):
    x_refs, w_ref, refs = refs[:count], refs[count], refs[count + 1 :]
    acc_in, stat_in = (None, None) if start else refs[:2]
    acc, stat = refs[-2:]
    weights = pl.ds(first * GROUP, count * GROUP)

    @pl.loop(0, TILES)
    def _(t):
        rows = rows_of(t)
        block = jnp.concatenate([ref[rows, :] for ref in x_refs], axis=1)
        total = dot(block, w_ref[weights, :])
        if start:
            acc[rows, :] = total
            stat[rows, :] = packed_stats(*row_stats(block))
        else:
            acc[rows, :] = acc_in[rows, :] + total
            stat[rows, :] = packed_stats(*merged_stats(stat_in[rows, :], first * GROUP, block))


def stage(blocks, weights, first, before=(), extra=()):
    count, start = len(blocks), not before
    inputs = [(VMEM, a) for a in (*blocks, weights, *before)]
    return call(
        functools.partial(stage_kernel, first, count, start),
        f"stage_{first}",
        4,
        inputs,
        extra,
        [pltpu.VMEM((VID, 3 * GROUP), F32), pltpu.VMEM((VID, HEAD), F32)],
        aliases={} if start else {count + 1: 0, count + 2: 1},
    )


def head_norm(part, floor):
    mean_square = jnp.mean(part * part, axis=-1, keepdims=True)
    return (part * lax.rsqrt(mean_square + floor)).astype(BF16)


def by_thirds(body, pieces):
    for k, piece in enumerate(pieces):

        @pl.loop(0, TILES // 3)
        def _(u, k=k, piece=piece):
            body(k * (TILES // 3) + u, piece[rows_of(u), :])


LAST = pl.ds(7 * GROUP, GROUP)


def query_kernel(
    meta_ref, xa, xb, xc, w_ref, acc, stat_in, sums_ref, qkv_ref, prev_ref, next_ref,
    pt_ref, stat,
):
    shard = meta_ref[AT_SHARD]
    before = prev_ref[...].astype(F32)
    own = qkv_ref[...].astype(F32)
    behind = next_ref[...].astype(F32)
    keys = cat(
        before[AUD : AUD + REACH], own[AUD : 2 * AUD], behind[AUD : AUD + REACH]
    ).astype(BF16)

    prev_at, next_at = jnp.maximum(shard - 1, 0), jnp.minimum(shard + 1, SHARDS - 1)
    slot = lax.broadcasted_iota(jnp.int32, (SPAN, 1), 0)
    end_prev = jnp.where(shard > 0, meta_ref[AT_AUDIO + prev_at] - (AUD - REACH), 0)
    reach = jnp.minimum(meta_ref[AT_AUDIO + next_at], meta_ref[AT_VWIN + SHARDS + shard])
    end_next = jnp.where(shard < SHARDS - 1, REACH + AUD + reach, 0)
    used = (slot >= REACH - meta_ref[AT_VWIN + shard]) & (slot < jnp.minimum(end_prev, REACH))
    used |= (slot >= REACH) & (slot < REACH + meta_ref[AT_AUDIO + shard])
    used |= (slot >= REACH + AUD) & (slot < end_next)
    sums = sums_ref[:1, :GROUP]

    def body(t, block):
        rows = rows_of(t)
        mean, square = merged_stats(stat_in[rows, :], 7 * GROUP, block)
        var = square / D
        stat[rows, :] = packed_stats(mean, var)
        total = acc[rows, :GROUP] + dot(block, w_ref[LAST, :GROUP]) - mean * sums
        floor = EPS * (var + EPS)
        for h in range(HEADS_DEV):
            cols = slice(h * HEAD, (h + 1) * HEAD)
            scores = dot_nt(keys[:, cols], head_norm(total[:, cols], floor))
            weights = jnp.where(used, jnp.exp2(scores * SCALE), 0.0)
            below = jnp.sum(weights, axis=0, keepdims=True)
            pt_ref[t, h * SPAN : (h + 1) * SPAN, :] = (weights * (1.0 / below)).astype(BF16)

    by_thirds(body, (xa, xb, xc))


def queries_out(meta, pieces, weights, acc, stat, sums, qkv, from_prev, from_next, *extra):
    return call(
        query_kernel,
        "queries_out",
        2,
        [(SMEM, meta)]
        + [(VMEM, a) for a in (*pieces, weights, acc, stat, sums, qkv, from_prev, from_next)],
        extra,
        [pltpu.VMEM((TILES, KEYS, TILE), BF16), pltpu.VMEM((VID, HEAD), F32)],
        aliases={6: 1},
    )


def audio_part_kernel(
    meta_ref, xa, xb, xc, w_ref, acc, stat, sums_ref, qkv_ref, prev_ref, next_ref,
    part_p, part_o, part_n,
):
    shard = meta_ref[AT_SHARD]
    queries = cat(prev_ref[:AUD], qkv_ref[:AUD], next_ref[:AUD])
    for ref in (part_p, part_o, part_n):
        ref[...] = jnp.zeros_like(ref)

    prev_at, next_at = jnp.maximum(shard - 1, 0), jnp.minimum(shard + 1, SHARDS - 1)
    count = meta_ref[AT_VIDEO + shard]
    row = lax.broadcasted_iota(jnp.int32, (3 * AUD, 1), 0)
    high_prev = jnp.where(shard > 0, jnp.minimum(count, meta_ref[AT_AWIN + SHARDS + prev_at]), 0)
    high_next = jnp.where(shard < SHARDS - 1, count, 0)
    low = jnp.where(row < 2 * AUD, 0, VID - meta_ref[AT_AWIN + next_at])
    high = jnp.where(row < AUD, high_prev, jnp.where(row < 2 * AUD, count, high_next))
    sums = sums_ref[:1, GROUP:]

    def body(t, block):
        rows = rows_of(t)
        mean, var = stat[rows, :1], stat[rows, 1:2]
        total = acc[rows, GROUP:] + dot(block, w_ref[LAST, GROUP:]) - mean * sums
        floor = EPS * (var + EPS)
        spread = lax.rsqrt(var + EPS)
        place = t * TILE + lax.broadcasted_iota(jnp.int32, (3 * AUD, TILE), 1)
        seen = (place >= low) & (place < high)
        for h in range(HEADS_DEV):
            cols = slice(h * HEAD, (h + 1) * HEAD)
            value = (total[:, GROUP + h * HEAD : GROUP + (h + 1) * HEAD] * spread).astype(BF16)
            scores = dot_nt(queries[:, cols], head_norm(total[:, cols], floor))
            weights = jnp.where(seen, jnp.exp2(scores * SCALE), 0.0)
            bottom = jnp.broadcast_to(jnp.sum(weights, axis=1, keepdims=True), (3 * AUD, HEAD))
            top = dot(weights.astype(BF16), value)
            for g, ref in enumerate((part_p, part_o, part_n)):
                ref[0, :, cols] += top[g * AUD : (g + 1) * AUD]
                ref[1, :, cols] += bottom[g * AUD : (g + 1) * AUD]

    by_thirds(body, (xa, xb, xc))


def audio_part(meta, pieces, weights, acc, stat, sums, qkv, from_prev, from_next, *extra):
    return call(
        audio_part_kernel,
        "audio_part",
        0,
        [(SMEM, meta)]
        + [(VMEM, a) for a in (*pieces, weights, acc, stat, sums, qkv, from_prev, from_next)],
        extra,
        [pltpu.VMEM((2, AUD, GROUP), F32)] * 3,
    )


def audio_out_kernel(meta_ref, own_ref, prev_ref, next_ref, w_ref, keep_ref, give_ref):
    total = own_ref[...] + prev_ref[...] + next_ref[...]
    attended = (total[0] / total[1]).astype(BF16)
    for j, (dy, dx) in enumerate(OFFSETS):
        product = dot(attended, w_ref[1, :, dest_cols(meta_ref, j)]).astype(BF16)
        (give_ref if dy else keep_ref)[dx] = product


def audio_out(meta, own, from_prev, from_next, w_out, *extra):
    return call(
        audio_out_kernel,
        "audio_out",
        0,
        [(SMEM, meta), (VMEM, own), (VMEM, from_prev), (VMEM, from_next), (VMEM, w_out)],
        extra,
        [pltpu.VMEM((4, AUD, GROUP), BF16)] * 2,
    )


def audio_pair_kernel(keep_ref, got_ref, *out_refs):
    for dx in range(4):
        total = keep_ref[dx].astype(F32) + got_ref[dx].astype(F32)
        out_refs[dx][...] = total.astype(BF16)


def audio_pair(keep, got):
    return call(
        audio_pair_kernel,
        "audio_pair",
        0,
        [(VMEM, keep), (VMEM, got)],
        (),
        [pltpu.VMEM((AUD, GROUP), BF16)] * 4,
    )


def audio_sum_kernel(meta_ref, *refs):
    total = sum(ref[...].astype(F32) for ref in refs[:4])
    row = lax.broadcasted_iota(jnp.int32, (AUD, 1), 0)
    valid = row < meta_ref[AT_AUDIO + meta_ref[AT_SHARD]]
    refs[4][...] = jnp.where(valid, total, 0.0).astype(BF16)


def audio_sum(meta, received):
    (out,) = call(
        audio_sum_kernel,
        "audio_sum",
        0,
        [(SMEM, meta)] + [(VMEM, a) for a in received],
        (),
        [sds((AUD, GROUP), BF16)],
    )
    return out


def output_first_kernel(*refs):
    p_refs, (keep, got, v1, v2, v3), (out_ref, projected) = refs[:7], refs[7:12], refs[12:]
    blocks = (keep[0], v3[0], v1[0], got[0], v3[1], v2[0], v1[1])
    for j, block in enumerate(blocks):
        projected[j * KEYS : (j + 1) * KEYS, :] = block

    @pl.loop(0, TILES)
    def _(t):
        probs = jnp.concatenate([ref[t] for ref in p_refs], axis=0)
        out_ref[rows_of(t), :] = dot_tn(probs, projected[...])


def output_first(probs, values, *extra):
    (out,) = call(
        output_first_kernel,
        "output_first",
        0,
        [(VMEM, a) for a in (*probs, *values)],
        extra,
        [pltpu.VMEM((VID, GROUP), F32)],
        [pltpu.VMEM((7 * KEYS, GROUP), BF16)],
    )
    return out


def output_last_kernel(meta_ref, low_ref, high_ref, v_ref, sum_ref, out_ref, out, sems):
    limit = meta_ref[AT_VIDEO + meta_ref[AT_SHARD]]
    value = v_ref[1]

    def copy(t):
        return pltpu.make_async_copy(out.at[rows_of(t), :], out_ref.at[rows_of(t), :], sems.at[t])

    for k, ref in enumerate((low_ref, high_ref)):

        @pl.loop(0, TILES // 2)
        def _(u, k=k, ref=ref):
            t = k * (TILES // 2) + u
            result = sum_ref[rows_of(t), :] + dot_tn(ref[u], value)
            row = t * TILE + lax.broadcasted_iota(jnp.int32, (TILE, 1), 0)
            out[rows_of(t), :] = jnp.where(row < limit, result, 0.0).astype(BF16)
            copy(t).start()

    for t in range(TILES):
        copy(t).wait()


def output_last(meta, low, high, values, sums):
    (out,) = call(
        output_last_kernel,
        "output_last",
        1,
        [(SMEM, meta), (VMEM, low), (VMEM, high), (VMEM, values), (VMEM, sums)],
        (),
        [sds((VID, GROUP), BF16)],
        [pltpu.VMEM((VID, GROUP), BF16), pltpu.SemaphoreType.DMA((TILES,))],
        out_spec=ANY,
    )
    return out


def shards(
    video_tokens,
    audio_tokens,
    w_query,
    w_key,
    w_value,
    w_out,
    video_counts,
    audio_counts,
    video_windows,
    audio_windows,
):
    me = lax.axis_index("tensor")
    shard = lax.axis_index(("tower", "tm"))
    up = [(i, i + 1) for i in range(SHARDS - 1)]
    down = [(i + 1, i) for i in range(SHARDS - 1)]

    def to_next(array):
        return lax.ppermute(array, ("tower", "tm"), up)

    def to_prev(array):
        return lax.ppermute(array, ("tower", "tm"), down)

    places = np.array(
        [
            [moved(i, dy, dx) for dy, dx in OFFSETS] + [moved(i, dy, -dx) for dy, dx in OFFSETS]
            for i in range(N_TENSOR)
        ]
    )
    order = lax.dynamic_index_in_dim(jnp.asarray(places, jnp.int32), me, 0, keepdims=False)
    meta = jnp.concatenate(
        [
            order,
            shard.reshape(1).astype(jnp.int32),
            video_counts,
            audio_counts,
            video_windows.T.reshape(-1),
            audio_windows.T.reshape(-1),
        ]
    )

    xl, xr, xy = right(video_tokens), left(video_tokens), across(video_tokens)
    audio_copies, weights, w_back, sums = prefetch(
        meta, audio_tokens, w_query, w_key, w_value, w_out
    )
    audio_blocks = lax.all_to_all(audio_copies, "tensor", 0, 0)

    xl, xr, xy = gate((xl, xr, xy), audio_blocks)
    yl, xq, yr = right(xy), left(xr), across(xr)
    qkv, for_prev, for_next = audio_in(audio_blocks, w_query, w_key, w_value, xl)
    from_next, from_prev = to_prev(for_prev), to_next(for_next)
    acc, stat = stage((video_tokens, xl, xr, xy), weights, 0, (), (for_prev, for_next))

    thirds = parts(((yl, 0, THIRD), (xq, THIRD, THIRD), (yr, 2 * THIRD, THIRD)), stat)
    pieces = right(thirds[0]), across(thirds[1]), left(thirds[2])
    keep_v, give_v = value_out(meta, qkv, from_prev, from_next, w_back, thirds[0])
    got_v = across(give_v)
    acc, stat = stage((yl, xq, yr), weights, 4, (acc, stat), (keep_v,))

    heard = (qkv, from_prev, from_next)
    probs, stat = queries_out(meta, pieces, weights, acc, stat, sums, *heard)
    pl_, pr_, py_ = right(probs), left(probs), across(probs)
    to_send = value_pairs(keep_v, got_v, probs)
    v1, v2, v3 = [send(pair, 0, -dx) for dx, pair in enumerate(to_send, 1)]
    part_prev, part_own, part_next = audio_part(
        meta, pieces, weights, acc, stat, sums, *heard, to_send[0]
    )
    pl_, pr_, py_ = gate((pl_, pr_, py_), part_prev)
    pyl, pq, pyr = right(py_), left(pr_), across(pr_)
    audio_from_next, audio_from_prev = to_prev(part_prev), to_next(part_next)
    half = TILES // 2
    low, high = parts(((pyl, 0, half), (pyr, half, half)), pq)
    far_low, far_high = right(low), left(high)
    keep, give = audio_out(meta, part_own, audio_from_prev, audio_from_next, w_back, low)
    pairs = audio_pair(keep, across(give))
    received = [pairs[0]] + [send(pairs[dx], 0, -dx) for dx in range(1, 4)]
    video_sums = output_first(
        (probs, pl_, pr_, py_, pyl, pq, pyr), (keep_v, got_v, v1, v2, v3), give
    )
    audio_update = audio_sum(meta, received)
    video_update = output_last(meta, far_low, far_high, v2, video_sums)
    return (video_update, audio_update)


def solution(mesh):
    in_specs = (
        P(("tower", "tm"), "tensor"),
        P(("tower", "tm"), "tensor"),
        P(None, None, "tensor"),
        P(None, None, "tensor"),
        P(None, None, "tensor"),
        P(None, "tensor", None),
        P(),
        P(),
        P(),
        P(),
    )
    out_specs = (P(("tower", "tm"), "tensor"), P(("tower", "tm"), "tensor"))
    return jax.shard_map(shards, mesh=mesh, in_specs=in_specs, out_specs=out_specs, check_vma=False)
```

time: 177 us -> 142 us (0.80)
  Pallas kernels: 70.4 us -> 46.9 us
  local copies, waits for them, and re-layouts: 17.6 us -> 3.7 us
  blocking collectives: 12.1 us -> 20.4 us
  starting transfers between devices: 46.2 us -> 42.4 us
    pallas_call x14 -> x17, Pallas kernels: 70.4 us -> 46.9 us  [call(): pl.pallas_call(run, in_specs=[spec for spec, _ in inputs] + [ANY] * len(e...]
    ppermute x17 -> x25, waiting for transfers between devices: 5.57 us -> 24.6 us  [send(): return lax.ppermute(array, 'tensor', pairs)]
    ppermute x2, waiting for transfers between devices: 12 us -> 0.01 us  [to_next(): return lax.ppermute(array, ('tower', 'tm'), up)]
    unnamed x61 -> x4, local copies, waits for them, and re-layouts: 11.4 us -> 0.75 us
    all_to_all x1, blocking collectives: 12.1 us -> 20.4 us  [shards(): audio_blocks = lax.all_to_all(audio_copies, 'tensor', 0, 0)]
    all_to_all x2 -> x0, starting transfers between devices: 7.62 us -> none  [the longest x1 4.21 us: shards(): values = lax.all_to_all(projected, 'tensor', 0, 0)]
    ppermute x2, waiting for transfers between devices: 9.47 us -> 2.26 us  [to_prev(): return lax.ppermute(array, ('tower', 'tm'), down)]
    ppermute x17 -> x25, starting transfers between devices: 22.5 us -> 29 us  [send(): return lax.ppermute(array, 'tensor', pairs)]
  transfers between devices with their start and end apart: 23 -> 29, of which waited for: 6 -> 13; matrix products, arithmetic and copies ran while one was open for 4% -> 2% of each run, Pallas kernels for 30% -> 30%
where the time goes in v3:
time: 142 us; the launch traced here: 141 us
  Pallas kernels  46.9 us (33%)
  starting transfers between devices  42.4 us (30%)
  waiting for transfers between devices  26.9 us (19%)
  blocking collectives  20.4 us (14%)
  local copies, waits for them, and re-layouts  3.7 us (3%)
    pallas_call x17, Pallas kernels, call(): pl.pallas_call(run, in_specs=[spec for spec, _ in inputs] + [ANY] * len(e...  46.9 us
    ppermute x25, starting transfers between devices, send(): return lax.ppermute(array, 'tensor', pairs)  29 us
    ppermute x25, waiting for transfers between devices, send(): return lax.ppermute(array, 'tensor', pairs)  24.6 us
    all_to_all x1, blocking collectives, shards(): audio_blocks = lax.all_to_all(audio_copies, 'tensor', 0, 0)  20.4 us
    ppermute x2, starting transfers between devices, to_next(): return lax.ppermute(array, ('tower', 'tm'), up)  10.8 us
  transfers between devices with their start and end apart: 29, of which 13 were waited for; matrix products, arithmetic and copies ran while one was open for 2% of the time, Pallas kernels for 30%

profile of v3, /device:TPU:0, one launch (start us, length us, event | category | flops | bytes accessed | tf_op | source)
XLA Modules:
  0.0 141.3 jit_solution(2464179266332457254)
XLA Ops:
  0.6 2.9 %collective-permute-start.1 = (bf16[1536,384]{1,0:T(8,128)(2,1)}, bf16[1536,384]{1,0:T(8,128)(2,1)S(1)}, u32[]{:S(2)}, u32[]{:S(2)}) collective-permute-start(bf16[1536,384]{1,0:T(8,128)(2,1)} %refs_0_.1), channel_id=1, source_target_pairs={{0,3},{1,0},{2,1},{3,2},{4,7},{5,4},{6,5},{7,6},{8,11},{9,8},{10,9... | collective-permute-start | bytes 3538952 | tf_op jit(solution)/shard_map/ppermute | solution.py:131
  3.5 1.6 %collective-permute-start.2 = (bf16[1536,384]{1,0:T(8,128)(2,1)}, bf16[1536,384]{1,0:T(8,128)(2,1)S(1)}, u32[]{:S(2)}, u32[]{:S(2)}) collective-permute-start(bf16[1536,384]{1,0:T(8,128)(2,1)} %refs_0_.1), channel_id=1, source_target_pairs={{0,4},{1,5},{2,6},{3,7},{4,0},{5,1},{6,2},{7,3},{8,12},{9,13},{10,... | collective-permute-start | bytes 3538952 | tf_op jit(solution)/shard_map/ppermute | solution.py:131
  8.8 6.3 %prefetch.1 = (bf16[8,32,384]{2,1,0:T(8,128)(2,1)S(1)}, bf16[3072,1152]{1,0:T(8,128)(2,1)S(1)}, bf16[2,384,3072]{2,1,0:T(8,128)(2,1)S(1)}, f32[8,1152]{1,0:T(8,128)S(1)}) custom-call(s32[113]{0:T(128)S(1)} %concatenate.3.refs_0_, bf16[32,384]{1,0:T(8,128)(2,1)S(1)} %copy-done, bf16[2,3072,384]{2,1,0:T(8,128)(2,1)} %refs_1_.3, bf16[2,3072,384]{2,1,0:T(8,128)(2,1)} %refs_2_.3, ...), custom_call_target="tpu_custom_call" | custom-call | tf_op jit(solution)/shard_map/prefetch/pallas_call | solution.py:79
  15.1 20.4 %all_to_all.5.refs_3_.refs_0_ = bf16[8,32,384]{2,1,0:T(8,128)(2,1)S(1)} all-to-all(bf16[8,32,384]{2,1,0:T(8,128)(2,1)S(1)} %get-tuple-element.40), channel_id=1, replica_groups=mesh['tower'=2,'tm'=8,'tensor'=8] {'tensor'}, dimensions={0} | all-to-all | bytes 393216 | tf_op jit(solution)/shard_map/all_to_all | solution.py:642
  36.1 3.1 %collective-permute-start.4 = (bf16[1536,384]{1,0:T(8,128)(2,1)S(1)}, bf16[1536,384]{1,0:T(8,128)(2,1)S(1)}, u32[]{:S(2)}, u32[]{:S(2)}) collective-permute-start(bf16[1536,384]{1,0:T(8,128)(2,1)S(1)} %get-tuple-element.42.refs_2_), channel_id=1, source_target_pairs={{0,3},{1,0},{2,1},{3,2},{4,7},{5,4},{6,5},{7,6},{8,11},{9,8},{10,9... | collective-permute-start | bytes 3538952 | tf_op jit(solution)/shard_map/ppermute | solution.py:131
  39.3 3.7 %audio_in.1 = (bf16[96,384]{1,0:T(8,128)(2,1)S(1)}, bf16[48,384]{1,0:T(8,128)(2,1)S(1)}, bf16[48,384]{1,0:T(8,128)(2,1)S(1)}) custom-call(bf16[8,32,384]{2,1,0:T(8,128)(2,1)S(1)} %all_to_all.5.refs_3_.refs_0_, bf16[2,3072,384]{2,1,0:T(8,128)(2,1)} %refs_1_.3, bf16[2,3072,384]{2,1,0:T(8,128)(2,1)} %refs_2_.3, bf16[2,3072,384]{2,1,0:T(8,128)(2,1)} %refs_3_.3, ...), custom_call_target="tpu_custom_call" | custom-call | flops 2000000000 | tf_op jit(solution)/shard_map/audio_in/pallas_call | solution.py:79
  43.0 1.3 collective-permute-start.10
  44.3 6.1 %collective-permute-start.9 = (bf16[48,384]{1,0:T(8,128)(2,1)S(1)}, bf16[48,384]{1,0:T(8,128)(2,1)S(1)}, u32[]{:S(2)}, u32[]{:S(2)}) collective-permute-start(bf16[48,384]{1,0:T(8,128)(2,1)S(1)} %get-tuple-element.46.refs_6_), channel_id=1, source_target_pairs={{0,8},{8,16},{16,24},{24,32},{32,40},{40,48},{48,56},{56,64},{64,7... | collective-permute-start | bytes 110600 | tf_op jit(solution)/shard_map/ppermute | solution.py:615
  50.3 7.9 %stage_0.1 = (f32[1536,1152]{1,0:T(8,128)S(1)}, f32[1536,128]{1,0:T(8,128)S(1)}) custom-call(bf16[1536,384]{1,0:T(8,128)(2,1)S(1)} %copy-done.1, bf16[1536,384]{1,0:T(8,128)(2,1)S(1)} %get-tuple-element.43.refs_4_.refs_1_, bf16[1536,384]{1,0:T(8,128)(2,1)S(1)} %get-tuple-element.42.refs_2_, bf16[1536,384]{1,0:T(8,128)(2,1)S(1)} %get-tuple-element.41.refs_3_, ...), custom_call_target="tpu_custom_call" | custom-call | flops 4000000000 | tf_op jit(solution)/shard_map/stage_0/pallas_call | solution.py:79
  58.2 4.3 %collective-permute-done.3.refs_0_ = bf16[1536,384]{1,0:T(8,128)(2,1)S(1)} collective-permute-done((bf16[1536,384]{1,0:T(8,128)(2,1)S(1)}, bf16[1536,384]{1,0:T(8,128)(2,1)S(1)}, u32[]{:S(2)}, u32[]{:S(2)}) %collective-permute-start.3) | collective-permute-done | bytes 1179680 | tf_op jit(solution)/shard_map/ppermute | solution.py:131
  63.7 3.7 %collective-permute-start.8 = (bf16[512,384]{1,0:T(8,128)(2,1)S(1)}, bf16[512,384]{1,0:T(8,128)(2,1)S(1)}, u32[]{:S(2)}, u32[]{:S(2)}) collective-permute-start(bf16[512,384]{1,0:T(8,128)(2,1)S(1)} %get-tuple-element.50), channel_id=1, source_target_pairs={{0,3},{1,0},{2,1},{3,2},{4,7},{5,4},{6,5},{7,6},{8,11},{9,8},{10,9... | collective-permute-start | bytes 1179656 | tf_op jit(solution)/shard_map/ppermute | solution.py:131
  67.4 1.1 value_out.1
  69.1 6.8 %stage_4.1 = (f32[1536,1152]{1,0:T(8,128)S(1)}, f32[1536,128]{1,0:T(8,128)S(1)}) custom-call(bf16[1536,384]{1,0:T(8,128)(2,1)S(1)} %collective-permute-done.3.refs_0_, bf16[1536,384]{1,0:T(8,128)(2,1)S(1)} %collective-permute-done.4.refs_1_, bf16[1536,384]{1,0:T(8,128)(2,1)S(1)} %collective-permute-done.5.refs_2_, ...), custom_call_target="tpu_custom_call", output_to_operand_aliasing={{0}: (4, {}), {1}: (5, {})} | custom-call | flops 4000000000 | tf_op jit(solution)/shard_map/stage_4/pallas_call | solution.py:79
  76.4 5.5 %queries_out.1 = (bf16[6,144,256]{2,1,0:T(8,128)(2,1)S(1)}, f32[1536,128]{1,0:T(8,128)S(1)}) custom-call(s32[113]{0:T(128)S(1)} %concatenate.3.refs_0_, bf16[512,384]{1,0:T(8,128)(2,1)S(1)} %collective-permute-done.6.refs_1_, bf16[512,384]{1,0:T(8,128)(2,1)S(1)} %collective-permute-done.7.refs_2_, ...), custom_call_target="tpu_custom_call", output_to_operand_aliasing={{1}: (6, {})} | custom-call | flops 2000000000 | tf_op jit(solution)/shard_map/queries_out/pallas_call | solution.py:79
  81.9 1.2 collective-permute-start.13
  83.1 3.2 %collective-permute-start.12 = (bf16[6,144,256]{2,1,0:T(8,128)(2,1)S(1)}, bf16[6,144,256]{2,1,0:T(8,128)(2,1)S(1)}, u32[]{:S(2)}, u32[]{:S(2)}) collective-permute-start(bf16[6,144,256]{2,1,0:T(8,128)(2,1)S(1)} %get-tuple-element.58.refs_2_.refs_0_), channel_id=1, source_target_pairs={{0,3},{1,0},{2,1},{3,2},{4,7},{5,4},{6,5},{7,6},{8,11},{9,8},{10,9... | collective-permute-start | bytes 1327112 | tf_op jit(solution)/shard_map/ppermute | solution.py:131
  86.4 7.4 %audio_part.1 = (f32[2,32,384]{2,1,0:T(8,128)S(1)}, f32[2,32,384]{2,1,0:T(8,128)S(1)}, f32[2,32,384]{2,1,0:T(8,128)S(1)}) custom-call(s32[113]{0:T(128)S(1)} %concatenate.3.refs_0_, bf16[512,384]{1,0:T(8,128)(2,1)S(1)} %collective-permute-done.6.refs_1_, bf16[512,384]{1,0:T(8,128)(2,1)S(1)} %collective-permute-done.7.refs_2_, ...), custom_call_target="tpu_custom_call" | custom-call | tf_op jit(solution)/shard_map/audio_part/pallas_call | solution.py:79
  93.9 1.5 %collective-permute-done.12.refs_1_ = bf16[6,144,256]{2,1,0:T(8,128)(2,1)S(1)} collective-permute-done((bf16[6,144,256]{2,1,0:T(8,128)(2,1)S(1)}, bf16[6,144,256]{2,1,0:T(8,128)(2,1)S(1)}, u32[]{:S(2)}, u32[]{:S(2)}) %collective-permute-start.12) | collective-permute-done | bytes 442400 | tf_op jit(solution)/shard_map/ppermute | solution.py:131
  95.5 3.4 %collective-permute-done.11.refs_0_ = bf16[6,144,256]{2,1,0:T(8,128)(2,1)S(1)} collective-permute-done((bf16[6,144,256]{2,1,0:T(8,128)(2,1)S(1)}, bf16[6,144,256]{2,1,0:T(8,128)(2,1)S(1)}, u32[]{:S(2)}, u32[]{:S(2)}) %collective-permute-start.11) | collective-permute-done | bytes 442400 | tf_op jit(solution)/shard_map/ppermute | solution.py:131
  98.9 3.2 %collective-permute-start.17 = (bf16[6,144,256]{2,1,0:T(8,128)(2,1)S(1)}, bf16[6,144,256]{2,1,0:T(8,128)(2,1)S(1)}, u32[]{:S(2)}, u32[]{:S(2)}) collective-permute-start(bf16[6,144,256]{2,1,0:T(8,128)(2,1)S(1)} %get-tuple-element.64.refs_2_), channel_id=1, source_target_pairs={{0,3},{1,0},{2,1},{3,2},{4,7},{5,4},{6,5},{7,6},{8,11},{9,8},{10,9... | collective-permute-start | bytes 1327112 | tf_op jit(solution)/shard_map/ppermute | solution.py:131
  102.5 4.8 %collective-permute-start.23 = (f32[2,32,384]{2,1,0:T(8,128)S(1)}, f32[2,32,384]{2,1,0:T(8,128)S(1)}, u32[]{:S(2)}, u32[]{:S(2)}) collective-permute-start(f32[2,32,384]{2,1,0:T(8,128)S(1)} %get-tuple-element.71), channel_id=1, source_target_pairs={{0,8},{8,16},{16,24},{24,32},{32,40},{40,48},{48,56},{56,64},{64,7... | collective-permute-start | bytes 294920 | tf_op jit(solution)/shard_map/ppermute | solution.py:615
  107.3 1.3 collective-permute-start.24
  108.6 1.9 %collective-permute-done.15.refs_0_.refs_4_ = bf16[6,144,256]{2,1,0:T(8,128)(2,1)S(1)} collective-permute-done((bf16[6,144,256]{2,1,0:T(8,128)(2,1)S(1)}, bf16[6,144,256]{2,1,0:T(8,128)(2,1)S(1)}, u32[]{:S(2)}, u32[]{:S(2)}) %collective-permute-start.15) | collective-permute-done | bytes 442400 | tf_op jit(solution)/shard_map/ppermute | solution.py:131
  110.5 2.5 %collective-permute-done.16.refs_1_.refs_6_ = bf16[6,144,256]{2,1,0:T(8,128)(2,1)S(1)} collective-permute-done((bf16[6,144,256]{2,1,0:T(8,128)(2,1)S(1)}, bf16[6,144,256]{2,1,0:T(8,128)(2,1)S(1)}, u32[]{:S(2)}, u32[]{:S(2)}) %collective-permute-start.16) | collective-permute-done | bytes 442400 | tf_op jit(solution)/shard_map/ppermute | solution.py:131
  113.0 2.3 %collective-permute-done.24.refs_3_ = f32[2,32,384]{2,1,0:T(8,128)S(1)} collective-permute-done((f32[2,32,384]{2,1,0:T(8,128)S(1)}, f32[2,32,384]{2,1,0:T(8,128)S(1)}, u32[]{:S(2)}, u32[]{:S(2)}) %collective-permute-start.24) | collective-permute-done | bytes 98336 | tf_op jit(solution)/shard_map/ppermute | solution.py:618
  117.9 2.4 %collective-permute-start.21 = (bf16[2,144,384]{2,1,0:T(8,128)(2,1)S(1)}, bf16[2,144,384]{2,1,0:T(8,128)(2,1)S(1)}, u32[]{:S(2)}, u32[]{:S(2)}) collective-permute-start(bf16[2,144,384]{2,1,0:T(8,128)(2,1)S(1)} %get-tuple-element.61.refs_11_), channel_id=1, source_target_pairs={{0,3},{1,0},{2,1},{3,2},{4,7},{5,4},{6,5},{7,6},{8,11},{9,8},{10,9... | collective-permute-start | bytes 663560 | tf_op jit(solution)/shard_map/ppermute | solution.py:131
  122.4 4.3 %collective-permute-done.20.refs_10_.refs_3_ = bf16[2,144,384]{2,1,0:T(8,128)(2,1)S(1)} collective-permute-done((bf16[2,144,384]{2,1,0:T(8,128)(2,1)S(1)}, bf16[2,144,384]{2,1,0:T(8,128)(2,1)S(1)}, u32[]{:S(2)}, u32[]{:S(2)}) %collective-permute-start.20) | collective-permute-done | bytes 221216 | tf_op jit(solution)/shard_map/ppermute | solution.py:131
  126.6 4.4 %collective-permute-done.22.refs_11_ = bf16[2,144,384]{2,1,0:T(8,128)(2,1)S(1)} collective-permute-done((bf16[2,144,384]{2,1,0:T(8,128)(2,1)S(1)}, bf16[2,144,384]{2,1,0:T(8,128)(2,1)S(1)}, u32[]{:S(2)}, u32[]{:S(2)}) %collective-permute-start.22) | collective-permute-done | bytes 221216 | tf_op jit(solution)/shard_map/ppermute | solution.py:131
  131.6 1.1 collective-permute-start.28
  132.7 2.9 %output_first.1.refs_4_ = f32[1536,384]{1,0:T(8,128)S(1)} custom-call(bf16[6,144,256]{2,1,0:T(8,128)(2,1)S(1)} %get-tuple-element.58.refs_2_.refs_0_, bf16[6,144,256]{2,1,0:T(8,128)(2,1)S(1)} %get-tuple-element.68.refs_1_, bf16[6,144,256]{2,1,0:T(8,128)(2,1)S(1)} %get-tuple-element.64.refs_2_, bf16[6,144,256]{2,1,0:T(8,128)(2,1)S(1)} %get-tuple-element.63.refs_3_, ...), custom_call_target="tpu_custom_call" | custom-call | tf_op jit(solution)/shard_map/output_first/pallas_call | solution.py:79
  137.1 1.2 audio_sum.1
  138.2 2.9 %output_last.1 = bf16[1536,384]{1,0:T(8,128)(2,1)} custom-call(s32[113]{0:T(128)S(1)} %concatenate.3.refs_0_, bf16[3,144,256]{2,1,0:T(8,128)(2,1)S(1)} %collective-permute-done.18.refs_1_, bf16[3,144,256]{2,1,0:T(8,128)(2,1)S(1)} %collective-permute-done.19.refs_2_, bf16[2,144,384]{2,1,0:T(8,128)(2,1)S(1)} %collective-permute-done.20.refs_10_.refs_3_, ...), custom_call_target="tpu_custom_call" | custom-call | flops 1000000000 | tf_op jit(solution)/shard_map/output_last/pallas_call | solution.py:79
  (52 shorter events, 13.8 us)
Async XLA Ops:
  0.6 34.9 %collective-permute-start.1 = (bf16[1536,384]{1,0:T(8,128)(2,1)}, bf16[1536,384]{1,0:T(8,128)(2,1)S(1)}, u32[]{:S(2)}, u32[]{:S(2)}) collective-permute-start(bf16[1536,384]{1,0:T(8,128)(2,1)} %refs_0_.1), channel_id=1, source_target_pairs={{0,3},{1,0},{2,1},{3,2},{4,7},{5,4},{6,5},{7,6},{8,11},{9,8},{10,9... | collective-permute-start | bytes 3538952 | tf_op jit(solution)/shard_map/ppermute | solution.py:131
  3.5 32.0 %collective-permute-start = (bf16[1536,384]{1,0:T(8,128)(2,1)}, bf16[1536,384]{1,0:T(8,128)(2,1)S(1)}, u32[]{:S(2)}, u32[]{:S(2)}) collective-permute-start(bf16[1536,384]{1,0:T(8,128)(2,1)} %refs_0_.1), channel_id=1, source_target_pairs={{0,1},{1,2},{2,3},{3,0},{4,5},{5,6},{6,7},{7,4},{8,9},{9,10},{10,1... | collective-permute-start | bytes 3538952 | tf_op jit(solution)/shard_map/ppermute | solution.py:131
  3.5 32.0 %collective-permute-start.2 = (bf16[1536,384]{1,0:T(8,128)(2,1)}, bf16[1536,384]{1,0:T(8,128)(2,1)S(1)}, u32[]{:S(2)}, u32[]{:S(2)}) collective-permute-start(bf16[1536,384]{1,0:T(8,128)(2,1)} %refs_0_.1), channel_id=1, source_target_pairs={{0,4},{1,5},{2,6},{3,7},{4,0},{5,1},{6,2},{7,3},{8,12},{9,13},{10,... | collective-permute-start | bytes 3538952 | tf_op jit(solution)/shard_map/ppermute | solution.py:131
  8.1 0.7 copy-start
  35.5 27.0 %collective-permute-start.3 = (bf16[1536,384]{1,0:T(8,128)(2,1)S(1)}, bf16[1536,384]{1,0:T(8,128)(2,1)S(1)}, u32[]{:S(2)}, u32[]{:S(2)}) collective-permute-start(bf16[1536,384]{1,0:T(8,128)(2,1)S(1)} %get-tuple-element.41.refs_3_), channel_id=1, source_target_pairs={{0,1},{1,2},{2,3},{3,0},{4,5},{5,6},{6,7},{7,4},{8,9},{9,10},{10,1... | collective-permute-start | bytes 3538952 | tf_op jit(solution)/shard_map/ppermute | solution.py:131
  35.6 26.9 %collective-permute-start.5 = (bf16[1536,384]{1,0:T(8,128)(2,1)S(1)}, bf16[1536,384]{1,0:T(8,128)(2,1)S(1)}, u32[]{:S(2)}, u32[]{:S(2)}) collective-permute-start(bf16[1536,384]{1,0:T(8,128)(2,1)S(1)} %get-tuple-element.42.refs_2_), channel_id=1, source_target_pairs={{0,4},{1,5},{2,6},{3,7},{4,0},{5,1},{6,2},{7,3},{8,12},{9,13},{10,... | collective-permute-start | bytes 3538952 | tf_op jit(solution)/shard_map/ppermute | solution.py:131
  36.1 26.4 %collective-permute-start.4 = (bf16[1536,384]{1,0:T(8,128)(2,1)S(1)}, bf16[1536,384]{1,0:T(8,128)(2,1)S(1)}, u32[]{:S(2)}, u32[]{:S(2)}) collective-permute-start(bf16[1536,384]{1,0:T(8,128)(2,1)S(1)} %get-tuple-element.42.refs_2_), channel_id=1, source_target_pairs={{0,3},{1,0},{2,1},{3,2},{4,7},{5,4},{6,5},{7,6},{8,11},{9,8},{10,9... | collective-permute-start | bytes 3538952 | tf_op jit(solution)/shard_map/ppermute | solution.py:131
  39.3 11.0 %copy-start.1 = (bf16[1536,384]{1,0:T(8,128)(2,1)S(1)}, bf16[1536,384]{1,0:T(8,128)(2,1)}, u32[]{:S(2)}) copy-start(bf16[1536,384]{1,0:T(8,128)(2,1)} %refs_0_.1) | copy-start | bytes 3538948
  43.0 24.5 %collective-permute-start.10 = (bf16[48,384]{1,0:T(8,128)(2,1)S(1)}, bf16[48,384]{1,0:T(8,128)(2,1)S(1)}, u32[]{:S(2)}, u32[]{:S(2)}) collective-permute-start(bf16[48,384]{1,0:T(8,128)(2,1)S(1)} %get-tuple-element.45.refs_5_), channel_id=1, source_target_pairs={{8,0},{16,8},{24,16},{32,24},{40,32},{48,40},{56,48},{64,56},{72,6... | collective-permute-start | bytes 110600 | tf_op jit(solution)/shard_map/ppermute | solution.py:618
  44.3 23.2 %collective-permute-start.9 = (bf16[48,384]{1,0:T(8,128)(2,1)S(1)}, bf16[48,384]{1,0:T(8,128)(2,1)S(1)}, u32[]{:S(2)}, u32[]{:S(2)}) collective-permute-start(bf16[48,384]{1,0:T(8,128)(2,1)S(1)} %get-tuple-element.46.refs_6_), channel_id=1, source_target_pairs={{0,8},{8,16},{16,24},{24,32},{32,40},{40,48},{48,56},{56,64},{64,7... | collective-permute-start | bytes 110600 | tf_op jit(solution)/shard_map/ppermute | solution.py:615
  62.6 13.3 %collective-permute-start.7 = (bf16[512,384]{1,0:T(8,128)(2,1)S(1)}, bf16[512,384]{1,0:T(8,128)(2,1)S(1)}, u32[]{:S(2)}, u32[]{:S(2)}) collective-permute-start(bf16[512,384]{1,0:T(8,128)(2,1)S(1)} %get-tuple-element.49), channel_id=1, source_target_pairs={{0,4},{1,5},{2,6},{3,7},{4,0},{5,1},{6,2},{7,3},{8,12},{9,13},{10,... | collective-permute-start | bytes 1179656 | tf_op jit(solution)/shard_map/ppermute | solution.py:131
  63.7 12.2 %collective-permute-start.8 = (bf16[512,384]{1,0:T(8,128)(2,1)S(1)}, bf16[512,384]{1,0:T(8,128)(2,1)S(1)}, u32[]{:S(2)}, u32[]{:S(2)}) collective-permute-start(bf16[512,384]{1,0:T(8,128)(2,1)S(1)} %get-tuple-element.50), channel_id=1, source_target_pairs={{0,3},{1,0},{2,1},{3,2},{4,7},{5,4},{6,5},{7,6},{8,11},{9,8},{10,9... | collective-permute-start | bytes 1179656 | tf_op jit(solution)/shard_map/ppermute | solution.py:131
  67.4 9.0 %collective-permute-start.6 = (bf16[512,384]{1,0:T(8,128)(2,1)S(1)}, bf16[512,384]{1,0:T(8,128)(2,1)S(1)}, u32[]{:S(2)}, u32[]{:S(2)}) collective-permute-start(bf16[512,384]{1,0:T(8,128)(2,1)S(1)} %get-tuple-element.48.refs_5_), channel_id=1, source_target_pairs={{0,1},{1,2},{2,3},{3,0},{4,5},{5,6},{6,7},{7,4},{8,9},{9,10},{10,1... | collective-permute-start | bytes 1179656 | tf_op jit(solution)/shard_map/ppermute | solution.py:131
  68.5 17.8 %collective-permute-start.14 = (bf16[4,144,384]{2,1,0:T(8,128)(2,1)S(1)}, bf16[4,144,384]{2,1,0:T(8,128)(2,1)S(1)}, u32[]{:S(2)}, u32[]{:S(2)}) collective-permute-start(bf16[4,144,384]{2,1,0:T(8,128)(2,1)S(1)} %get-tuple-element.60), channel_id=1, source_target_pairs={{0,4},{1,5},{2,6},{3,7},{4,0},{5,1},{6,2},{7,3},{8,12},{9,13},{10,... | collective-permute-start | bytes 1327112 | tf_op jit(solution)/shard_map/ppermute | solution.py:131
  81.9 12.0 %collective-permute-start.13 = (bf16[6,144,256]{2,1,0:T(8,128)(2,1)S(1)}, bf16[6,144,256]{2,1,0:T(8,128)(2,1)S(1)}, u32[]{:S(2)}, u32[]{:S(2)}) collective-permute-start(bf16[6,144,256]{2,1,0:T(8,128)(2,1)S(1)} %get-tuple-element.58.refs_2_.refs_0_), channel_id=1, source_target_pairs={{0,4},{1,5},{2,6},{3,7},{4,0},{5,1},{6,2},{7,3},{8,12},{9,13},{10,... | collective-permute-start | bytes 1327112 | tf_op jit(solution)/shard_map/ppermute | solution.py:131
  83.1 12.3 %collective-permute-start.12 = (bf16[6,144,256]{2,1,0:T(8,128)(2,1)S(1)}, bf16[6,144,256]{2,1,0:T(8,128)(2,1)S(1)}, u32[]{:S(2)}, u32[]{:S(2)}) collective-permute-start(bf16[6,144,256]{2,1,0:T(8,128)(2,1)S(1)} %get-tuple-element.58.refs_2_.refs_0_), channel_id=1, source_target_pairs={{0,3},{1,0},{2,1},{3,2},{4,7},{5,4},{6,5},{7,6},{8,11},{9,8},{10,9... | collective-permute-start | bytes 1327112 | tf_op jit(solution)/shard_map/ppermute | solution.py:131
  86.3 12.5 %collective-permute-start.11 = (bf16[6,144,256]{2,1,0:T(8,128)(2,1)S(1)}, bf16[6,144,256]{2,1,0:T(8,128)(2,1)S(1)}, u32[]{:S(2)}, u32[]{:S(2)}) collective-permute-start(bf16[6,144,256]{2,1,0:T(8,128)(2,1)S(1)} %get-tuple-element.58.refs_2_.refs_0_), channel_id=1, source_target_pairs={{0,1},{1,2},{2,3},{3,0},{4,5},{5,6},{6,7},{7,4},{8,9},{9,10},{10,1... | collective-permute-start | bytes 1327112 | tf_op jit(solution)/shard_map/ppermute | solution.py:131
  98.9 11.6 %collective-permute-start.15 = (bf16[6,144,256]{2,1,0:T(8,128)(2,1)S(1)}, bf16[6,144,256]{2,1,0:T(8,128)(2,1)S(1)}, u32[]{:S(2)}, u32[]{:S(2)}) collective-permute-start(bf16[6,144,256]{2,1,0:T(8,128)(2,1)S(1)} %get-tuple-element.63.refs_3_), channel_id=1, source_target_pairs={{0,1},{1,2},{2,3},{3,0},{4,5},{5,6},{6,7},{7,4},{8,9},{9,10},{10,1... | collective-permute-start | bytes 1327112 | tf_op jit(solution)/shard_map/ppermute | solution.py:131
  98.9 11.6 %collective-permute-start.17 = (bf16[6,144,256]{2,1,0:T(8,128)(2,1)S(1)}, bf16[6,144,256]{2,1,0:T(8,128)(2,1)S(1)}, u32[]{:S(2)}, u32[]{:S(2)}) collective-permute-start(bf16[6,144,256]{2,1,0:T(8,128)(2,1)S(1)} %get-tuple-element.64.refs_2_), channel_id=1, source_target_pairs={{0,3},{1,0},{2,1},{3,2},{4,7},{5,4},{6,5},{7,6},{8,11},{9,8},{10,9... | collective-permute-start | bytes 1327112 | tf_op jit(solution)/shard_map/ppermute | solution.py:131
  102.1 10.9 %collective-permute-start.16 = (bf16[6,144,256]{2,1,0:T(8,128)(2,1)S(1)}, bf16[6,144,256]{2,1,0:T(8,128)(2,1)S(1)}, u32[]{:S(2)}, u32[]{:S(2)}) collective-permute-start(bf16[6,144,256]{2,1,0:T(8,128)(2,1)S(1)} %get-tuple-element.64.refs_2_), channel_id=1, source_target_pairs={{0,4},{1,5},{2,6},{3,7},{4,0},{5,1},{6,2},{7,3},{8,12},{9,13},{10,... | collective-permute-start | bytes 1327112 | tf_op jit(solution)/shard_map/ppermute | solution.py:131
  102.5 10.6 %collective-permute-start.23 = (f32[2,32,384]{2,1,0:T(8,128)S(1)}, f32[2,32,384]{2,1,0:T(8,128)S(1)}, u32[]{:S(2)}, u32[]{:S(2)}) collective-permute-start(f32[2,32,384]{2,1,0:T(8,128)S(1)} %get-tuple-element.71), channel_id=1, source_target_pairs={{0,8},{8,16},{16,24},{24,32},{32,40},{40,48},{48,56},{56,64},{64,7... | collective-permute-start | bytes 294920 | tf_op jit(solution)/shard_map/ppermute | solution.py:615
  107.3 8.0 %collective-permute-start.24 = (f32[2,32,384]{2,1,0:T(8,128)S(1)}, f32[2,32,384]{2,1,0:T(8,128)S(1)}, u32[]{:S(2)}, u32[]{:S(2)}) collective-permute-start(f32[2,32,384]{2,1,0:T(8,128)S(1)} %get-tuple-element.62.refs_3_), channel_id=1, source_target_pairs={{8,0},{16,8},{24,16},{32,24},{40,32},{48,40},{56,48},{64,56},{72,6... | collective-permute-start | bytes 294920 | tf_op jit(solution)/shard_map/ppermute | solution.py:618
  116.3 5.2 %collective-permute-start.25 = (bf16[4,32,384]{2,1,0:T(8,128)(2,1)S(1)}, bf16[4,32,384]{2,1,0:T(8,128)(2,1)S(1)}, u32[]{:S(2)}, u32[]{:S(2)}) collective-permute-start(bf16[4,32,384]{2,1,0:T(8,128)(2,1)S(1)} %get-tuple-element.72.refs_12_), channel_id=1, source_target_pairs={{0,4},{1,5},{2,6},{3,7},{4,0},{5,1},{6,2},{7,3},{8,12},{9,13},{10,... | collective-permute-start | bytes 294920 | tf_op jit(solution)/shard_map/ppermute | solution.py:131
  117.1 9.6 %collective-permute-start.20 = (bf16[2,144,384]{2,1,0:T(8,128)(2,1)S(1)}, bf16[2,144,384]{2,1,0:T(8,128)(2,1)S(1)}, u32[]{:S(2)}, u32[]{:S(2)}) collective-permute-start(bf16[2,144,384]{2,1,0:T(8,128)(2,1)S(1)} %get-tuple-element.67), channel_id=1, source_target_pairs={{0,2},{1,3},{2,0},{3,1},{4,6},{5,7},{6,4},{7,5},{8,10},{9,11},{10,... | collective-permute-start | bytes 663560 | tf_op jit(solution)/shard_map/ppermute | solution.py:131
  117.1 13.9 %collective-permute-start.22 = (bf16[2,144,384]{2,1,0:T(8,128)(2,1)S(1)}, bf16[2,144,384]{2,1,0:T(8,128)(2,1)S(1)}, u32[]{:S(2)}, u32[]{:S(2)}) collective-permute-start(bf16[2,144,384]{2,1,0:T(8,128)(2,1)S(1)} %get-tuple-element.69), channel_id=1, source_target_pairs={{0,1},{1,2},{2,3},{3,0},{4,5},{5,6},{6,7},{7,4},{8,9},{9,10},{10,1... | collective-permute-start | bytes 663560 | tf_op jit(solution)/shard_map/ppermute | solution.py:131
  117.9 13.7 %collective-permute-start.21 = (bf16[2,144,384]{2,1,0:T(8,128)(2,1)S(1)}, bf16[2,144,384]{2,1,0:T(8,128)(2,1)S(1)}, u32[]{:S(2)}, u32[]{:S(2)}) collective-permute-start(bf16[2,144,384]{2,1,0:T(8,128)(2,1)S(1)} %get-tuple-element.61.refs_11_), channel_id=1, source_target_pairs={{0,3},{1,0},{2,1},{3,2},{4,7},{5,4},{6,5},{7,6},{8,11},{9,8},{10,9... | collective-permute-start | bytes 663560 | tf_op jit(solution)/shard_map/ppermute | solution.py:131
  120.3 17.9 %collective-permute-start.19 = (bf16[3,144,256]{2,1,0:T(8,128)(2,1)S(1)}, bf16[3,144,256]{2,1,0:T(8,128)(2,1)S(1)}, u32[]{:S(2)}, u32[]{:S(2)}) collective-permute-start(bf16[3,144,256]{2,1,0:T(8,128)(2,1)S(1)} %get-tuple-element.66), channel_id=1, source_target_pairs={{0,3},{1,0},{2,1},{3,2},{4,7},{5,4},{6,5},{7,6},{8,11},{9,8},{10,9... | collective-permute-start | bytes 663560 | tf_op jit(solution)/shard_map/ppermute | solution.py:131
  121.5 16.8 %collective-permute-start.18 = (bf16[3,144,256]{2,1,0:T(8,128)(2,1)S(1)}, bf16[3,144,256]{2,1,0:T(8,128)(2,1)S(1)}, u32[]{:S(2)}, u32[]{:S(2)}) collective-permute-start(bf16[3,144,256]{2,1,0:T(8,128)(2,1)S(1)} %get-tuple-element.65.refs_5_), channel_id=1, source_target_pairs={{0,1},{1,2},{2,3},{3,0},{4,5},{5,6},{6,7},{7,4},{8,9},{9,10},{10,1... | collective-permute-start | bytes 663560 | tf_op jit(solution)/shard_map/ppermute | solution.py:131
  126.6 9.1 %collective-permute-start.26 = (bf16[32,384]{1,0:T(8,128)(2,1)S(1)}, bf16[32,384]{1,0:T(8,128)(2,1)S(1)}, u32[]{:S(2)}, u32[]{:S(2)}) collective-permute-start(bf16[32,384]{1,0:T(8,128)(2,1)S(1)} %get-tuple-element.75), channel_id=1, source_target_pairs={{0,3},{1,0},{2,1},{3,2},{4,7},{5,4},{6,5},{7,6},{8,11},{9,8},{10,9... | collective-permute-start | bytes 73736 | tf_op jit(solution)/shard_map/ppermute | solution.py:131
  131.0 5.8 %collective-permute-start.27 = (bf16[32,384]{1,0:T(8,128)(2,1)S(1)}, bf16[32,384]{1,0:T(8,128)(2,1)S(1)}, u32[]{:S(2)}, u32[]{:S(2)}) collective-permute-start(bf16[32,384]{1,0:T(8,128)(2,1)S(1)} %get-tuple-element.76), channel_id=1, source_target_pairs={{0,2},{1,3},{2,0},{3,1},{4,6},{5,7},{6,4},{7,5},{8,10},{9,11},{10,... | collective-permute-start | bytes 73736 | tf_op jit(solution)/shard_map/ppermute | solution.py:131
  131.6 5.5 %collective-permute-start.28 = (bf16[32,384]{1,0:T(8,128)(2,1)S(1)}, bf16[32,384]{1,0:T(8,128)(2,1)S(1)}, u32[]{:S(2)}, u32[]{:S(2)}) collective-permute-start(bf16[32,384]{1,0:T(8,128)(2,1)S(1)} %get-tuple-element.77), channel_id=1, source_target_pairs={{0,1},{1,2},{2,3},{3,0},{4,5},{5,6},{6,7},{7,4},{8,9},{9,10},{10,1... | collective-permute-start | bytes 73736 | tf_op jit(solution)/shard_map/ppermute | solution.py:131

commit v4 on v3

--- a/solution.py
+++ b/solution.py
@@ -287,20 +287,55 @@
     )
 
 
-def value_pairs_kernel(keep_ref, got_ref, *out_refs):
-    for dx in range(1, 4):
-        out_refs[dx - 1][0] = keep_ref[dx]
-        out_refs[dx - 1][1] = got_ref[dx]
-
-
-def value_pairs(keep, got, *extra):
-    return call(
-        value_pairs_kernel,
-        "value_pairs",
-        0,
-        [(VMEM, keep), (VMEM, got)],
-        extra,
-        [pltpu.VMEM((2, KEYS, GROUP), BF16)] * 3,
+FAR = TILES
+NEAR = FAR + 2
+MID = NEAR + 3
+LATE = TILES // 2 + 2
+
+
+def mid_parts_kernel(across_ref, right_ref, keep_ref, got_ref, for_right, for_left, for_across):
+    for ref, far, dx, out in (
+        (across_ref, keep_ref, 3, for_right),
+        (right_ref, got_ref, 1, for_left),
+    ):
+        out[:TILES] = ref[...]
+        out[FAR] = far[2, :, :TILE]
+        out[FAR + 1, :, :HEAD] = far[2, :, TILE:]
+        out[FAR + 1, :, HEAD:] = jnp.zeros((KEYS, HEAD), BF16)
+        out[NEAR] = keep_ref[dx, :, :TILE]
+        out[NEAR + 1] = got_ref[dx, :, :TILE]
+        out[NEAR + 2, :, :HEAD] = keep_ref[dx, :, TILE:]
+        out[NEAR + 2, :, HEAD:] = got_ref[dx, :, TILE:]
+    for_across[...] = right_ref[...]
+
+
+def mid_parts(from_across, from_right, keep, got, *extra):
+    return call(
+        mid_parts_kernel,
+        "mid_parts",
+        0,
+        [(VMEM, a) for a in (from_across, from_right, keep, got)],
+        extra,
+        [pltpu.VMEM((MID, KEYS, TILE), BF16)] * 2 + [pltpu.VMEM((TILES, KEYS, TILE), BF16)],
+    )
+
+
+def last_parts_kernel(left_ref, far_ref, right_ref, for_right, for_left):
+    half = TILES // 2
+    for_right[:half] = left_ref[:half]
+    for_right[half:] = left_ref[FAR:NEAR]
+    for_left[:half] = right_ref[half:TILES]
+    for_left[half:] = far_ref[FAR:NEAR]
+
+
+def last_parts(from_left, far, from_right, *extra):
+    return call(
+        last_parts_kernel,
+        "last_parts",
+        0,
+        [(VMEM, a) for a in (from_left, far, from_right)],
+        extra,
+        [pltpu.VMEM((LATE, KEYS, TILE), BF16)] * 2,
     )
 
 
@@ -326,36 +361,52 @@
     return jnp.where(lane == 0, mean, square)
 
 
-def stage_kernel(first, count, start, *refs):
-    x_refs, w_ref, refs = refs[:count], refs[count], refs[count + 1 :]
-    acc_in, stat_in = (None, None) if start else refs[:2]
-    acc, stat = refs[-2:]
-    weights = pl.ds(first * GROUP, count * GROUP)
+def first_kernel(*refs):
+    x_refs, (w_ref, acc_q, acc_kv, stat) = refs[:4], refs[4:]
 
     @pl.loop(0, TILES)
     def _(t):
         rows = rows_of(t)
         block = jnp.concatenate([ref[rows, :] for ref in x_refs], axis=1)
-        total = dot(block, w_ref[weights, :])
-        if start:
-            acc[rows, :] = total
-            stat[rows, :] = packed_stats(*row_stats(block))
-        else:
-            acc[rows, :] = acc_in[rows, :] + total
-            stat[rows, :] = packed_stats(*merged_stats(stat_in[rows, :], first * GROUP, block))
-
-
-def stage(blocks, weights, first, before=(), extra=()):
-    count, start = len(blocks), not before
-    inputs = [(VMEM, a) for a in (*blocks, weights, *before)]
-    return call(
-        functools.partial(stage_kernel, first, count, start),
-        f"stage_{first}",
+        total = dot(block, w_ref[: 4 * GROUP, :])
+        acc_q[rows, :] = total[:, :GROUP]
+        acc_kv[rows, :] = total[:, GROUP:]
+        stat[rows, :] = packed_stats(*row_stats(block))
+
+
+def first_half(blocks, weights, *extra):
+    return call(
+        first_kernel,
+        "first_half",
         4,
-        inputs,
-        extra,
-        [pltpu.VMEM((VID, 3 * GROUP), F32), pltpu.VMEM((VID, HEAD), F32)],
-        aliases={} if start else {count + 1: 0, count + 2: 1},
+        [(VMEM, a) for a in (*blocks, weights)],
+        extra,
+        [
+            pltpu.VMEM((VID, GROUP), F32),
+            pltpu.VMEM((VID, 2 * GROUP), F32),
+            pltpu.VMEM((VID, HEAD), F32),
+        ],
+    )
+
+
+def middle_kernel(xa, xb, xc, w_ref, acc_in, stat_in, acc, stat):
+    @pl.loop(0, TILES, unroll=2)
+    def _(t):
+        rows = rows_of(t)
+        block = jnp.concatenate([xa[rows, :], xb[rows, :], xc[rows, :]], axis=1)
+        acc[rows, :] = acc_in[rows, :] + dot(block, w_ref[4 * GROUP : 7 * GROUP, :GROUP])
+        stat[rows, :] = packed_stats(*merged_stats(stat_in[rows, :], 4 * GROUP, block))
+
+
+def middle(blocks, weights, acc, stat, *extra):
+    return call(
+        middle_kernel,
+        "middle",
+        4,
+        [(VMEM, a) for a in (*blocks, weights, acc, stat)],
+        extra,
+        [pltpu.VMEM((VID, GROUP), F32), pltpu.VMEM((VID, HEAD), F32)],
+        aliases={4: 0, 5: 1},
     )
 
 
@@ -367,7 +418,7 @@
 def by_thirds(body, pieces):
     for k, piece in enumerate(pieces):
 
-        @pl.loop(0, TILES // 3)
+        @pl.loop(0, TILES // 3, unroll=True)
         def _(u, k=k, piece=piece):
             body(k * (TILES // 3) + u, piece[rows_of(u), :])
 
@@ -402,7 +453,7 @@
         mean, square = merged_stats(stat_in[rows, :], 7 * GROUP, block)
         var = square / D
         stat[rows, :] = packed_stats(mean, var)
-        total = acc[rows, :GROUP] + dot(block, w_ref[LAST, :GROUP]) - mean * sums
+        total = acc[rows, :] + dot(block, w_ref[LAST, :GROUP]) - mean * sums
         floor = EPS * (var + EPS)
         for h in range(HEADS_DEV):
             cols = slice(h * HEAD, (h + 1) * HEAD)
@@ -428,7 +479,7 @@
 
 
 def audio_part_kernel(
-    meta_ref, xa, xb, xc, w_ref, acc, stat, sums_ref, qkv_ref, prev_ref, next_ref,
+    meta_ref, ya, yb, yc, xa, xb, xc, w_ref, acc, stat, sums_ref, qkv_ref, prev_ref, next_ref,
     part_p, part_o, part_n,
 ):
     shard = meta_ref[AT_SHARD]
@@ -448,7 +499,8 @@
     def body(t, block):
         rows = rows_of(t)
         mean, var = stat[rows, :1], stat[rows, 1:2]
-        total = acc[rows, GROUP:] + dot(block, w_ref[LAST, GROUP:]) - mean * sums
+        block = jnp.concatenate([ya[rows, :], yb[rows, :], yc[rows, :], block], axis=1)
+        total = acc[rows, :] + dot(block, w_ref[4 * GROUP :, GROUP:]) - mean * sums
         floor = EPS * (var + EPS)
         spread = lax.rsqrt(var + EPS)
         place = t * TILE + lax.broadcasted_iota(jnp.int32, (3 * AUD, TILE), 1)
@@ -515,63 +567,56 @@
     )
 
 
-def audio_sum_kernel(meta_ref, *refs):
+def audio_sum_kernel(meta_ref, done_ref, *refs):
     total = sum(ref[...].astype(F32) for ref in refs[:4])
     row = lax.broadcasted_iota(jnp.int32, (AUD, 1), 0)
     valid = row < meta_ref[AT_AUDIO + meta_ref[AT_SHARD]]
     refs[4][...] = jnp.where(valid, total, 0.0).astype(BF16)
 
 
-def audio_sum(meta, received):
+def audio_sum(meta, received, done):
     (out,) = call(
         audio_sum_kernel,
         "audio_sum",
         0,
-        [(SMEM, meta)] + [(VMEM, a) for a in received],
+        [(SMEM, meta), (HBM, done)] + [(VMEM, a) for a in received],
         (),
         [sds((AUD, GROUP), BF16)],
     )
     return out
 
 
-def output_first_kernel(*refs):
-    p_refs, (keep, got, v1, v2, v3), (out_ref, projected) = refs[:7], refs[7:12], refs[12:]
-    blocks = (keep[0], v3[0], v1[0], got[0], v3[1], v2[0], v1[1])
+def output_kernel(meta_ref, *refs):
+    p_refs, (low_ref, high_ref, keep, got, out_ref, projected, out, sems) = refs[:7], refs[7:]
+    half = TILES // 2
+
+    left_ref, right_ref = p_refs[4], p_refs[5]
+
+    def near(ref, k):
+        tail = slice(k * HEAD, (k + 1) * HEAD)
+        return jnp.concatenate([ref[NEAR + k], ref[NEAR + 2, :, tail]], axis=1)
+
+    def far(ref):
+        return jnp.concatenate([ref[half], ref[half + 1, :, :HEAD]], axis=1)
+
+    blocks = (
+        keep[0], near(left_ref, 0), near(right_ref, 0), got[0],
+        near(left_ref, 1), far(low_ref), near(right_ref, 1), far(high_ref),
+    )
     for j, block in enumerate(blocks):
         projected[j * KEYS : (j + 1) * KEYS, :] = block
-
-    @pl.loop(0, TILES)
-    def _(t):
-        probs = jnp.concatenate([ref[t] for ref in p_refs], axis=0)
-        out_ref[rows_of(t), :] = dot_tn(probs, projected[...])
-
-
-def output_first(probs, values, *extra):
-    (out,) = call(
-        output_first_kernel,
-        "output_first",
-        0,
-        [(VMEM, a) for a in (*probs, *values)],
-        extra,
-        [pltpu.VMEM((VID, GROUP), F32)],
-        [pltpu.VMEM((7 * KEYS, GROUP), BF16)],
-    )
-    return out
-
-
-def output_last_kernel(meta_ref, low_ref, high_ref, v_ref, sum_ref, out_ref, out, sems):
     limit = meta_ref[AT_VIDEO + meta_ref[AT_SHARD]]
-    value = v_ref[1]
 
     def copy(t):
         return pltpu.make_async_copy(out.at[rows_of(t), :], out_ref.at[rows_of(t), :], sems.at[t])
 
     for k, ref in enumerate((low_ref, high_ref)):
 
-        @pl.loop(0, TILES // 2)
+        @pl.loop(0, half)
         def _(u, k=k, ref=ref):
-            t = k * (TILES // 2) + u
-            result = sum_ref[rows_of(t), :] + dot_tn(ref[u], value)
+            t = k * half + u
+            probs = jnp.concatenate([p[t] for p in p_refs] + [ref[u]], axis=0)
+            result = dot_tn(probs, projected[...])
             row = t * TILE + lax.broadcasted_iota(jnp.int32, (TILE, 1), 0)
             out[rows_of(t), :] = jnp.where(row < limit, result, 0.0).astype(BF16)
             copy(t).start()
@@ -580,15 +625,19 @@
         copy(t).wait()
 
 
-def output_last(meta, low, high, values, sums):
+def output(meta, probs, low, high, keep, got, *extra):
     (out,) = call(
-        output_last_kernel,
-        "output_last",
+        output_kernel,
+        "output",
         1,
-        [(SMEM, meta), (VMEM, low), (VMEM, high), (VMEM, values), (VMEM, sums)],
+        [(SMEM, meta)] + [(VMEM, a) for a in (*probs, low, high, keep, got)],
         (),
         [sds((VID, GROUP), BF16)],
-        [pltpu.VMEM((VID, GROUP), BF16), pltpu.SemaphoreType.DMA((TILES,))],
+        [
+            pltpu.VMEM((N_TENSOR * KEYS, GROUP), BF16),
+            pltpu.VMEM((VID, GROUP), BF16),
+            pltpu.SemaphoreType.DMA((TILES,)),
+        ],
         out_spec=ANY,
     )
     return out
@@ -645,36 +694,35 @@
     yl, xq, yr = right(xy), left(xr), across(xr)
     qkv, for_prev, for_next = audio_in(audio_blocks, w_query, w_key, w_value, xl)
     from_next, from_prev = to_prev(for_prev), to_next(for_next)
-    acc, stat = stage((video_tokens, xl, xr, xy), weights, 0, (), (for_prev, for_next))
+    acc_q, acc_kv, stat = first_half(
+        (video_tokens, xl, xr, xy), weights, for_prev, for_next
+    )
 
     thirds = parts(((yl, 0, THIRD), (xq, THIRD, THIRD), (yr, 2 * THIRD, THIRD)), stat)
     pieces = right(thirds[0]), across(thirds[1]), left(thirds[2])
     keep_v, give_v = value_out(meta, qkv, from_prev, from_next, w_back, thirds[0])
     got_v = across(give_v)
-    acc, stat = stage((yl, xq, yr), weights, 4, (acc, stat), (keep_v,))
+    blocks = (yl, xq, yr)
+    acc_q, stat = middle(blocks, weights, acc_q, stat, keep_v)
 
     heard = (qkv, from_prev, from_next)
-    probs, stat = queries_out(meta, pieces, weights, acc, stat, sums, *heard)
+    probs, stat = queries_out(meta, pieces, weights, acc_q, stat, sums, *heard)
     pl_, pr_, py_ = right(probs), left(probs), across(probs)
-    to_send = value_pairs(keep_v, got_v, probs)
-    v1, v2, v3 = [send(pair, 0, -dx) for dx, pair in enumerate(to_send, 1)]
     part_prev, part_own, part_next = audio_part(
-        meta, pieces, weights, acc, stat, sums, *heard, to_send[0]
-    )
-    pl_, pr_, py_ = gate((pl_, pr_, py_), part_prev)
-    pyl, pq, pyr = right(py_), left(pr_), across(pr_)
+        meta, (*blocks, *pieces), weights, acc_kv, stat, sums, *heard
+    )
+    for_right, for_left, for_across = mid_parts(py_, pr_, keep_v, got_v, part_prev, pl_)
+    pyl, pq, pyr = right(for_right), left(for_left), across(for_across)
     audio_from_next, audio_from_prev = to_prev(part_prev), to_next(part_next)
-    half = TILES // 2
-    low, high = parts(((pyl, 0, half), (pyr, half, half)), pq)
-    far_low, far_high = right(low), left(high)
-    keep, give = audio_out(meta, part_own, audio_from_prev, audio_from_next, w_back, low)
+    keep, give = audio_out(meta, part_own, audio_from_prev, audio_from_next, w_back, for_right)
+    for_right, for_left = last_parts(pyl, pq, pyr, give)
+    low, high = right(for_right), left(for_left)
     pairs = audio_pair(keep, across(give))
     received = [pairs[0]] + [send(pairs[dx], 0, -dx) for dx in range(1, 4)]
-    video_sums = output_first(
-        (probs, pl_, pr_, py_, pyl, pq, pyr), (keep_v, got_v, v1, v2, v3), give
-    )
-    audio_update = audio_sum(meta, received)
-    video_update = output_last(meta, far_low, far_high, v2, video_sums)
+    video_update = output(
+        meta, (probs, pl_, pr_, py_, pyl, pq, pyr), low, high, keep_v, got_v, pairs[0]
+    )
+    audio_update = audio_sum(meta, received, video_update)
     return (video_update, audio_update)
 
 

time: 142 us -> 133 us (0.937)
  starting transfers between devices: 42.4 us -> 37.7 us
  Pallas kernels: 46.9 us -> 42.3 us
    ppermute x25 -> x22, starting transfers between devices: 29 us -> 24.1 us  [send(): return lax.ppermute(array, 'tensor', pairs)]
    pallas_call x17 -> x15, Pallas kernels: 46.9 us -> 42.3 us  [call(): pl.pallas_call(run, in_specs=[spec for spec, _ in inputs] + [ANY] * len(e...]
    ppermute x25 -> x22, waiting for transfers between devices: 24.6 us -> 20.8 us  [send(): return lax.ppermute(array, 'tensor', pairs)]
    ppermute x2, waiting for transfers between devices: 0.01 us -> 3.11 us  [to_next(): return lax.ppermute(array, ('tower', 'tm'), up)]
  transfers between devices with their start and end apart: 29 -> 26, of which waited for: 13 -> 10; matrix products, arithmetic and copies ran while one was open for 2% -> 2% of each run, Pallas kernels for 30% -> 31%
where the time goes in v4:
time: 133 us
  Pallas kernels  42.3 us (32%)
  starting transfers between devices  37.7 us (28%)
  waiting for transfers between devices  27.5 us (21%)
  blocking collectives  20.4 us (15%)
  local copies, waits for them, and re-layouts  3.7 us (3%)
    pallas_call x15, Pallas kernels, call(): pl.pallas_call(run, in_specs=[spec for spec, _ in inputs] + [ANY] * len(e...  42.3 us
    ppermute x22, starting transfers between devices, send(): return lax.ppermute(array, 'tensor', pairs)  24.1 us
    ppermute x22, waiting for transfers between devices, send(): return lax.ppermute(array, 'tensor', pairs)  20.8 us
    all_to_all x1, blocking collectives, shards(): audio_blocks = lax.all_to_all(audio_copies, 'tensor', 0, 0)  20.4 us
    ppermute x2, starting transfers between devices, to_next(): return lax.ppermute(array, ('tower', 'tm'), up)  11 us
    ppermute x2, waiting for transfers between devices, to_prev(): return lax.ppermute(array, ('tower', 'tm'), down)  3.61 us
    ppermute x2, waiting for transfers between devices, to_next(): return lax.ppermute(array, ('tower', 'tm'), up)  3.11 us
  transfers between devices with their start and end apart: 26, of which 10 were waited for; matrix products, arithmetic and copies ran while one was open for 2% of the time, Pallas kernels for 31%

profile of v4, /device:TPU:0, one launch (start us, length us, event | category | flops | bytes accessed | tf_op | source)
XLA Modules:
  0.0 132.5 jit_solution(11130017196782420418)
XLA Ops:
  0.6 2.9 %collective-permute-start.1 = (bf16[1536,384]{1,0:T(8,128)(2,1)}, bf16[1536,384]{1,0:T(8,128)(2,1)S(1)}, u32[]{:S(2)}, u32[]{:S(2)}) collective-permute-start(bf16[1536,384]{1,0:T(8,128)(2,1)} %refs_0_.1), channel_id=1, source_target_pairs={{0,3},{1,0},{2,1},{3,2},{4,7},{5,4},{6,5},{7,6},{8,11},{9,8},{10,9... | collective-permute-start | bytes 3538952 | tf_op jit(solution)/shard_map/ppermute | solution.py:131
  3.5 1.6 %collective-permute-start.2 = (bf16[1536,384]{1,0:T(8,128)(2,1)}, bf16[1536,384]{1,0:T(8,128)(2,1)S(1)}, u32[]{:S(2)}, u32[]{:S(2)}) collective-permute-start(bf16[1536,384]{1,0:T(8,128)(2,1)} %refs_0_.1), channel_id=1, source_target_pairs={{0,4},{1,5},{2,6},{3,7},{4,0},{5,1},{6,2},{7,3},{8,12},{9,13},{10,... | collective-permute-start | bytes 3538952 | tf_op jit(solution)/shard_map/ppermute | solution.py:131
  8.8 6.3 %prefetch.1 = (bf16[8,32,384]{2,1,0:T(8,128)(2,1)S(1)}, bf16[3072,1152]{1,0:T(8,128)(2,1)S(1)}, bf16[2,384,3072]{2,1,0:T(8,128)(2,1)S(1)}, f32[8,1152]{1,0:T(8,128)S(1)}) custom-call(s32[113]{0:T(128)S(1)} %concatenate.3.refs_0_, bf16[32,384]{1,0:T(8,128)(2,1)S(1)} %copy-done, bf16[2,3072,384]{2,1,0:T(8,128)(2,1)} %refs_1_.3, bf16[2,3072,384]{2,1,0:T(8,128)(2,1)} %refs_2_.3, ...), custom_call_target="tpu_custom_call" | custom-call | tf_op jit(solution)/shard_map/prefetch/pallas_call | solution.py:79
  15.1 20.4 %all_to_all.5.refs_3_.refs_0_ = bf16[8,32,384]{2,1,0:T(8,128)(2,1)S(1)} all-to-all(bf16[8,32,384]{2,1,0:T(8,128)(2,1)S(1)} %get-tuple-element.38), channel_id=1, replica_groups=mesh['tower'=2,'tm'=8,'tensor'=8] {'tensor'}, dimensions={0} | all-to-all | bytes 393216 | tf_op jit(solution)/shard_map/all_to_all | solution.py:691
  36.1 3.1 %collective-permute-start.4 = (bf16[1536,384]{1,0:T(8,128)(2,1)S(1)}, bf16[1536,384]{1,0:T(8,128)(2,1)S(1)}, u32[]{:S(2)}, u32[]{:S(2)}) collective-permute-start(bf16[1536,384]{1,0:T(8,128)(2,1)S(1)} %get-tuple-element.40.refs_2_), channel_id=1, source_target_pairs={{0,3},{1,0},{2,1},{3,2},{4,7},{5,4},{6,5},{7,6},{8,11},{9,8},{10,9... | collective-permute-start | bytes 3538952 | tf_op jit(solution)/shard_map/ppermute | solution.py:131
  39.3 3.7 %audio_in.1 = (bf16[96,384]{1,0:T(8,128)(2,1)S(1)}, bf16[48,384]{1,0:T(8,128)(2,1)S(1)}, bf16[48,384]{1,0:T(8,128)(2,1)S(1)}) custom-call(bf16[8,32,384]{2,1,0:T(8,128)(2,1)S(1)} %all_to_all.5.refs_3_.refs_0_, bf16[2,3072,384]{2,1,0:T(8,128)(2,1)} %refs_1_.3, bf16[2,3072,384]{2,1,0:T(8,128)(2,1)} %refs_2_.3, bf16[2,3072,384]{2,1,0:T(8,128)(2,1)} %refs_3_.3, ...), custom_call_target="tpu_custom_call" | custom-call | flops 2000000000 | tf_op jit(solution)/shard_map/audio_in/pallas_call | solution.py:79
  43.0 1.3 collective-permute-start.10
  44.3 6.1 %collective-permute-start.9 = (bf16[48,384]{1,0:T(8,128)(2,1)S(1)}, bf16[48,384]{1,0:T(8,128)(2,1)S(1)}, u32[]{:S(2)}, u32[]{:S(2)}) collective-permute-start(bf16[48,384]{1,0:T(8,128)(2,1)S(1)} %get-tuple-element.44.refs_6_), channel_id=1, source_target_pairs={{0,8},{8,16},{16,24},{24,32},{32,40},{40,48},{48,56},{56,64},{64,7... | collective-permute-start | bytes 110600 | tf_op jit(solution)/shard_map/ppermute | solution.py:664
  50.3 7.9 %first_half.1 = (f32[1536,384]{1,0:T(8,128)S(1)}, f32[1536,768]{1,0:T(8,128)S(1)}, f32[1536,128]{1,0:T(8,128)S(1)}) custom-call(bf16[1536,384]{1,0:T(8,128)(2,1)S(1)} %copy-done.1, bf16[1536,384]{1,0:T(8,128)(2,1)S(1)} %get-tuple-element.41.refs_4_.refs_1_, bf16[1536,384]{1,0:T(8,128)(2,1)S(1)} %get-tuple-element.40.refs_2_, ...), custom_call_target="tpu_custom_call" | custom-call | flops 4000000000 | tf_op jit(solution)/shard_map/first_half/pallas_call | solution.py:79
  58.2 4.3 %collective-permute-done.3.refs_0_.refs_1_ = bf16[1536,384]{1,0:T(8,128)(2,1)S(1)} collective-permute-done((bf16[1536,384]{1,0:T(8,128)(2,1)S(1)}, bf16[1536,384]{1,0:T(8,128)(2,1)S(1)}, u32[]{:S(2)}, u32[]{:S(2)}) %collective-permute-start.3) | collective-permute-done | bytes 1179680 | tf_op jit(solution)/shard_map/ppermute | solution.py:131
  62.6 1.1 collective-permute-start.7
  63.7 3.7 %collective-permute-start.8 = (bf16[512,384]{1,0:T(8,128)(2,1)S(1)}, bf16[512,384]{1,0:T(8,128)(2,1)S(1)}, u32[]{:S(2)}, u32[]{:S(2)}) collective-permute-start(bf16[512,384]{1,0:T(8,128)(2,1)S(1)} %get-tuple-element.48), channel_id=1, source_target_pairs={{0,3},{1,0},{2,1},{3,2},{4,7},{5,4},{6,5},{7,6},{8,11},{9,8},{10,9... | collective-permute-start | bytes 1179656 | tf_op jit(solution)/shard_map/ppermute | solution.py:131
  67.4 1.1 value_out.1
  69.2 3.5 %middle.1 = (f32[1536,384]{1,0:T(8,128)S(1)}, f32[1536,128]{1,0:T(8,128)S(1)}) custom-call(bf16[1536,384]{1,0:T(8,128)(2,1)S(1)} %collective-permute-done.3.refs_0_.refs_1_, bf16[1536,384]{1,0:T(8,128)(2,1)S(1)} %collective-permute-done.4.refs_1_.refs_2_, ...), custom_call_target="tpu_custom_call", output_to_operand_aliasing={{0}: (4, {}), {1}: (5, {})} | custom-call | flops 4000000000 | tf_op jit(solution)/shard_map/middle/pallas_call | solution.py:79
  73.6 2.8 %collective-permute-done.6.refs_1_.refs_4_ = bf16[512,384]{1,0:T(8,128)(2,1)S(1)} collective-permute-done((bf16[512,384]{1,0:T(8,128)(2,1)S(1)}, bf16[512,384]{1,0:T(8,128)(2,1)S(1)}, u32[]{:S(2)}, u32[]{:S(2)}) %collective-permute-start.6) | collective-permute-done | bytes 393248 | tf_op jit(solution)/shard_map/ppermute | solution.py:131
  76.4 4.9 %queries_out.1 = (bf16[6,144,256]{2,1,0:T(8,128)(2,1)S(1)}, f32[1536,128]{1,0:T(8,128)S(1)}) custom-call(s32[113]{0:T(128)S(1)} %concatenate.3.refs_0_, bf16[512,384]{1,0:T(8,128)(2,1)S(1)} %collective-permute-done.6.refs_1_.refs_4_, bf16[512,384]{1,0:T(8,128)(2,1)S(1)} %collective-permute-done.7.refs_2_.refs_5_, ...), custom_call_target="tpu_custom_call", output_to_operand_aliasing={{1}: (6, {})} | custom-call | flops 2000000000 | tf_op jit(solution)/shard_map/queries_out/pallas_call | solution.py:79
  82.6 1.3 collective-permute-start.11
  83.8 8.0 %audio_part.1 = (f32[2,32,384]{2,1,0:T(8,128)S(1)}, f32[2,32,384]{2,1,0:T(8,128)S(1)}, f32[2,32,384]{2,1,0:T(8,128)S(1)}) custom-call(s32[113]{0:T(128)S(1)} %concatenate.3.refs_0_, bf16[1536,384]{1,0:T(8,128)(2,1)S(1)} %collective-permute-done.3.refs_0_.refs_1_, bf16[1536,384]{1,0:T(8,128)(2,1)S(1)} %collective-permute-done.4.refs_1_.refs_2_, ...), custom_call_target="tpu_custom_call" | custom-call | tf_op jit(solution)/shard_map/audio_part/pallas_call | solution.py:79
  91.8 3.2 %collective-permute-done.11.refs_5_.refs_2_ = bf16[6,144,256]{2,1,0:T(8,128)(2,1)S(1)} collective-permute-done((bf16[6,144,256]{2,1,0:T(8,128)(2,1)S(1)}, bf16[6,144,256]{2,1,0:T(8,128)(2,1)S(1)}, u32[]{:S(2)}, u32[]{:S(2)}) %collective-permute-start.11) | collective-permute-done | bytes 442400 | tf_op jit(solution)/shard_map/ppermute | solution.py:131
  95.6 1.7 %collective-permute-start.15 = (bf16[11,144,256]{2,1,0:T(8,128)(2,1)S(1)}, bf16[11,144,256]{2,1,0:T(8,128)(2,1)S(1)}, u32[]{:S(2)}, u32[]{:S(2)}) collective-permute-start(bf16[11,144,256]{2,1,0:T(8,128)(2,1)S(1)} %get-tuple-element.61.refs_5_), channel_id=1, source_target_pairs={{0,1},{1,2},{2,3},{3,0},{4,5},{5,6},{6,7},{7,4},{8,9},{9,10},{10,1... | collective-permute-start | bytes 2433032 | tf_op jit(solution)/shard_map/ppermute | solution.py:131
  97.7 5.0 %collective-permute-start.18 = (f32[2,32,384]{2,1,0:T(8,128)S(1)}, f32[2,32,384]{2,1,0:T(8,128)S(1)}, u32[]{:S(2)}, u32[]{:S(2)}) collective-permute-start(f32[2,32,384]{2,1,0:T(8,128)S(1)} %get-tuple-element.65), channel_id=1, source_target_pairs={{0,8},{8,16},{16,24},{24,32},{32,40},{40,48},{48,56},{56,64},{64,7... | collective-permute-start | bytes 294920 | tf_op jit(solution)/shard_map/ppermute | solution.py:664
  102.7 1.3 collective-permute-start.19
  104.0 3.1 %collective-permute-done.18.refs_2_ = f32[2,32,384]{2,1,0:T(8,128)S(1)} collective-permute-done((f32[2,32,384]{2,1,0:T(8,128)S(1)}, f32[2,32,384]{2,1,0:T(8,128)S(1)}, u32[]{:S(2)}, u32[]{:S(2)}) %collective-permute-start.18) | collective-permute-done | bytes 98336 | tf_op jit(solution)/shard_map/ppermute | solution.py:664
  107.1 3.6 %collective-permute-done.19.refs_3_ = f32[2,32,384]{2,1,0:T(8,128)S(1)} collective-permute-done((f32[2,32,384]{2,1,0:T(8,128)S(1)}, f32[2,32,384]{2,1,0:T(8,128)S(1)}, u32[]{:S(2)}, u32[]{:S(2)}) %collective-permute-start.19) | collective-permute-done | bytes 98336 | tf_op jit(solution)/shard_map/ppermute | solution.py:667
  110.7 1.0 audio_out.1
  111.7 1.9 %collective-permute-done.16.refs_1_.refs_6_ = bf16[11,144,256]{2,1,0:T(8,128)(2,1)S(1)} collective-permute-done((bf16[11,144,256]{2,1,0:T(8,128)(2,1)S(1)}, bf16[11,144,256]{2,1,0:T(8,128)(2,1)S(1)}, u32[]{:S(2)}, u32[]{:S(2)}) %collective-permute-start.16) | collective-permute-done | bytes 811040 | tf_op jit(solution)/shard_map/ppermute | solution.py:131
  113.6 2.5 %collective-permute-done.15.refs_0_.refs_5_ = bf16[11,144,256]{2,1,0:T(8,128)(2,1)S(1)} collective-permute-done((bf16[11,144,256]{2,1,0:T(8,128)(2,1)S(1)}, bf16[11,144,256]{2,1,0:T(8,128)(2,1)S(1)}, u32[]{:S(2)}, u32[]{:S(2)}) %collective-permute-start.15) | collective-permute-done | bytes 811040 | tf_op jit(solution)/shard_map/ppermute | solution.py:131
  116.2 3.2 %collective-permute-start.21 = (bf16[5,144,256]{2,1,0:T(8,128)(2,1)S(1)}, bf16[5,144,256]{2,1,0:T(8,128)(2,1)S(1)}, u32[]{:S(2)}, u32[]{:S(2)}) collective-permute-start(bf16[5,144,256]{2,1,0:T(8,128)(2,1)S(1)} %get-tuple-element.68), channel_id=1, source_target_pairs={{0,3},{1,0},{2,1},{3,2},{4,7},{5,4},{6,5},{7,6},{8,11},{9,8},{10,9... | collective-permute-start | bytes 1105928 | tf_op jit(solution)/shard_map/ppermute | solution.py:131
  119.4 4.6 %collective-permute-done.22.refs_1_ = bf16[4,32,384]{2,1,0:T(8,128)(2,1)S(1)} collective-permute-done((bf16[4,32,384]{2,1,0:T(8,128)(2,1)S(1)}, bf16[4,32,384]{2,1,0:T(8,128)(2,1)S(1)}, u32[]{:S(2)}, u32[]{:S(2)}) %collective-permute-start.22) | collective-permute-done | bytes 98336 | tf_op jit(solution)/shard_map/ppermute | solution.py:131
  125.1 1.1 collective-permute-start.25
  126.8 4.5 %output.1.refs_1_ = bf16[1536,384]{1,0:T(8,128)(2,1)} custom-call(s32[113]{0:T(128)S(1)} %concatenate.3.refs_0_, bf16[6,144,256]{2,1,0:T(8,128)(2,1)S(1)} %get-tuple-element.56.refs_1_, bf16[6,144,256]{2,1,0:T(8,128)(2,1)S(1)} %collective-permute-done.11.refs_5_.refs_2_, bf16[6,144,256]{2,1,0:T(8,128)(2,1)S(1)} %collective-permute-done.12.refs_1_.refs_3_, ...), custom_call_target="tpu_custom_call" | custom-call | flops 1000000000 | tf_op jit(solution)/shard_map/output/pallas_call | solution.py:79
  131.3 1.2 audio_sum.1
  (44 shorter events, 9.9 us)
Async XLA Ops:
  0.6 34.9 %collective-permute-start.1 = (bf16[1536,384]{1,0:T(8,128)(2,1)}, bf16[1536,384]{1,0:T(8,128)(2,1)S(1)}, u32[]{:S(2)}, u32[]{:S(2)}) collective-permute-start(bf16[1536,384]{1,0:T(8,128)(2,1)} %refs_0_.1), channel_id=1, source_target_pairs={{0,3},{1,0},{2,1},{3,2},{4,7},{5,4},{6,5},{7,6},{8,11},{9,8},{10,9... | collective-permute-start | bytes 3538952 | tf_op jit(solution)/shard_map/ppermute | solution.py:131
  3.5 32.0 %collective-permute-start = (bf16[1536,384]{1,0:T(8,128)(2,1)}, bf16[1536,384]{1,0:T(8,128)(2,1)S(1)}, u32[]{:S(2)}, u32[]{:S(2)}) collective-permute-start(bf16[1536,384]{1,0:T(8,128)(2,1)} %refs_0_.1), channel_id=1, source_target_pairs={{0,1},{1,2},{2,3},{3,0},{4,5},{5,6},{6,7},{7,4},{8,9},{9,10},{10,1... | collective-permute-start | bytes 3538952 | tf_op jit(solution)/shard_map/ppermute | solution.py:131
  3.5 32.0 %collective-permute-start.2 = (bf16[1536,384]{1,0:T(8,128)(2,1)}, bf16[1536,384]{1,0:T(8,128)(2,1)S(1)}, u32[]{:S(2)}, u32[]{:S(2)}) collective-permute-start(bf16[1536,384]{1,0:T(8,128)(2,1)} %refs_0_.1), channel_id=1, source_target_pairs={{0,4},{1,5},{2,6},{3,7},{4,0},{5,1},{6,2},{7,3},{8,12},{9,13},{10,... | collective-permute-start | bytes 3538952 | tf_op jit(solution)/shard_map/ppermute | solution.py:131
  8.1 0.7 copy-start
  35.5 27.0 %collective-permute-start.3 = (bf16[1536,384]{1,0:T(8,128)(2,1)S(1)}, bf16[1536,384]{1,0:T(8,128)(2,1)S(1)}, u32[]{:S(2)}, u32[]{:S(2)}) collective-permute-start(bf16[1536,384]{1,0:T(8,128)(2,1)S(1)} %get-tuple-element.39.refs_3_), channel_id=1, source_target_pairs={{0,1},{1,2},{2,3},{3,0},{4,5},{5,6},{6,7},{7,4},{8,9},{9,10},{10,1... | collective-permute-start | bytes 3538952 | tf_op jit(solution)/shard_map/ppermute | solution.py:131
  35.6 26.9 %collective-permute-start.5 = (bf16[1536,384]{1,0:T(8,128)(2,1)S(1)}, bf16[1536,384]{1,0:T(8,128)(2,1)S(1)}, u32[]{:S(2)}, u32[]{:S(2)}) collective-permute-start(bf16[1536,384]{1,0:T(8,128)(2,1)S(1)} %get-tuple-element.40.refs_2_), channel_id=1, source_target_pairs={{0,4},{1,5},{2,6},{3,7},{4,0},{5,1},{6,2},{7,3},{8,12},{9,13},{10,... | collective-permute-start | bytes 3538952 | tf_op jit(solution)/shard_map/ppermute | solution.py:131
  36.1 26.4 %collective-permute-start.4 = (bf16[1536,384]{1,0:T(8,128)(2,1)S(1)}, bf16[1536,384]{1,0:T(8,128)(2,1)S(1)}, u32[]{:S(2)}, u32[]{:S(2)}) collective-permute-start(bf16[1536,384]{1,0:T(8,128)(2,1)S(1)} %get-tuple-element.40.refs_2_), channel_id=1, source_target_pairs={{0,3},{1,0},{2,1},{3,2},{4,7},{5,4},{6,5},{7,6},{8,11},{9,8},{10,9... | collective-permute-start | bytes 3538952 | tf_op jit(solution)/shard_map/ppermute | solution.py:131
  39.3 11.0 %copy-start.1 = (bf16[1536,384]{1,0:T(8,128)(2,1)S(1)}, bf16[1536,384]{1,0:T(8,128)(2,1)}, u32[]{:S(2)}) copy-start(bf16[1536,384]{1,0:T(8,128)(2,1)} %refs_0_.1) | copy-start | bytes 3538948
  43.0 24.5 %collective-permute-start.10 = (bf16[48,384]{1,0:T(8,128)(2,1)S(1)}, bf16[48,384]{1,0:T(8,128)(2,1)S(1)}, u32[]{:S(2)}, u32[]{:S(2)}) collective-permute-start(bf16[48,384]{1,0:T(8,128)(2,1)S(1)} %get-tuple-element.43.refs_5_), channel_id=1, source_target_pairs={{8,0},{16,8},{24,16},{32,24},{40,32},{48,40},{56,48},{64,56},{72,6... | collective-permute-start | bytes 110600 | tf_op jit(solution)/shard_map/ppermute | solution.py:667
  44.3 23.2 %collective-permute-start.9 = (bf16[48,384]{1,0:T(8,128)(2,1)S(1)}, bf16[48,384]{1,0:T(8,128)(2,1)S(1)}, u32[]{:S(2)}, u32[]{:S(2)}) collective-permute-start(bf16[48,384]{1,0:T(8,128)(2,1)S(1)} %get-tuple-element.44.refs_6_), channel_id=1, source_target_pairs={{0,8},{8,16},{16,24},{24,32},{32,40},{40,48},{48,56},{56,64},{64,7... | collective-permute-start | bytes 110600 | tf_op jit(solution)/shard_map/ppermute | solution.py:664
  62.6 11.0 %collective-permute-start.7 = (bf16[512,384]{1,0:T(8,128)(2,1)S(1)}, bf16[512,384]{1,0:T(8,128)(2,1)S(1)}, u32[]{:S(2)}, u32[]{:S(2)}) collective-permute-start(bf16[512,384]{1,0:T(8,128)(2,1)S(1)} %get-tuple-element.47), channel_id=1, source_target_pairs={{0,4},{1,5},{2,6},{3,7},{4,0},{5,1},{6,2},{7,3},{8,12},{9,13},{10,... | collective-permute-start | bytes 1179656 | tf_op jit(solution)/shard_map/ppermute | solution.py:131
  63.7 9.9 %collective-permute-start.8 = (bf16[512,384]{1,0:T(8,128)(2,1)S(1)}, bf16[512,384]{1,0:T(8,128)(2,1)S(1)}, u32[]{:S(2)}, u32[]{:S(2)}) collective-permute-start(bf16[512,384]{1,0:T(8,128)(2,1)S(1)} %get-tuple-element.48), channel_id=1, source_target_pairs={{0,3},{1,0},{2,1},{3,2},{4,7},{5,4},{6,5},{7,6},{8,11},{9,8},{10,9... | collective-permute-start | bytes 1179656 | tf_op jit(solution)/shard_map/ppermute | solution.py:131
  67.4 9.0 %collective-permute-start.6 = (bf16[512,384]{1,0:T(8,128)(2,1)S(1)}, bf16[512,384]{1,0:T(8,128)(2,1)S(1)}, u32[]{:S(2)}, u32[]{:S(2)}) collective-permute-start(bf16[512,384]{1,0:T(8,128)(2,1)S(1)} %get-tuple-element.46.refs_5_), channel_id=1, source_target_pairs={{0,1},{1,2},{2,3},{3,0},{4,5},{5,6},{6,7},{7,4},{8,9},{9,10},{10,1... | collective-permute-start | bytes 1179656 | tf_op jit(solution)/shard_map/ppermute | solution.py:131
  68.5 23.3 %collective-permute-start.14 = (bf16[4,144,384]{2,1,0:T(8,128)(2,1)S(1)}, bf16[4,144,384]{2,1,0:T(8,128)(2,1)S(1)}, u32[]{:S(2)}, u32[]{:S(2)}) collective-permute-start(bf16[4,144,384]{2,1,0:T(8,128)(2,1)S(1)} %get-tuple-element.57), channel_id=1, source_target_pairs={{0,4},{1,5},{2,6},{3,7},{4,0},{5,1},{6,2},{7,3},{8,12},{9,13},{10,... | collective-permute-start | bytes 1327112 | tf_op jit(solution)/shard_map/ppermute | solution.py:131
  81.3 10.5 %collective-permute-start.13 = (bf16[6,144,256]{2,1,0:T(8,128)(2,1)S(1)}, bf16[6,144,256]{2,1,0:T(8,128)(2,1)S(1)}, u32[]{:S(2)}, u32[]{:S(2)}) collective-permute-start(bf16[6,144,256]{2,1,0:T(8,128)(2,1)S(1)} %get-tuple-element.56.refs_1_), channel_id=1, source_target_pairs={{0,4},{1,5},{2,6},{3,7},{4,0},{5,1},{6,2},{7,3},{8,12},{9,13},{10,... | collective-permute-start | bytes 1327112 | tf_op jit(solution)/shard_map/ppermute | solution.py:131
  81.8 10.0 %collective-permute-start.12 = (bf16[6,144,256]{2,1,0:T(8,128)(2,1)S(1)}, bf16[6,144,256]{2,1,0:T(8,128)(2,1)S(1)}, u32[]{:S(2)}, u32[]{:S(2)}) collective-permute-start(bf16[6,144,256]{2,1,0:T(8,128)(2,1)S(1)} %get-tuple-element.56.refs_1_), channel_id=1, source_target_pairs={{0,3},{1,0},{2,1},{3,2},{4,7},{5,4},{6,5},{7,6},{8,11},{9,8},{10,9... | collective-permute-start | bytes 1327112 | tf_op jit(solution)/shard_map/ppermute | solution.py:131
  82.6 12.5 %collective-permute-start.11 = (bf16[6,144,256]{2,1,0:T(8,128)(2,1)S(1)}, bf16[6,144,256]{2,1,0:T(8,128)(2,1)S(1)}, u32[]{:S(2)}, u32[]{:S(2)}) collective-permute-start(bf16[6,144,256]{2,1,0:T(8,128)(2,1)S(1)} %get-tuple-element.56.refs_1_), channel_id=1, source_target_pairs={{0,1},{1,2},{2,3},{3,0},{4,5},{5,6},{6,7},{7,4},{8,9},{9,10},{10,1... | collective-permute-start | bytes 1327112 | tf_op jit(solution)/shard_map/ppermute | solution.py:131
  95.2 18.4 %collective-permute-start.16 = (bf16[11,144,256]{2,1,0:T(8,128)(2,1)S(1)}, bf16[11,144,256]{2,1,0:T(8,128)(2,1)S(1)}, u32[]{:S(2)}, u32[]{:S(2)}) collective-permute-start(bf16[11,144,256]{2,1,0:T(8,128)(2,1)S(1)} %get-tuple-element.62), channel_id=1, source_target_pairs={{0,3},{1,0},{2,1},{3,2},{4,7},{5,4},{6,5},{7,6},{8,11},{9,8},{10,9... | collective-permute-start | bytes 2433032 | tf_op jit(solution)/shard_map/ppermute | solution.py:131
  95.6 20.5 %collective-permute-start.15 = (bf16[11,144,256]{2,1,0:T(8,128)(2,1)S(1)}, bf16[11,144,256]{2,1,0:T(8,128)(2,1)S(1)}, u32[]{:S(2)}, u32[]{:S(2)}) collective-permute-start(bf16[11,144,256]{2,1,0:T(8,128)(2,1)S(1)} %get-tuple-element.61.refs_5_), channel_id=1, source_target_pairs={{0,1},{1,2},{2,3},{3,0},{4,5},{5,6},{6,7},{7,4},{8,9},{9,10},{10,1... | collective-permute-start | bytes 2433032 | tf_op jit(solution)/shard_map/ppermute | solution.py:131
  97.3 14.4 %collective-permute-start.17 = (bf16[6,144,256]{2,1,0:T(8,128)(2,1)S(1)}, bf16[6,144,256]{2,1,0:T(8,128)(2,1)S(1)}, u32[]{:S(2)}, u32[]{:S(2)}) collective-permute-start(bf16[6,144,256]{2,1,0:T(8,128)(2,1)S(1)} %get-tuple-element.63), channel_id=1, source_target_pairs={{0,4},{1,5},{2,6},{3,7},{4,0},{5,1},{6,2},{7,3},{8,12},{9,13},{10,... | collective-permute-start | bytes 1327112 | tf_op jit(solution)/shard_map/ppermute | solution.py:131
  97.7 9.4 %collective-permute-start.18 = (f32[2,32,384]{2,1,0:T(8,128)S(1)}, f32[2,32,384]{2,1,0:T(8,128)S(1)}, u32[]{:S(2)}, u32[]{:S(2)}) collective-permute-start(f32[2,32,384]{2,1,0:T(8,128)S(1)} %get-tuple-element.65), channel_id=1, source_target_pairs={{0,8},{8,16},{16,24},{24,32},{32,40},{40,48},{48,56},{56,64},{64,7... | collective-permute-start | bytes 294920 | tf_op jit(solution)/shard_map/ppermute | solution.py:664
  102.7 8.0 %collective-permute-start.19 = (f32[2,32,384]{2,1,0:T(8,128)S(1)}, f32[2,32,384]{2,1,0:T(8,128)S(1)}, u32[]{:S(2)}, u32[]{:S(2)}) collective-permute-start(f32[2,32,384]{2,1,0:T(8,128)S(1)} %get-tuple-element.60.refs_4_), channel_id=1, source_target_pairs={{8,0},{16,8},{24,16},{32,24},{40,32},{48,40},{56,48},{64,56},{72,6... | collective-permute-start | bytes 294920 | tf_op jit(solution)/shard_map/ppermute | solution.py:667
  116.1 10.7 %collective-permute-start.20 = (bf16[5,144,256]{2,1,0:T(8,128)(2,1)S(1)}, bf16[5,144,256]{2,1,0:T(8,128)(2,1)S(1)}, u32[]{:S(2)}, u32[]{:S(2)}) collective-permute-start(bf16[5,144,256]{2,1,0:T(8,128)(2,1)S(1)} %get-tuple-element.67), channel_id=1, source_target_pairs={{0,1},{1,2},{2,3},{3,0},{4,5},{5,6},{6,7},{7,4},{8,9},{9,10},{10,1... | collective-permute-start | bytes 1105928 | tf_op jit(solution)/shard_map/ppermute | solution.py:131
  116.2 10.6 %collective-permute-start.21 = (bf16[5,144,256]{2,1,0:T(8,128)(2,1)S(1)}, bf16[5,144,256]{2,1,0:T(8,128)(2,1)S(1)}, u32[]{:S(2)}, u32[]{:S(2)}) collective-permute-start(bf16[5,144,256]{2,1,0:T(8,128)(2,1)S(1)} %get-tuple-element.68), channel_id=1, source_target_pairs={{0,3},{1,0},{2,1},{3,2},{4,7},{5,4},{6,5},{7,6},{8,11},{9,8},{10,9... | collective-permute-start | bytes 1105928 | tf_op jit(solution)/shard_map/ppermute | solution.py:131
  119.4 4.6 %collective-permute-start.22 = (bf16[4,32,384]{2,1,0:T(8,128)(2,1)S(1)}, bf16[4,32,384]{2,1,0:T(8,128)(2,1)S(1)}, u32[]{:S(2)}, u32[]{:S(2)}) collective-permute-start(bf16[4,32,384]{2,1,0:T(8,128)(2,1)S(1)} %get-tuple-element.66.refs_3_), channel_id=1, source_target_pairs={{0,4},{1,5},{2,6},{3,7},{4,0},{5,1},{6,2},{7,3},{8,12},{9,13},{10,... | collective-permute-start | bytes 294920 | tf_op jit(solution)/shard_map/ppermute | solution.py:131
  124.1 7.2 %collective-permute-start.23 = (bf16[32,384]{1,0:T(8,128)(2,1)S(1)}, bf16[32,384]{1,0:T(8,128)(2,1)S(1)}, u32[]{:S(2)}, u32[]{:S(2)}) collective-permute-start(bf16[32,384]{1,0:T(8,128)(2,1)S(1)} %get-tuple-element.71), channel_id=1, source_target_pairs={{0,3},{1,0},{2,1},{3,2},{4,7},{5,4},{6,5},{7,6},{8,11},{9,8},{10,9... | collective-permute-start | bytes 73736 | tf_op jit(solution)/shard_map/ppermute | solution.py:131
  124.2 7.2 %collective-permute-start.24 = (bf16[32,384]{1,0:T(8,128)(2,1)S(1)}, bf16[32,384]{1,0:T(8,128)(2,1)S(1)}, u32[]{:S(2)}, u32[]{:S(2)}) collective-permute-start(bf16[32,384]{1,0:T(8,128)(2,1)S(1)} %get-tuple-element.72), channel_id=1, source_target_pairs={{0,2},{1,3},{2,0},{3,1},{4,6},{5,7},{6,4},{7,5},{8,10},{9,11},{10,... | collective-permute-start | bytes 73736 | tf_op jit(solution)/shard_map/ppermute | solution.py:131
  125.1 6.3 %collective-permute-start.25 = (bf16[32,384]{1,0:T(8,128)(2,1)S(1)}, bf16[32,384]{1,0:T(8,128)(2,1)S(1)}, u32[]{:S(2)}, u32[]{:S(2)}) collective-permute-start(bf16[32,384]{1,0:T(8,128)(2,1)S(1)} %get-tuple-element.73), channel_id=1, source_target_pairs={{0,1},{1,2},{2,3},{3,0},{4,5},{5,6},{6,7},{7,4},{8,9},{9,10},{10,1... | collective-permute-start | bytes 73736 | tf_op jit(solution)/shard_map/ppermute | solution.py:131

commit v5 on v4

--- a/solution.py
+++ b/solution.py
@@ -347,13 +347,13 @@
 
 
 def merged_stats(stat, count1, block):
-    count2 = block.shape[1]
+    count = count1 + block.shape[1]
     mean1, square1 = stat[:, :1], stat[:, 1:2]
-    mean2, square2 = row_stats(block)
-    gap = mean2 - mean1
-    total = count1 + count2
-    mean = mean1 + gap * (count2 / total)
-    return mean, square1 + square2 + gap * gap * (count1 * count2 / total)
+    offset = block.astype(F32) - mean1
+    first = jnp.sum(offset, axis=-1, keepdims=True)
+    second = jnp.sum(offset * offset, axis=-1, keepdims=True)
+    shift = first / count
+    return mean1 + shift, square1 + (second - first * shift)
 
 
 def packed_stats(mean, square):
@@ -612,7 +612,7 @@
 
     for k, ref in enumerate((low_ref, high_ref)):
 
-        @pl.loop(0, half)
+        @pl.loop(0, half, unroll=True)
         def _(u, k=k, ref=ref):
             t = k * half + u
             probs = jnp.concatenate([p[t] for p in p_refs] + [ref[u]], axis=0)

time: 133 us -> 132 us (level)
  Pallas kernels: 42.3 us -> 40.9 us
    pallas_call x15, Pallas kernels: 42.3 us -> 40.9 us  [call(): pl.pallas_call(run, in_specs=[spec for spec, _ in inputs] + [ANY] * len(e...]
  transfers between devices with their start and end apart: 26 -> 26, of which waited for: 10 -> 11; matrix products, arithmetic and copies ran while one was open for 2% -> 2% of each run, Pallas kernels for 31% -> 30%
where the time goes in v5:
time: 132 us
  Pallas kernels  40.9 us (31%)
  starting transfers between devices  38 us (29%)
  waiting for transfers between devices  27.9 us (21%)
  blocking collectives  20.4 us (15%)
  local copies, waits for them, and re-layouts  3.7 us (3%)
    pallas_call x15, Pallas kernels, call(): pl.pallas_call(run, in_specs=[spec for spec, _ in inputs] + [ANY] * len(e...  40.9 us
    ppermute x22, starting transfers between devices, send(): return lax.ppermute(array, 'tensor', pairs)  24.4 us
    ppermute x22, waiting for transfers between devices, send(): return lax.ppermute(array, 'tensor', pairs)  21.1 us
    all_to_all x1, blocking collectives, shards(): audio_blocks = lax.all_to_all(audio_copies, 'tensor', 0, 0)  20.4 us
    ppermute x2, starting transfers between devices, to_next(): return lax.ppermute(array, ('tower', 'tm'), up)  11 us
    ppermute x2, waiting for transfers between devices, to_prev(): return lax.ppermute(array, ('tower', 'tm'), down)  3.61 us
    ppermute x2, waiting for transfers between devices, to_next(): return lax.ppermute(array, ('tower', 'tm'), up)  3.11 us
  transfers between devices with their start and end apart: 26, of which 11 were waited for; matrix products, arithmetic and copies ran while one was open for 2% of the time, Pallas kernels for 30%

profile of v5, /device:TPU:0, one launch (start us, length us, event | category | flops | bytes accessed | tf_op | source)
XLA Modules:
  0.0 131.7 jit_solution(5425378480836595096)
XLA Ops:
  0.6 2.9 %collective-permute-start.1 = (bf16[1536,384]{1,0:T(8,128)(2,1)}, bf16[1536,384]{1,0:T(8,128)(2,1)S(1)}, u32[]{:S(2)}, u32[]{:S(2)}) collective-permute-start(bf16[1536,384]{1,0:T(8,128)(2,1)} %refs_0_.1), channel_id=1, source_target_pairs={{0,3},{1,0},{2,1},{3,2},{4,7},{5,4},{6,5},{7,6},{8,11},{9,8},{10,9... | collective-permute-start | bytes 3538952 | tf_op jit(solution)/shard_map/ppermute | solution.py:131
  3.5 1.6 %collective-permute-start.2 = (bf16[1536,384]{1,0:T(8,128)(2,1)}, bf16[1536,384]{1,0:T(8,128)(2,1)S(1)}, u32[]{:S(2)}, u32[]{:S(2)}) collective-permute-start(bf16[1536,384]{1,0:T(8,128)(2,1)} %refs_0_.1), channel_id=1, source_target_pairs={{0,4},{1,5},{2,6},{3,7},{4,0},{5,1},{6,2},{7,3},{8,12},{9,13},{10,... | collective-permute-start | bytes 3538952 | tf_op jit(solution)/shard_map/ppermute | solution.py:131
  8.8 6.3 %prefetch.1 = (bf16[8,32,384]{2,1,0:T(8,128)(2,1)S(1)}, bf16[3072,1152]{1,0:T(8,128)(2,1)S(1)}, bf16[2,384,3072]{2,1,0:T(8,128)(2,1)S(1)}, f32[8,1152]{1,0:T(8,128)S(1)}) custom-call(s32[113]{0:T(128)S(1)} %concatenate.3.refs_0_, bf16[32,384]{1,0:T(8,128)(2,1)S(1)} %copy-done, bf16[2,3072,384]{2,1,0:T(8,128)(2,1)} %refs_1_.3, bf16[2,3072,384]{2,1,0:T(8,128)(2,1)} %refs_2_.3, ...), custom_call_target="tpu_custom_call" | custom-call | tf_op jit(solution)/shard_map/prefetch/pallas_call | solution.py:79
  15.1 20.4 %all_to_all.5.refs_3_.refs_0_ = bf16[8,32,384]{2,1,0:T(8,128)(2,1)S(1)} all-to-all(bf16[8,32,384]{2,1,0:T(8,128)(2,1)S(1)} %get-tuple-element.38), channel_id=1, replica_groups=mesh['tower'=2,'tm'=8,'tensor'=8] {'tensor'}, dimensions={0} | all-to-all | bytes 393216 | tf_op jit(solution)/shard_map/all_to_all | solution.py:691
  36.1 3.1 %collective-permute-start.4 = (bf16[1536,384]{1,0:T(8,128)(2,1)S(1)}, bf16[1536,384]{1,0:T(8,128)(2,1)S(1)}, u32[]{:S(2)}, u32[]{:S(2)}) collective-permute-start(bf16[1536,384]{1,0:T(8,128)(2,1)S(1)} %get-tuple-element.40.refs_2_), channel_id=1, source_target_pairs={{0,3},{1,0},{2,1},{3,2},{4,7},{5,4},{6,5},{7,6},{8,11},{9,8},{10,9... | collective-permute-start | bytes 3538952 | tf_op jit(solution)/shard_map/ppermute | solution.py:131
  39.3 3.7 %audio_in.1 = (bf16[96,384]{1,0:T(8,128)(2,1)S(1)}, bf16[48,384]{1,0:T(8,128)(2,1)S(1)}, bf16[48,384]{1,0:T(8,128)(2,1)S(1)}) custom-call(bf16[8,32,384]{2,1,0:T(8,128)(2,1)S(1)} %all_to_all.5.refs_3_.refs_0_, bf16[2,3072,384]{2,1,0:T(8,128)(2,1)} %refs_1_.3, bf16[2,3072,384]{2,1,0:T(8,128)(2,1)} %refs_2_.3, bf16[2,3072,384]{2,1,0:T(8,128)(2,1)} %refs_3_.3, ...), custom_call_target="tpu_custom_call" | custom-call | flops 2000000000 | tf_op jit(solution)/shard_map/audio_in/pallas_call | solution.py:79
  43.0 1.3 collective-permute-start.10
  44.3 6.1 %collective-permute-start.9 = (bf16[48,384]{1,0:T(8,128)(2,1)S(1)}, bf16[48,384]{1,0:T(8,128)(2,1)S(1)}, u32[]{:S(2)}, u32[]{:S(2)}) collective-permute-start(bf16[48,384]{1,0:T(8,128)(2,1)S(1)} %get-tuple-element.44.refs_6_), channel_id=1, source_target_pairs={{0,8},{8,16},{16,24},{24,32},{32,40},{40,48},{48,56},{56,64},{64,7... | collective-permute-start | bytes 110600 | tf_op jit(solution)/shard_map/ppermute | solution.py:664
  50.3 7.9 %first_half.1 = (f32[1536,384]{1,0:T(8,128)S(1)}, f32[1536,768]{1,0:T(8,128)S(1)}, f32[1536,128]{1,0:T(8,128)S(1)}) custom-call(bf16[1536,384]{1,0:T(8,128)(2,1)S(1)} %copy-done.1, bf16[1536,384]{1,0:T(8,128)(2,1)S(1)} %get-tuple-element.41.refs_4_.refs_1_, bf16[1536,384]{1,0:T(8,128)(2,1)S(1)} %get-tuple-element.40.refs_2_, ...), custom_call_target="tpu_custom_call" | custom-call | flops 4000000000 | tf_op jit(solution)/shard_map/first_half/pallas_call | solution.py:79
  58.2 4.3 %collective-permute-done.3.refs_0_.refs_1_ = bf16[1536,384]{1,0:T(8,128)(2,1)S(1)} collective-permute-done((bf16[1536,384]{1,0:T(8,128)(2,1)S(1)}, bf16[1536,384]{1,0:T(8,128)(2,1)S(1)}, u32[]{:S(2)}, u32[]{:S(2)}) %collective-permute-start.3) | collective-permute-done | bytes 1179680 | tf_op jit(solution)/shard_map/ppermute | solution.py:131
  62.6 1.1 collective-permute-start.7
  63.7 3.7 %collective-permute-start.8 = (bf16[512,384]{1,0:T(8,128)(2,1)S(1)}, bf16[512,384]{1,0:T(8,128)(2,1)S(1)}, u32[]{:S(2)}, u32[]{:S(2)}) collective-permute-start(bf16[512,384]{1,0:T(8,128)(2,1)S(1)} %get-tuple-element.48), channel_id=1, source_target_pairs={{0,3},{1,0},{2,1},{3,2},{4,7},{5,4},{6,5},{7,6},{8,11},{9,8},{10,9... | collective-permute-start | bytes 1179656 | tf_op jit(solution)/shard_map/ppermute | solution.py:131
  67.4 1.1 value_out.1
  69.2 3.2 %middle.1 = (f32[1536,384]{1,0:T(8,128)S(1)}, f32[1536,128]{1,0:T(8,128)S(1)}) custom-call(bf16[1536,384]{1,0:T(8,128)(2,1)S(1)} %collective-permute-done.3.refs_0_.refs_1_, bf16[1536,384]{1,0:T(8,128)(2,1)S(1)} %collective-permute-done.4.refs_1_.refs_2_, ...), custom_call_target="tpu_custom_call", output_to_operand_aliasing={{0}: (4, {}), {1}: (5, {})} | custom-call | flops 4000000000 | tf_op jit(solution)/shard_map/middle/pallas_call | solution.py:79
  72.5 1.2 collective-permute-done.7.refs_2_.refs_5_
  73.6 2.8 %collective-permute-done.6.refs_1_.refs_4_ = bf16[512,384]{1,0:T(8,128)(2,1)S(1)} collective-permute-done((bf16[512,384]{1,0:T(8,128)(2,1)S(1)}, bf16[512,384]{1,0:T(8,128)(2,1)S(1)}, u32[]{:S(2)}, u32[]{:S(2)}) %collective-permute-start.6) | collective-permute-done | bytes 393248 | tf_op jit(solution)/shard_map/ppermute | solution.py:131
  76.4 4.8 %queries_out.1 = (bf16[6,144,256]{2,1,0:T(8,128)(2,1)S(1)}, f32[1536,128]{1,0:T(8,128)S(1)}) custom-call(s32[113]{0:T(128)S(1)} %concatenate.3.refs_0_, bf16[512,384]{1,0:T(8,128)(2,1)S(1)} %collective-permute-done.6.refs_1_.refs_4_, bf16[512,384]{1,0:T(8,128)(2,1)S(1)} %collective-permute-done.7.refs_2_.refs_5_, ...), custom_call_target="tpu_custom_call", output_to_operand_aliasing={{1}: (6, {})} | custom-call | flops 2000000000 | tf_op jit(solution)/shard_map/queries_out/pallas_call | solution.py:79
  82.2 1.6 %collective-permute-start.11 = (bf16[6,144,256]{2,1,0:T(8,128)(2,1)S(1)}, bf16[6,144,256]{2,1,0:T(8,128)(2,1)S(1)}, u32[]{:S(2)}, u32[]{:S(2)}) collective-permute-start(bf16[6,144,256]{2,1,0:T(8,128)(2,1)S(1)} %get-tuple-element.56.refs_1_), channel_id=1, source_target_pairs={{0,1},{1,2},{2,3},{3,0},{4,5},{5,6},{6,7},{7,4},{8,9},{9,10},{10,1... | collective-permute-start | bytes 1327112 | tf_op jit(solution)/shard_map/ppermute | solution.py:131
  83.8 8.0 %audio_part.1 = (f32[2,32,384]{2,1,0:T(8,128)S(1)}, f32[2,32,384]{2,1,0:T(8,128)S(1)}, f32[2,32,384]{2,1,0:T(8,128)S(1)}) custom-call(s32[113]{0:T(128)S(1)} %concatenate.3.refs_0_, bf16[1536,384]{1,0:T(8,128)(2,1)S(1)} %collective-permute-done.3.refs_0_.refs_1_, bf16[1536,384]{1,0:T(8,128)(2,1)S(1)} %collective-permute-done.4.refs_1_.refs_2_, ...), custom_call_target="tpu_custom_call" | custom-call | tf_op jit(solution)/shard_map/audio_part/pallas_call | solution.py:79
  91.8 3.0 %collective-permute-done.11.refs_5_.refs_2_ = bf16[6,144,256]{2,1,0:T(8,128)(2,1)S(1)} collective-permute-done((bf16[6,144,256]{2,1,0:T(8,128)(2,1)S(1)}, bf16[6,144,256]{2,1,0:T(8,128)(2,1)S(1)}, u32[]{:S(2)}, u32[]{:S(2)}) %collective-permute-start.11) | collective-permute-done | bytes 442400 | tf_op jit(solution)/shard_map/ppermute | solution.py:131
  95.5 1.7 %collective-permute-start.15 = (bf16[11,144,256]{2,1,0:T(8,128)(2,1)S(1)}, bf16[11,144,256]{2,1,0:T(8,128)(2,1)S(1)}, u32[]{:S(2)}, u32[]{:S(2)}) collective-permute-start(bf16[11,144,256]{2,1,0:T(8,128)(2,1)S(1)} %get-tuple-element.61.refs_5_), channel_id=1, source_target_pairs={{0,1},{1,2},{2,3},{3,0},{4,5},{5,6},{6,7},{7,4},{8,9},{9,10},{10,1... | collective-permute-start | bytes 2433032 | tf_op jit(solution)/shard_map/ppermute | solution.py:131
  97.6 5.0 %collective-permute-start.18 = (f32[2,32,384]{2,1,0:T(8,128)S(1)}, f32[2,32,384]{2,1,0:T(8,128)S(1)}, u32[]{:S(2)}, u32[]{:S(2)}) collective-permute-start(f32[2,32,384]{2,1,0:T(8,128)S(1)} %get-tuple-element.65), channel_id=1, source_target_pairs={{0,8},{8,16},{16,24},{24,32},{32,40},{40,48},{48,56},{56,64},{64,7... | collective-permute-start | bytes 294920 | tf_op jit(solution)/shard_map/ppermute | solution.py:664
  102.6 1.3 collective-permute-start.19
  103.9 3.1 %collective-permute-done.18.refs_2_ = f32[2,32,384]{2,1,0:T(8,128)S(1)} collective-permute-done((f32[2,32,384]{2,1,0:T(8,128)S(1)}, f32[2,32,384]{2,1,0:T(8,128)S(1)}, u32[]{:S(2)}, u32[]{:S(2)}) %collective-permute-start.18) | collective-permute-done | bytes 98336 | tf_op jit(solution)/shard_map/ppermute | solution.py:664
  107.0 3.6 %collective-permute-done.19.refs_3_ = f32[2,32,384]{2,1,0:T(8,128)S(1)} collective-permute-done((f32[2,32,384]{2,1,0:T(8,128)S(1)}, f32[2,32,384]{2,1,0:T(8,128)S(1)}, u32[]{:S(2)}, u32[]{:S(2)}) %collective-permute-start.19) | collective-permute-done | bytes 98336 | tf_op jit(solution)/shard_map/ppermute | solution.py:667
  111.6 1.9 %collective-permute-done.16.refs_1_.refs_6_ = bf16[11,144,256]{2,1,0:T(8,128)(2,1)S(1)} collective-permute-done((bf16[11,144,256]{2,1,0:T(8,128)(2,1)S(1)}, bf16[11,144,256]{2,1,0:T(8,128)(2,1)S(1)}, u32[]{:S(2)}, u32[]{:S(2)}) %collective-permute-start.16) | collective-permute-done | bytes 811040 | tf_op jit(solution)/shard_map/ppermute | solution.py:131
  113.5 2.5 %collective-permute-done.15.refs_0_.refs_5_ = bf16[11,144,256]{2,1,0:T(8,128)(2,1)S(1)} collective-permute-done((bf16[11,144,256]{2,1,0:T(8,128)(2,1)S(1)}, bf16[11,144,256]{2,1,0:T(8,128)(2,1)S(1)}, u32[]{:S(2)}, u32[]{:S(2)}) %collective-permute-start.15) | collective-permute-done | bytes 811040 | tf_op jit(solution)/shard_map/ppermute | solution.py:131
  116.1 3.2 %collective-permute-start.21 = (bf16[5,144,256]{2,1,0:T(8,128)(2,1)S(1)}, bf16[5,144,256]{2,1,0:T(8,128)(2,1)S(1)}, u32[]{:S(2)}, u32[]{:S(2)}) collective-permute-start(bf16[5,144,256]{2,1,0:T(8,128)(2,1)S(1)} %get-tuple-element.68), channel_id=1, source_target_pairs={{0,3},{1,0},{2,1},{3,2},{4,7},{5,4},{6,5},{7,6},{8,11},{9,8},{10,9... | collective-permute-start | bytes 1105928 | tf_op jit(solution)/shard_map/ppermute | solution.py:131
  119.3 4.6 %collective-permute-done.22.refs_1_ = bf16[4,32,384]{2,1,0:T(8,128)(2,1)S(1)} collective-permute-done((bf16[4,32,384]{2,1,0:T(8,128)(2,1)S(1)}, bf16[4,32,384]{2,1,0:T(8,128)(2,1)S(1)}, u32[]{:S(2)}, u32[]{:S(2)}) %collective-permute-start.22) | collective-permute-done | bytes 98336 | tf_op jit(solution)/shard_map/ppermute | solution.py:131
  125.0 1.1 collective-permute-start.25
  126.7 3.5 %output.1.refs_1_ = bf16[1536,384]{1,0:T(8,128)(2,1)} custom-call(s32[113]{0:T(128)S(1)} %concatenate.3.refs_0_, bf16[6,144,256]{2,1,0:T(8,128)(2,1)S(1)} %get-tuple-element.56.refs_1_, bf16[6,144,256]{2,1,0:T(8,128)(2,1)S(1)} %collective-permute-done.11.refs_5_.refs_2_, bf16[6,144,256]{2,1,0:T(8,128)(2,1)S(1)} %collective-permute-done.12.refs_1_.refs_3_, ...), custom_call_target="tpu_custom_call" | custom-call | flops 1000000000 | tf_op jit(solution)/shard_map/output/pallas_call | solution.py:79
  130.5 1.2 audio_sum.1
  (44 shorter events, 10.4 us)
Async XLA Ops:
  0.6 34.9 %collective-permute-start.1 = (bf16[1536,384]{1,0:T(8,128)(2,1)}, bf16[1536,384]{1,0:T(8,128)(2,1)S(1)}, u32[]{:S(2)}, u32[]{:S(2)}) collective-permute-start(bf16[1536,384]{1,0:T(8,128)(2,1)} %refs_0_.1), channel_id=1, source_target_pairs={{0,3},{1,0},{2,1},{3,2},{4,7},{5,4},{6,5},{7,6},{8,11},{9,8},{10,9... | collective-permute-start | bytes 3538952 | tf_op jit(solution)/shard_map/ppermute | solution.py:131
  3.5 32.0 %collective-permute-start = (bf16[1536,384]{1,0:T(8,128)(2,1)}, bf16[1536,384]{1,0:T(8,128)(2,1)S(1)}, u32[]{:S(2)}, u32[]{:S(2)}) collective-permute-start(bf16[1536,384]{1,0:T(8,128)(2,1)} %refs_0_.1), channel_id=1, source_target_pairs={{0,1},{1,2},{2,3},{3,0},{4,5},{5,6},{6,7},{7,4},{8,9},{9,10},{10,1... | collective-permute-start | bytes 3538952 | tf_op jit(solution)/shard_map/ppermute | solution.py:131
  3.5 32.0 %collective-permute-start.2 = (bf16[1536,384]{1,0:T(8,128)(2,1)}, bf16[1536,384]{1,0:T(8,128)(2,1)S(1)}, u32[]{:S(2)}, u32[]{:S(2)}) collective-permute-start(bf16[1536,384]{1,0:T(8,128)(2,1)} %refs_0_.1), channel_id=1, source_target_pairs={{0,4},{1,5},{2,6},{3,7},{4,0},{5,1},{6,2},{7,3},{8,12},{9,13},{10,... | collective-permute-start | bytes 3538952 | tf_op jit(solution)/shard_map/ppermute | solution.py:131
  8.1 0.7 copy-start
  35.5 27.0 %collective-permute-start.3 = (bf16[1536,384]{1,0:T(8,128)(2,1)S(1)}, bf16[1536,384]{1,0:T(8,128)(2,1)S(1)}, u32[]{:S(2)}, u32[]{:S(2)}) collective-permute-start(bf16[1536,384]{1,0:T(8,128)(2,1)S(1)} %get-tuple-element.39.refs_3_), channel_id=1, source_target_pairs={{0,1},{1,2},{2,3},{3,0},{4,5},{5,6},{6,7},{7,4},{8,9},{9,10},{10,1... | collective-permute-start | bytes 3538952 | tf_op jit(solution)/shard_map/ppermute | solution.py:131
  35.6 26.9 %collective-permute-start.5 = (bf16[1536,384]{1,0:T(8,128)(2,1)S(1)}, bf16[1536,384]{1,0:T(8,128)(2,1)S(1)}, u32[]{:S(2)}, u32[]{:S(2)}) collective-permute-start(bf16[1536,384]{1,0:T(8,128)(2,1)S(1)} %get-tuple-element.40.refs_2_), channel_id=1, source_target_pairs={{0,4},{1,5},{2,6},{3,7},{4,0},{5,1},{6,2},{7,3},{8,12},{9,13},{10,... | collective-permute-start | bytes 3538952 | tf_op jit(solution)/shard_map/ppermute | solution.py:131
  36.1 26.4 %collective-permute-start.4 = (bf16[1536,384]{1,0:T(8,128)(2,1)S(1)}, bf16[1536,384]{1,0:T(8,128)(2,1)S(1)}, u32[]{:S(2)}, u32[]{:S(2)}) collective-permute-start(bf16[1536,384]{1,0:T(8,128)(2,1)S(1)} %get-tuple-element.40.refs_2_), channel_id=1, source_target_pairs={{0,3},{1,0},{2,1},{3,2},{4,7},{5,4},{6,5},{7,6},{8,11},{9,8},{10,9... | collective-permute-start | bytes 3538952 | tf_op jit(solution)/shard_map/ppermute | solution.py:131
  39.3 11.0 %copy-start.1 = (bf16[1536,384]{1,0:T(8,128)(2,1)S(1)}, bf16[1536,384]{1,0:T(8,128)(2,1)}, u32[]{:S(2)}) copy-start(bf16[1536,384]{1,0:T(8,128)(2,1)} %refs_0_.1) | copy-start | bytes 3538948
  43.0 24.5 %collective-permute-start.10 = (bf16[48,384]{1,0:T(8,128)(2,1)S(1)}, bf16[48,384]{1,0:T(8,128)(2,1)S(1)}, u32[]{:S(2)}, u32[]{:S(2)}) collective-permute-start(bf16[48,384]{1,0:T(8,128)(2,1)S(1)} %get-tuple-element.43.refs_5_), channel_id=1, source_target_pairs={{8,0},{16,8},{24,16},{32,24},{40,32},{48,40},{56,48},{64,56},{72,6... | collective-permute-start | bytes 110600 | tf_op jit(solution)/shard_map/ppermute | solution.py:667
  44.3 23.2 %collective-permute-start.9 = (bf16[48,384]{1,0:T(8,128)(2,1)S(1)}, bf16[48,384]{1,0:T(8,128)(2,1)S(1)}, u32[]{:S(2)}, u32[]{:S(2)}) collective-permute-start(bf16[48,384]{1,0:T(8,128)(2,1)S(1)} %get-tuple-element.44.refs_6_), channel_id=1, source_target_pairs={{0,8},{8,16},{16,24},{24,32},{32,40},{40,48},{48,56},{56,64},{64,7... | collective-permute-start | bytes 110600 | tf_op jit(solution)/shard_map/ppermute | solution.py:664
  62.6 11.0 %collective-permute-start.7 = (bf16[512,384]{1,0:T(8,128)(2,1)S(1)}, bf16[512,384]{1,0:T(8,128)(2,1)S(1)}, u32[]{:S(2)}, u32[]{:S(2)}) collective-permute-start(bf16[512,384]{1,0:T(8,128)(2,1)S(1)} %get-tuple-element.47), channel_id=1, source_target_pairs={{0,4},{1,5},{2,6},{3,7},{4,0},{5,1},{6,2},{7,3},{8,12},{9,13},{10,... | collective-permute-start | bytes 1179656 | tf_op jit(solution)/shard_map/ppermute | solution.py:131
  63.7 9.9 %collective-permute-start.8 = (bf16[512,384]{1,0:T(8,128)(2,1)S(1)}, bf16[512,384]{1,0:T(8,128)(2,1)S(1)}, u32[]{:S(2)}, u32[]{:S(2)}) collective-permute-start(bf16[512,384]{1,0:T(8,128)(2,1)S(1)} %get-tuple-element.48), channel_id=1, source_target_pairs={{0,3},{1,0},{2,1},{3,2},{4,7},{5,4},{6,5},{7,6},{8,11},{9,8},{10,9... | collective-permute-start | bytes 1179656 | tf_op jit(solution)/shard_map/ppermute | solution.py:131
  67.4 9.0 %collective-permute-start.6 = (bf16[512,384]{1,0:T(8,128)(2,1)S(1)}, bf16[512,384]{1,0:T(8,128)(2,1)S(1)}, u32[]{:S(2)}, u32[]{:S(2)}) collective-permute-start(bf16[512,384]{1,0:T(8,128)(2,1)S(1)} %get-tuple-element.46.refs_5_), channel_id=1, source_target_pairs={{0,1},{1,2},{2,3},{3,0},{4,5},{5,6},{6,7},{7,4},{8,9},{9,10},{10,1... | collective-permute-start | bytes 1179656 | tf_op jit(solution)/shard_map/ppermute | solution.py:131
  68.5 23.2 %collective-permute-start.14 = (bf16[4,144,384]{2,1,0:T(8,128)(2,1)S(1)}, bf16[4,144,384]{2,1,0:T(8,128)(2,1)S(1)}, u32[]{:S(2)}, u32[]{:S(2)}) collective-permute-start(bf16[4,144,384]{2,1,0:T(8,128)(2,1)S(1)} %get-tuple-element.57), channel_id=1, source_target_pairs={{0,4},{1,5},{2,6},{3,7},{4,0},{5,1},{6,2},{7,3},{8,12},{9,13},{10,... | collective-permute-start | bytes 1327112 | tf_op jit(solution)/shard_map/ppermute | solution.py:131
  81.2 10.6 %collective-permute-start.13 = (bf16[6,144,256]{2,1,0:T(8,128)(2,1)S(1)}, bf16[6,144,256]{2,1,0:T(8,128)(2,1)S(1)}, u32[]{:S(2)}, u32[]{:S(2)}) collective-permute-start(bf16[6,144,256]{2,1,0:T(8,128)(2,1)S(1)} %get-tuple-element.56.refs_1_), channel_id=1, source_target_pairs={{0,4},{1,5},{2,6},{3,7},{4,0},{5,1},{6,2},{7,3},{8,12},{9,13},{10,... | collective-permute-start | bytes 1327112 | tf_op jit(solution)/shard_map/ppermute | solution.py:131
  81.8 10.0 %collective-permute-start.12 = (bf16[6,144,256]{2,1,0:T(8,128)(2,1)S(1)}, bf16[6,144,256]{2,1,0:T(8,128)(2,1)S(1)}, u32[]{:S(2)}, u32[]{:S(2)}) collective-permute-start(bf16[6,144,256]{2,1,0:T(8,128)(2,1)S(1)} %get-tuple-element.56.refs_1_), channel_id=1, source_target_pairs={{0,3},{1,0},{2,1},{3,2},{4,7},{5,4},{6,5},{7,6},{8,11},{9,8},{10,9... | collective-permute-start | bytes 1327112 | tf_op jit(solution)/shard_map/ppermute | solution.py:131
  82.2 12.5 %collective-permute-start.11 = (bf16[6,144,256]{2,1,0:T(8,128)(2,1)S(1)}, bf16[6,144,256]{2,1,0:T(8,128)(2,1)S(1)}, u32[]{:S(2)}, u32[]{:S(2)}) collective-permute-start(bf16[6,144,256]{2,1,0:T(8,128)(2,1)S(1)} %get-tuple-element.56.refs_1_), channel_id=1, source_target_pairs={{0,1},{1,2},{2,3},{3,0},{4,5},{5,6},{6,7},{7,4},{8,9},{9,10},{10,1... | collective-permute-start | bytes 1327112 | tf_op jit(solution)/shard_map/ppermute | solution.py:131
  94.9 18.6 %collective-permute-start.16 = (bf16[11,144,256]{2,1,0:T(8,128)(2,1)S(1)}, bf16[11,144,256]{2,1,0:T(8,128)(2,1)S(1)}, u32[]{:S(2)}, u32[]{:S(2)}) collective-permute-start(bf16[11,144,256]{2,1,0:T(8,128)(2,1)S(1)} %get-tuple-element.62), channel_id=1, source_target_pairs={{0,3},{1,0},{2,1},{3,2},{4,7},{5,4},{6,5},{7,6},{8,11},{9,8},{10,9... | collective-permute-start | bytes 2433032 | tf_op jit(solution)/shard_map/ppermute | solution.py:131
  95.5 20.5 %collective-permute-start.15 = (bf16[11,144,256]{2,1,0:T(8,128)(2,1)S(1)}, bf16[11,144,256]{2,1,0:T(8,128)(2,1)S(1)}, u32[]{:S(2)}, u32[]{:S(2)}) collective-permute-start(bf16[11,144,256]{2,1,0:T(8,128)(2,1)S(1)} %get-tuple-element.61.refs_5_), channel_id=1, source_target_pairs={{0,1},{1,2},{2,3},{3,0},{4,5},{5,6},{6,7},{7,4},{8,9},{9,10},{10,1... | collective-permute-start | bytes 2433032 | tf_op jit(solution)/shard_map/ppermute | solution.py:131
  97.2 14.4 %collective-permute-start.17 = (bf16[6,144,256]{2,1,0:T(8,128)(2,1)S(1)}, bf16[6,144,256]{2,1,0:T(8,128)(2,1)S(1)}, u32[]{:S(2)}, u32[]{:S(2)}) collective-permute-start(bf16[6,144,256]{2,1,0:T(8,128)(2,1)S(1)} %get-tuple-element.63), channel_id=1, source_target_pairs={{0,4},{1,5},{2,6},{3,7},{4,0},{5,1},{6,2},{7,3},{8,12},{9,13},{10,... | collective-permute-start | bytes 1327112 | tf_op jit(solution)/shard_map/ppermute | solution.py:131
  97.6 9.4 %collective-permute-start.18 = (f32[2,32,384]{2,1,0:T(8,128)S(1)}, f32[2,32,384]{2,1,0:T(8,128)S(1)}, u32[]{:S(2)}, u32[]{:S(2)}) collective-permute-start(f32[2,32,384]{2,1,0:T(8,128)S(1)} %get-tuple-element.65), channel_id=1, source_target_pairs={{0,8},{8,16},{16,24},{24,32},{32,40},{40,48},{48,56},{56,64},{64,7... | collective-permute-start | bytes 294920 | tf_op jit(solution)/shard_map/ppermute | solution.py:664
  102.6 8.0 %collective-permute-start.19 = (f32[2,32,384]{2,1,0:T(8,128)S(1)}, f32[2,32,384]{2,1,0:T(8,128)S(1)}, u32[]{:S(2)}, u32[]{:S(2)}) collective-permute-start(f32[2,32,384]{2,1,0:T(8,128)S(1)} %get-tuple-element.60.refs_4_), channel_id=1, source_target_pairs={{8,0},{16,8},{24,16},{32,24},{40,32},{48,40},{56,48},{64,56},{72,6... | collective-permute-start | bytes 294920 | tf_op jit(solution)/shard_map/ppermute | solution.py:667
  116.0 10.7 %collective-permute-start.20 = (bf16[5,144,256]{2,1,0:T(8,128)(2,1)S(1)}, bf16[5,144,256]{2,1,0:T(8,128)(2,1)S(1)}, u32[]{:S(2)}, u32[]{:S(2)}) collective-permute-start(bf16[5,144,256]{2,1,0:T(8,128)(2,1)S(1)} %get-tuple-element.67), channel_id=1, source_target_pairs={{0,1},{1,2},{2,3},{3,0},{4,5},{5,6},{6,7},{7,4},{8,9},{9,10},{10,1... | collective-permute-start | bytes 1105928 | tf_op jit(solution)/shard_map/ppermute | solution.py:131
  116.1 10.6 %collective-permute-start.21 = (bf16[5,144,256]{2,1,0:T(8,128)(2,1)S(1)}, bf16[5,144,256]{2,1,0:T(8,128)(2,1)S(1)}, u32[]{:S(2)}, u32[]{:S(2)}) collective-permute-start(bf16[5,144,256]{2,1,0:T(8,128)(2,1)S(1)} %get-tuple-element.68), channel_id=1, source_target_pairs={{0,3},{1,0},{2,1},{3,2},{4,7},{5,4},{6,5},{7,6},{8,11},{9,8},{10,9... | collective-permute-start | bytes 1105928 | tf_op jit(solution)/shard_map/ppermute | solution.py:131
  119.3 4.6 %collective-permute-start.22 = (bf16[4,32,384]{2,1,0:T(8,128)(2,1)S(1)}, bf16[4,32,384]{2,1,0:T(8,128)(2,1)S(1)}, u32[]{:S(2)}, u32[]{:S(2)}) collective-permute-start(bf16[4,32,384]{2,1,0:T(8,128)(2,1)S(1)} %get-tuple-element.66.refs_3_), channel_id=1, source_target_pairs={{0,4},{1,5},{2,6},{3,7},{4,0},{5,1},{6,2},{7,3},{8,12},{9,13},{10,... | collective-permute-start | bytes 294920 | tf_op jit(solution)/shard_map/ppermute | solution.py:131
  124.0 6.2 %collective-permute-start.23 = (bf16[32,384]{1,0:T(8,128)(2,1)S(1)}, bf16[32,384]{1,0:T(8,128)(2,1)S(1)}, u32[]{:S(2)}, u32[]{:S(2)}) collective-permute-start(bf16[32,384]{1,0:T(8,128)(2,1)S(1)} %get-tuple-element.71), channel_id=1, source_target_pairs={{0,3},{1,0},{2,1},{3,2},{4,7},{5,4},{6,5},{7,6},{8,11},{9,8},{10,9... | collective-permute-start | bytes 73736 | tf_op jit(solution)/shard_map/ppermute | solution.py:131
  124.0 6.1 %collective-permute-start.24 = (bf16[32,384]{1,0:T(8,128)(2,1)S(1)}, bf16[32,384]{1,0:T(8,128)(2,1)S(1)}, u32[]{:S(2)}, u32[]{:S(2)}) collective-permute-start(bf16[32,384]{1,0:T(8,128)(2,1)S(1)} %get-tuple-element.72), channel_id=1, source_target_pairs={{0,2},{1,3},{2,0},{3,1},{4,6},{5,7},{6,4},{7,5},{8,10},{9,11},{10,... | collective-permute-start | bytes 73736 | tf_op jit(solution)/shard_map/ppermute | solution.py:131
  125.0 5.6 %collective-permute-start.25 = (bf16[32,384]{1,0:T(8,128)(2,1)S(1)}, bf16[32,384]{1,0:T(8,128)(2,1)S(1)}, u32[]{:S(2)}, u32[]{:S(2)}) collective-permute-start(bf16[32,384]{1,0:T(8,128)(2,1)S(1)} %get-tuple-element.73), channel_id=1, source_target_pairs={{0,1},{1,2},{2,3},{3,0},{4,5},{5,6},{6,7},{7,4},{8,9},{9,10},{10,1... | collective-permute-start | bytes 73736 | tf_op jit(solution)/shard_map/ppermute | solution.py:131

commit v6 on v5

--- a/solution.py
+++ b/solution.py
@@ -455,12 +455,14 @@
         stat[rows, :] = packed_stats(mean, var)
         total = acc[rows, :] + dot(block, w_ref[LAST, :GROUP]) - mean * sums
         floor = EPS * (var + EPS)
+        place = t * TILE + lax.broadcasted_iota(jnp.int32, (1, TILE), 1)
+        valid = place < meta_ref[AT_VIDEO + shard]
         for h in range(HEADS_DEV):
             cols = slice(h * HEAD, (h + 1) * HEAD)
             scores = dot_nt(keys[:, cols], head_norm(total[:, cols], floor))
             weights = jnp.where(used, jnp.exp2(scores * SCALE), 0.0)
-            below = jnp.sum(weights, axis=0, keepdims=True)
-            pt_ref[t, h * SPAN : (h + 1) * SPAN, :] = (weights * (1.0 / below)).astype(BF16)
+            share = jnp.where(valid, 1.0 / jnp.sum(weights, axis=0, keepdims=True), 0.0)
+            pt_ref[t, h * SPAN : (h + 1) * SPAN, :] = (weights * share).astype(BF16)
 
     by_thirds(body, (xa, xb, xc))
 
@@ -533,7 +535,9 @@
 
 def audio_out_kernel(meta_ref, own_ref, prev_ref, next_ref, w_ref, keep_ref, give_ref):
     total = own_ref[...] + prev_ref[...] + next_ref[...]
-    attended = (total[0] / total[1]).astype(BF16)
+    row = lax.broadcasted_iota(jnp.int32, (AUD, 1), 0)
+    valid = row < meta_ref[AT_AUDIO + meta_ref[AT_SHARD]]
+    attended = jnp.where(valid, total[0] / total[1], 0.0).astype(BF16)
     for j, (dy, dx) in enumerate(OFFSETS):
         product = dot(attended, w_ref[1, :, dest_cols(meta_ref, j)]).astype(BF16)
         (give_ref if dy else keep_ref)[dx] = product
@@ -567,26 +571,23 @@
     )
 
 
-def audio_sum_kernel(meta_ref, done_ref, *refs):
-    total = sum(ref[...].astype(F32) for ref in refs[:4])
-    row = lax.broadcasted_iota(jnp.int32, (AUD, 1), 0)
-    valid = row < meta_ref[AT_AUDIO + meta_ref[AT_SHARD]]
-    refs[4][...] = jnp.where(valid, total, 0.0).astype(BF16)
-
-
-def audio_sum(meta, received, done):
+def audio_sum_kernel(done_ref, *refs):
+    refs[4][...] = sum(ref[...].astype(F32) for ref in refs[:4]).astype(BF16)
+
+
+def audio_sum(received, done):
     (out,) = call(
         audio_sum_kernel,
         "audio_sum",
         0,
-        [(SMEM, meta), (HBM, done)] + [(VMEM, a) for a in received],
+        [(HBM, done)] + [(VMEM, a) for a in received],
         (),
         [sds((AUD, GROUP), BF16)],
     )
     return out
 
 
-def output_kernel(meta_ref, *refs):
+def output_kernel(*refs):
     p_refs, (low_ref, high_ref, keep, got, out_ref, projected, out, sems) = refs[:7], refs[7:]
     half = TILES // 2
 
@@ -605,7 +606,6 @@
     )
     for j, block in enumerate(blocks):
         projected[j * KEYS : (j + 1) * KEYS, :] = block
-    limit = meta_ref[AT_VIDEO + meta_ref[AT_SHARD]]
 
     def copy(t):
         return pltpu.make_async_copy(out.at[rows_of(t), :], out_ref.at[rows_of(t), :], sems.at[t])
@@ -617,20 +617,19 @@
             t = k * half + u
             probs = jnp.concatenate([p[t] for p in p_refs] + [ref[u]], axis=0)
             result = dot_tn(probs, projected[...])
-            row = t * TILE + lax.broadcasted_iota(jnp.int32, (TILE, 1), 0)
-            out[rows_of(t), :] = jnp.where(row < limit, result, 0.0).astype(BF16)
+            out[rows_of(t), :] = result.astype(BF16)
             copy(t).start()
 
     for t in range(TILES):
         copy(t).wait()
 
 
-def output(meta, probs, low, high, keep, got, *extra):
+def output(probs, low, high, keep, got, *extra):
     (out,) = call(
         output_kernel,
         "output",
         1,
-        [(SMEM, meta)] + [(VMEM, a) for a in (*probs, low, high, keep, got)],
+        [(VMEM, a) for a in (*probs, low, high, keep, got)],
         (),
         [sds((VID, GROUP), BF16)],
         [
@@ -720,9 +719,9 @@
     pairs = audio_pair(keep, across(give))
     received = [pairs[0]] + [send(pairs[dx], 0, -dx) for dx in range(1, 4)]
     video_update = output(
-        meta, (probs, pl_, pr_, py_, pyl, pq, pyr), low, high, keep_v, got_v, pairs[0]
-    )
-    audio_update = audio_sum(meta, received, video_update)
+        (probs, pl_, pr_, py_, pyl, pq, pyr), low, high, keep_v, got_v, pairs[0]
+    )
+    audio_update = audio_sum(received, video_update)
     return (video_update, audio_update)
 
 

time: 132 us -> 131 us (level)
  no operation moved by 1% of the time
where the time goes in v6:
time: 131 us
  Pallas kernels  39.8 us (30%)
  starting transfers between devices  37.9 us (29%)
  waiting for transfers between devices  28.4 us (22%)
  blocking collectives  20.4 us (16%)
  local copies, waits for them, and re-layouts  3.7 us (3%)
    pallas_call x15, Pallas kernels, call(): pl.pallas_call(run, in_specs=[spec for spec, _ in inputs] + [ANY] * len(e...  39.8 us
    ppermute x22, starting transfers between devices, send(): return lax.ppermute(array, 'tensor', pairs)  24.3 us
    ppermute x22, waiting for transfers between devices, send(): return lax.ppermute(array, 'tensor', pairs)  21.7 us
    all_to_all x1, blocking collectives, shards(): audio_blocks = lax.all_to_all(audio_copies, 'tensor', 0, 0)  20.4 us
    ppermute x2, starting transfers between devices, to_next(): return lax.ppermute(array, ('tower', 'tm'), up)  11 us
    ppermute x2, waiting for transfers between devices, to_prev(): return lax.ppermute(array, ('tower', 'tm'), down)  3.6 us
    ppermute x2, waiting for transfers between devices, to_next(): return lax.ppermute(array, ('tower', 'tm'), up)  3.11 us
  transfers between devices with their start and end apart: 26, of which 11 were waited for; matrix products, arithmetic and copies ran while one was open for 2% of the time, Pallas kernels for 30%

profile of v6, /device:TPU:0, one launch (start us, length us, event | category | flops | bytes accessed | tf_op | source)
XLA Modules:
  0.0 131.1 jit_solution(5992849764354883187)
XLA Ops:
  0.6 2.9 %collective-permute-start.1 = (bf16[1536,384]{1,0:T(8,128)(2,1)}, bf16[1536,384]{1,0:T(8,128)(2,1)S(1)}, u32[]{:S(2)}, u32[]{:S(2)}) collective-permute-start(bf16[1536,384]{1,0:T(8,128)(2,1)} %refs_0_.1), channel_id=1, source_target_pairs={{0,3},{1,0},{2,1},{3,2},{4,7},{5,4},{6,5},{7,6},{8,11},{9,8},{10,9... | collective-permute-start | bytes 3538952 | tf_op jit(solution)/shard_map/ppermute | solution.py:131
  3.5 1.6 %collective-permute-start.2 = (bf16[1536,384]{1,0:T(8,128)(2,1)}, bf16[1536,384]{1,0:T(8,128)(2,1)S(1)}, u32[]{:S(2)}, u32[]{:S(2)}) collective-permute-start(bf16[1536,384]{1,0:T(8,128)(2,1)} %refs_0_.1), channel_id=1, source_target_pairs={{0,4},{1,5},{2,6},{3,7},{4,0},{5,1},{6,2},{7,3},{8,12},{9,13},{10,... | collective-permute-start | bytes 3538952 | tf_op jit(solution)/shard_map/ppermute | solution.py:131
  8.8 6.3 %prefetch.1 = (bf16[8,32,384]{2,1,0:T(8,128)(2,1)S(1)}, bf16[3072,1152]{1,0:T(8,128)(2,1)S(1)}, bf16[2,384,3072]{2,1,0:T(8,128)(2,1)S(1)}, f32[8,1152]{1,0:T(8,128)S(1)}) custom-call(s32[113]{0:T(128)S(1)} %concatenate.3.refs_0_, bf16[32,384]{1,0:T(8,128)(2,1)S(1)} %copy-done, bf16[2,3072,384]{2,1,0:T(8,128)(2,1)} %refs_1_.3, bf16[2,3072,384]{2,1,0:T(8,128)(2,1)} %refs_2_.3, ...), custom_call_target="tpu_custom_call" | custom-call | tf_op jit(solution)/shard_map/prefetch/pallas_call | solution.py:79
  15.1 20.4 %all_to_all.5.refs_3_.refs_0_ = bf16[8,32,384]{2,1,0:T(8,128)(2,1)S(1)} all-to-all(bf16[8,32,384]{2,1,0:T(8,128)(2,1)S(1)} %get-tuple-element.38), channel_id=1, replica_groups=mesh['tower'=2,'tm'=8,'tensor'=8] {'tensor'}, dimensions={0} | all-to-all | bytes 393216 | tf_op jit(solution)/shard_map/all_to_all | solution.py:690
  36.1 3.1 %collective-permute-start.4 = (bf16[1536,384]{1,0:T(8,128)(2,1)S(1)}, bf16[1536,384]{1,0:T(8,128)(2,1)S(1)}, u32[]{:S(2)}, u32[]{:S(2)}) collective-permute-start(bf16[1536,384]{1,0:T(8,128)(2,1)S(1)} %get-tuple-element.40.refs_2_), channel_id=1, source_target_pairs={{0,3},{1,0},{2,1},{3,2},{4,7},{5,4},{6,5},{7,6},{8,11},{9,8},{10,9... | collective-permute-start | bytes 3538952 | tf_op jit(solution)/shard_map/ppermute | solution.py:131
  39.3 3.7 %audio_in.1 = (bf16[96,384]{1,0:T(8,128)(2,1)S(1)}, bf16[48,384]{1,0:T(8,128)(2,1)S(1)}, bf16[48,384]{1,0:T(8,128)(2,1)S(1)}) custom-call(bf16[8,32,384]{2,1,0:T(8,128)(2,1)S(1)} %all_to_all.5.refs_3_.refs_0_, bf16[2,3072,384]{2,1,0:T(8,128)(2,1)} %refs_1_.3, bf16[2,3072,384]{2,1,0:T(8,128)(2,1)} %refs_2_.3, bf16[2,3072,384]{2,1,0:T(8,128)(2,1)} %refs_3_.3, ...), custom_call_target="tpu_custom_call" | custom-call | flops 2000000000 | tf_op jit(solution)/shard_map/audio_in/pallas_call | solution.py:79
  43.0 1.3 collective-permute-start.10
  44.3 6.1 %collective-permute-start.9 = (bf16[48,384]{1,0:T(8,128)(2,1)S(1)}, bf16[48,384]{1,0:T(8,128)(2,1)S(1)}, u32[]{:S(2)}, u32[]{:S(2)}) collective-permute-start(bf16[48,384]{1,0:T(8,128)(2,1)S(1)} %get-tuple-element.44.refs_6_), channel_id=1, source_target_pairs={{0,8},{8,16},{16,24},{24,32},{32,40},{40,48},{48,56},{56,64},{64,7... | collective-permute-start | bytes 110600 | tf_op jit(solution)/shard_map/ppermute | solution.py:663
  50.3 7.9 %first_half.1 = (f32[1536,384]{1,0:T(8,128)S(1)}, f32[1536,768]{1,0:T(8,128)S(1)}, f32[1536,128]{1,0:T(8,128)S(1)}) custom-call(bf16[1536,384]{1,0:T(8,128)(2,1)S(1)} %copy-done.1, bf16[1536,384]{1,0:T(8,128)(2,1)S(1)} %get-tuple-element.41.refs_4_.refs_1_, bf16[1536,384]{1,0:T(8,128)(2,1)S(1)} %get-tuple-element.40.refs_2_, ...), custom_call_target="tpu_custom_call" | custom-call | flops 4000000000 | tf_op jit(solution)/shard_map/first_half/pallas_call | solution.py:79
  58.2 4.3 %collective-permute-done.3.refs_0_.refs_1_ = bf16[1536,384]{1,0:T(8,128)(2,1)S(1)} collective-permute-done((bf16[1536,384]{1,0:T(8,128)(2,1)S(1)}, bf16[1536,384]{1,0:T(8,128)(2,1)S(1)}, u32[]{:S(2)}, u32[]{:S(2)}) %collective-permute-start.3) | collective-permute-done | bytes 1179680 | tf_op jit(solution)/shard_map/ppermute | solution.py:131
  62.6 1.1 collective-permute-start.7
  63.7 3.7 %collective-permute-start.8 = (bf16[512,384]{1,0:T(8,128)(2,1)S(1)}, bf16[512,384]{1,0:T(8,128)(2,1)S(1)}, u32[]{:S(2)}, u32[]{:S(2)}) collective-permute-start(bf16[512,384]{1,0:T(8,128)(2,1)S(1)} %get-tuple-element.48), channel_id=1, source_target_pairs={{0,3},{1,0},{2,1},{3,2},{4,7},{5,4},{6,5},{7,6},{8,11},{9,8},{10,9... | collective-permute-start | bytes 1179656 | tf_op jit(solution)/shard_map/ppermute | solution.py:131
  67.4 1.1 value_out.1
  69.2 3.2 %middle.1 = (f32[1536,384]{1,0:T(8,128)S(1)}, f32[1536,128]{1,0:T(8,128)S(1)}) custom-call(bf16[1536,384]{1,0:T(8,128)(2,1)S(1)} %collective-permute-done.3.refs_0_.refs_1_, bf16[1536,384]{1,0:T(8,128)(2,1)S(1)} %collective-permute-done.4.refs_1_.refs_2_, ...), custom_call_target="tpu_custom_call", output_to_operand_aliasing={{0}: (4, {}), {1}: (5, {})} | custom-call | flops 4000000000 | tf_op jit(solution)/shard_map/middle/pallas_call | solution.py:79
  72.5 1.2 collective-permute-done.7.refs_2_.refs_5_
  73.6 2.8 %collective-permute-done.6.refs_1_.refs_4_ = bf16[512,384]{1,0:T(8,128)(2,1)S(1)} collective-permute-done((bf16[512,384]{1,0:T(8,128)(2,1)S(1)}, bf16[512,384]{1,0:T(8,128)(2,1)S(1)}, u32[]{:S(2)}, u32[]{:S(2)}) %collective-permute-start.6) | collective-permute-done | bytes 393248 | tf_op jit(solution)/shard_map/ppermute | solution.py:131
  76.4 4.8 %queries_out.1 = (bf16[6,144,256]{2,1,0:T(8,128)(2,1)S(1)}, f32[1536,128]{1,0:T(8,128)S(1)}) custom-call(s32[113]{0:T(128)S(1)} %concatenate.3.refs_0_, bf16[512,384]{1,0:T(8,128)(2,1)S(1)} %collective-permute-done.6.refs_1_.refs_4_, bf16[512,384]{1,0:T(8,128)(2,1)S(1)} %collective-permute-done.7.refs_2_.refs_5_, ...), custom_call_target="tpu_custom_call", output_to_operand_aliasing={{1}: (6, {})} | custom-call | flops 2000000000 | tf_op jit(solution)/shard_map/queries_out/pallas_call | solution.py:79
  82.2 1.6 %collective-permute-start.11 = (bf16[6,144,256]{2,1,0:T(8,128)(2,1)S(1)}, bf16[6,144,256]{2,1,0:T(8,128)(2,1)S(1)}, u32[]{:S(2)}, u32[]{:S(2)}) collective-permute-start(bf16[6,144,256]{2,1,0:T(8,128)(2,1)S(1)} %get-tuple-element.56.refs_0_), channel_id=1, source_target_pairs={{0,1},{1,2},{2,3},{3,0},{4,5},{5,6},{6,7},{7,4},{8,9},{9,10},{10,1... | collective-permute-start | bytes 1327112 | tf_op jit(solution)/shard_map/ppermute | solution.py:131
  83.8 8.0 %audio_part.1 = (f32[2,32,384]{2,1,0:T(8,128)S(1)}, f32[2,32,384]{2,1,0:T(8,128)S(1)}, f32[2,32,384]{2,1,0:T(8,128)S(1)}) custom-call(s32[113]{0:T(128)S(1)} %concatenate.3.refs_0_, bf16[1536,384]{1,0:T(8,128)(2,1)S(1)} %collective-permute-done.3.refs_0_.refs_1_, bf16[1536,384]{1,0:T(8,128)(2,1)S(1)} %collective-permute-done.4.refs_1_.refs_2_, ...), custom_call_target="tpu_custom_call" | custom-call | tf_op jit(solution)/shard_map/audio_part/pallas_call | solution.py:79
  91.8 2.9 %collective-permute-done.11.refs_5_.refs_1_ = bf16[6,144,256]{2,1,0:T(8,128)(2,1)S(1)} collective-permute-done((bf16[6,144,256]{2,1,0:T(8,128)(2,1)S(1)}, bf16[6,144,256]{2,1,0:T(8,128)(2,1)S(1)}, u32[]{:S(2)}, u32[]{:S(2)}) %collective-permute-start.11) | collective-permute-done | bytes 442400 | tf_op jit(solution)/shard_map/ppermute | solution.py:131
  95.5 1.7 %collective-permute-start.15 = (bf16[11,144,256]{2,1,0:T(8,128)(2,1)S(1)}, bf16[11,144,256]{2,1,0:T(8,128)(2,1)S(1)}, u32[]{:S(2)}, u32[]{:S(2)}) collective-permute-start(bf16[11,144,256]{2,1,0:T(8,128)(2,1)S(1)} %get-tuple-element.61.refs_5_), channel_id=1, source_target_pairs={{0,1},{1,2},{2,3},{3,0},{4,5},{5,6},{6,7},{7,4},{8,9},{9,10},{10,1... | collective-permute-start | bytes 2433032 | tf_op jit(solution)/shard_map/ppermute | solution.py:131
  97.6 5.0 %collective-permute-start.18 = (f32[2,32,384]{2,1,0:T(8,128)S(1)}, f32[2,32,384]{2,1,0:T(8,128)S(1)}, u32[]{:S(2)}, u32[]{:S(2)}) collective-permute-start(f32[2,32,384]{2,1,0:T(8,128)S(1)} %get-tuple-element.65), channel_id=1, source_target_pairs={{0,8},{8,16},{16,24},{24,32},{32,40},{40,48},{48,56},{56,64},{64,7... | collective-permute-start | bytes 294920 | tf_op jit(solution)/shard_map/ppermute | solution.py:663
  102.5 1.3 collective-permute-start.19
  103.8 3.1 %collective-permute-done.18.refs_2_ = f32[2,32,384]{2,1,0:T(8,128)S(1)} collective-permute-done((f32[2,32,384]{2,1,0:T(8,128)S(1)}, f32[2,32,384]{2,1,0:T(8,128)S(1)}, u32[]{:S(2)}, u32[]{:S(2)}) %collective-permute-start.18) | collective-permute-done | bytes 98336 | tf_op jit(solution)/shard_map/ppermute | solution.py:663
  106.9 3.6 %collective-permute-done.19.refs_3_ = f32[2,32,384]{2,1,0:T(8,128)S(1)} collective-permute-done((f32[2,32,384]{2,1,0:T(8,128)S(1)}, f32[2,32,384]{2,1,0:T(8,128)S(1)}, u32[]{:S(2)}, u32[]{:S(2)}) %collective-permute-start.19) | collective-permute-done | bytes 98336 | tf_op jit(solution)/shard_map/ppermute | solution.py:666
  110.5 1.0 audio_out.1
  111.6 1.9 %collective-permute-done.16.refs_1_.refs_5_ = bf16[11,144,256]{2,1,0:T(8,128)(2,1)S(1)} collective-permute-done((bf16[11,144,256]{2,1,0:T(8,128)(2,1)S(1)}, bf16[11,144,256]{2,1,0:T(8,128)(2,1)S(1)}, u32[]{:S(2)}, u32[]{:S(2)}) %collective-permute-start.16) | collective-permute-done | bytes 811040 | tf_op jit(solution)/shard_map/ppermute | solution.py:131
  113.5 2.5 %collective-permute-done.15.refs_0_.refs_4_ = bf16[11,144,256]{2,1,0:T(8,128)(2,1)S(1)} collective-permute-done((bf16[11,144,256]{2,1,0:T(8,128)(2,1)S(1)}, bf16[11,144,256]{2,1,0:T(8,128)(2,1)S(1)}, u32[]{:S(2)}, u32[]{:S(2)}) %collective-permute-start.15) | collective-permute-done | bytes 811040 | tf_op jit(solution)/shard_map/ppermute | solution.py:131
  116.0 3.2 %collective-permute-start.21 = (bf16[5,144,256]{2,1,0:T(8,128)(2,1)S(1)}, bf16[5,144,256]{2,1,0:T(8,128)(2,1)S(1)}, u32[]{:S(2)}, u32[]{:S(2)}) collective-permute-start(bf16[5,144,256]{2,1,0:T(8,128)(2,1)S(1)} %get-tuple-element.68), channel_id=1, source_target_pairs={{0,3},{1,0},{2,1},{3,2},{4,7},{5,4},{6,5},{7,6},{8,11},{9,8},{10,9... | collective-permute-start | bytes 1105928 | tf_op jit(solution)/shard_map/ppermute | solution.py:131
  119.3 4.6 %collective-permute-done.22.refs_1_ = bf16[4,32,384]{2,1,0:T(8,128)(2,1)S(1)} collective-permute-done((bf16[4,32,384]{2,1,0:T(8,128)(2,1)S(1)}, bf16[4,32,384]{2,1,0:T(8,128)(2,1)S(1)}, u32[]{:S(2)}, u32[]{:S(2)}) %collective-permute-start.22) | collective-permute-done | bytes 98336 | tf_op jit(solution)/shard_map/ppermute | solution.py:131
  124.9 1.1 collective-permute-start.25
  126.6 2.9 %output.1.refs_0_ = bf16[1536,384]{1,0:T(8,128)(2,1)} custom-call(bf16[6,144,256]{2,1,0:T(8,128)(2,1)S(1)} %get-tuple-element.56.refs_0_, bf16[6,144,256]{2,1,0:T(8,128)(2,1)S(1)} %collective-permute-done.11.refs_5_.refs_1_, bf16[6,144,256]{2,1,0:T(8,128)(2,1)S(1)} %collective-permute-done.12.refs_1_.refs_2_, ...), custom_call_target="tpu_custom_call" | custom-call | flops 1000000000 | tf_op jit(solution)/shard_map/output/pallas_call | solution.py:79
  (44 shorter events, 10.5 us)
Async XLA Ops:
  0.6 34.9 %collective-permute-start.1 = (bf16[1536,384]{1,0:T(8,128)(2,1)}, bf16[1536,384]{1,0:T(8,128)(2,1)S(1)}, u32[]{:S(2)}, u32[]{:S(2)}) collective-permute-start(bf16[1536,384]{1,0:T(8,128)(2,1)} %refs_0_.1), channel_id=1, source_target_pairs={{0,3},{1,0},{2,1},{3,2},{4,7},{5,4},{6,5},{7,6},{8,11},{9,8},{10,9... | collective-permute-start | bytes 3538952 | tf_op jit(solution)/shard_map/ppermute | solution.py:131
  3.5 32.0 %collective-permute-start = (bf16[1536,384]{1,0:T(8,128)(2,1)}, bf16[1536,384]{1,0:T(8,128)(2,1)S(1)}, u32[]{:S(2)}, u32[]{:S(2)}) collective-permute-start(bf16[1536,384]{1,0:T(8,128)(2,1)} %refs_0_.1), channel_id=1, source_target_pairs={{0,1},{1,2},{2,3},{3,0},{4,5},{5,6},{6,7},{7,4},{8,9},{9,10},{10,1... | collective-permute-start | bytes 3538952 | tf_op jit(solution)/shard_map/ppermute | solution.py:131
  3.5 32.0 %collective-permute-start.2 = (bf16[1536,384]{1,0:T(8,128)(2,1)}, bf16[1536,384]{1,0:T(8,128)(2,1)S(1)}, u32[]{:S(2)}, u32[]{:S(2)}) collective-permute-start(bf16[1536,384]{1,0:T(8,128)(2,1)} %refs_0_.1), channel_id=1, source_target_pairs={{0,4},{1,5},{2,6},{3,7},{4,0},{5,1},{6,2},{7,3},{8,12},{9,13},{10,... | collective-permute-start | bytes 3538952 | tf_op jit(solution)/shard_map/ppermute | solution.py:131
  8.1 0.7 copy-start
  35.5 27.0 %collective-permute-start.3 = (bf16[1536,384]{1,0:T(8,128)(2,1)S(1)}, bf16[1536,384]{1,0:T(8,128)(2,1)S(1)}, u32[]{:S(2)}, u32[]{:S(2)}) collective-permute-start(bf16[1536,384]{1,0:T(8,128)(2,1)S(1)} %get-tuple-element.39.refs_3_), channel_id=1, source_target_pairs={{0,1},{1,2},{2,3},{3,0},{4,5},{5,6},{6,7},{7,4},{8,9},{9,10},{10,1... | collective-permute-start | bytes 3538952 | tf_op jit(solution)/shard_map/ppermute | solution.py:131
  35.6 26.9 %collective-permute-start.5 = (bf16[1536,384]{1,0:T(8,128)(2,1)S(1)}, bf16[1536,384]{1,0:T(8,128)(2,1)S(1)}, u32[]{:S(2)}, u32[]{:S(2)}) collective-permute-start(bf16[1536,384]{1,0:T(8,128)(2,1)S(1)} %get-tuple-element.40.refs_2_), channel_id=1, source_target_pairs={{0,4},{1,5},{2,6},{3,7},{4,0},{5,1},{6,2},{7,3},{8,12},{9,13},{10,... | collective-permute-start | bytes 3538952 | tf_op jit(solution)/shard_map/ppermute | solution.py:131
  36.1 26.4 %collective-permute-start.4 = (bf16[1536,384]{1,0:T(8,128)(2,1)S(1)}, bf16[1536,384]{1,0:T(8,128)(2,1)S(1)}, u32[]{:S(2)}, u32[]{:S(2)}) collective-permute-start(bf16[1536,384]{1,0:T(8,128)(2,1)S(1)} %get-tuple-element.40.refs_2_), channel_id=1, source_target_pairs={{0,3},{1,0},{2,1},{3,2},{4,7},{5,4},{6,5},{7,6},{8,11},{9,8},{10,9... | collective-permute-start | bytes 3538952 | tf_op jit(solution)/shard_map/ppermute | solution.py:131
  39.3 11.0 %copy-start.1 = (bf16[1536,384]{1,0:T(8,128)(2,1)S(1)}, bf16[1536,384]{1,0:T(8,128)(2,1)}, u32[]{:S(2)}) copy-start(bf16[1536,384]{1,0:T(8,128)(2,1)} %refs_0_.1) | copy-start | bytes 3538948
  43.0 24.5 %collective-permute-start.10 = (bf16[48,384]{1,0:T(8,128)(2,1)S(1)}, bf16[48,384]{1,0:T(8,128)(2,1)S(1)}, u32[]{:S(2)}, u32[]{:S(2)}) collective-permute-start(bf16[48,384]{1,0:T(8,128)(2,1)S(1)} %get-tuple-element.43.refs_5_), channel_id=1, source_target_pairs={{8,0},{16,8},{24,16},{32,24},{40,32},{48,40},{56,48},{64,56},{72,6... | collective-permute-start | bytes 110600 | tf_op jit(solution)/shard_map/ppermute | solution.py:666
  44.3 23.2 %collective-permute-start.9 = (bf16[48,384]{1,0:T(8,128)(2,1)S(1)}, bf16[48,384]{1,0:T(8,128)(2,1)S(1)}, u32[]{:S(2)}, u32[]{:S(2)}) collective-permute-start(bf16[48,384]{1,0:T(8,128)(2,1)S(1)} %get-tuple-element.44.refs_6_), channel_id=1, source_target_pairs={{0,8},{8,16},{16,24},{24,32},{32,40},{40,48},{48,56},{56,64},{64,7... | collective-permute-start | bytes 110600 | tf_op jit(solution)/shard_map/ppermute | solution.py:663
  62.6 11.0 %collective-permute-start.7 = (bf16[512,384]{1,0:T(8,128)(2,1)S(1)}, bf16[512,384]{1,0:T(8,128)(2,1)S(1)}, u32[]{:S(2)}, u32[]{:S(2)}) collective-permute-start(bf16[512,384]{1,0:T(8,128)(2,1)S(1)} %get-tuple-element.47), channel_id=1, source_target_pairs={{0,4},{1,5},{2,6},{3,7},{4,0},{5,1},{6,2},{7,3},{8,12},{9,13},{10,... | collective-permute-start | bytes 1179656 | tf_op jit(solution)/shard_map/ppermute | solution.py:131
  63.7 9.9 %collective-permute-start.8 = (bf16[512,384]{1,0:T(8,128)(2,1)S(1)}, bf16[512,384]{1,0:T(8,128)(2,1)S(1)}, u32[]{:S(2)}, u32[]{:S(2)}) collective-permute-start(bf16[512,384]{1,0:T(8,128)(2,1)S(1)} %get-tuple-element.48), channel_id=1, source_target_pairs={{0,3},{1,0},{2,1},{3,2},{4,7},{5,4},{6,5},{7,6},{8,11},{9,8},{10,9... | collective-permute-start | bytes 1179656 | tf_op jit(solution)/shard_map/ppermute | solution.py:131
  67.4 9.0 %collective-permute-start.6 = (bf16[512,384]{1,0:T(8,128)(2,1)S(1)}, bf16[512,384]{1,0:T(8,128)(2,1)S(1)}, u32[]{:S(2)}, u32[]{:S(2)}) collective-permute-start(bf16[512,384]{1,0:T(8,128)(2,1)S(1)} %get-tuple-element.46.refs_5_), channel_id=1, source_target_pairs={{0,1},{1,2},{2,3},{3,0},{4,5},{5,6},{6,7},{7,4},{8,9},{9,10},{10,1... | collective-permute-start | bytes 1179656 | tf_op jit(solution)/shard_map/ppermute | solution.py:131
  68.5 23.2 %collective-permute-start.14 = (bf16[4,144,384]{2,1,0:T(8,128)(2,1)S(1)}, bf16[4,144,384]{2,1,0:T(8,128)(2,1)S(1)}, u32[]{:S(2)}, u32[]{:S(2)}) collective-permute-start(bf16[4,144,384]{2,1,0:T(8,128)(2,1)S(1)} %get-tuple-element.57), channel_id=1, source_target_pairs={{0,4},{1,5},{2,6},{3,7},{4,0},{5,1},{6,2},{7,3},{8,12},{9,13},{10,... | collective-permute-start | bytes 1327112 | tf_op jit(solution)/shard_map/ppermute | solution.py:131
  81.2 10.5 %collective-permute-start.13 = (bf16[6,144,256]{2,1,0:T(8,128)(2,1)S(1)}, bf16[6,144,256]{2,1,0:T(8,128)(2,1)S(1)}, u32[]{:S(2)}, u32[]{:S(2)}) collective-permute-start(bf16[6,144,256]{2,1,0:T(8,128)(2,1)S(1)} %get-tuple-element.56.refs_0_), channel_id=1, source_target_pairs={{0,4},{1,5},{2,6},{3,7},{4,0},{5,1},{6,2},{7,3},{8,12},{9,13},{10,... | collective-permute-start | bytes 1327112 | tf_op jit(solution)/shard_map/ppermute | solution.py:131
  81.7 10.0 %collective-permute-start.12 = (bf16[6,144,256]{2,1,0:T(8,128)(2,1)S(1)}, bf16[6,144,256]{2,1,0:T(8,128)(2,1)S(1)}, u32[]{:S(2)}, u32[]{:S(2)}) collective-permute-start(bf16[6,144,256]{2,1,0:T(8,128)(2,1)S(1)} %get-tuple-element.56.refs_0_), channel_id=1, source_target_pairs={{0,3},{1,0},{2,1},{3,2},{4,7},{5,4},{6,5},{7,6},{8,11},{9,8},{10,9... | collective-permute-start | bytes 1327112 | tf_op jit(solution)/shard_map/ppermute | solution.py:131
  82.2 12.5 %collective-permute-start.11 = (bf16[6,144,256]{2,1,0:T(8,128)(2,1)S(1)}, bf16[6,144,256]{2,1,0:T(8,128)(2,1)S(1)}, u32[]{:S(2)}, u32[]{:S(2)}) collective-permute-start(bf16[6,144,256]{2,1,0:T(8,128)(2,1)S(1)} %get-tuple-element.56.refs_0_), channel_id=1, source_target_pairs={{0,1},{1,2},{2,3},{3,0},{4,5},{5,6},{6,7},{7,4},{8,9},{9,10},{10,1... | collective-permute-start | bytes 1327112 | tf_op jit(solution)/shard_map/ppermute | solution.py:131
  94.9 18.6 %collective-permute-start.16 = (bf16[11,144,256]{2,1,0:T(8,128)(2,1)S(1)}, bf16[11,144,256]{2,1,0:T(8,128)(2,1)S(1)}, u32[]{:S(2)}, u32[]{:S(2)}) collective-permute-start(bf16[11,144,256]{2,1,0:T(8,128)(2,1)S(1)} %get-tuple-element.62), channel_id=1, source_target_pairs={{0,3},{1,0},{2,1},{3,2},{4,7},{5,4},{6,5},{7,6},{8,11},{9,8},{10,9... | collective-permute-start | bytes 2433032 | tf_op jit(solution)/shard_map/ppermute | solution.py:131
  95.5 20.5 %collective-permute-start.15 = (bf16[11,144,256]{2,1,0:T(8,128)(2,1)S(1)}, bf16[11,144,256]{2,1,0:T(8,128)(2,1)S(1)}, u32[]{:S(2)}, u32[]{:S(2)}) collective-permute-start(bf16[11,144,256]{2,1,0:T(8,128)(2,1)S(1)} %get-tuple-element.61.refs_5_), channel_id=1, source_target_pairs={{0,1},{1,2},{2,3},{3,0},{4,5},{5,6},{6,7},{7,4},{8,9},{9,10},{10,1... | collective-permute-start | bytes 2433032 | tf_op jit(solution)/shard_map/ppermute | solution.py:131
  97.2 14.4 %collective-permute-start.17 = (bf16[6,144,256]{2,1,0:T(8,128)(2,1)S(1)}, bf16[6,144,256]{2,1,0:T(8,128)(2,1)S(1)}, u32[]{:S(2)}, u32[]{:S(2)}) collective-permute-start(bf16[6,144,256]{2,1,0:T(8,128)(2,1)S(1)} %get-tuple-element.63), channel_id=1, source_target_pairs={{0,4},{1,5},{2,6},{3,7},{4,0},{5,1},{6,2},{7,3},{8,12},{9,13},{10,... | collective-permute-start | bytes 1327112 | tf_op jit(solution)/shard_map/ppermute | solution.py:131
  97.6 9.4 %collective-permute-start.18 = (f32[2,32,384]{2,1,0:T(8,128)S(1)}, f32[2,32,384]{2,1,0:T(8,128)S(1)}, u32[]{:S(2)}, u32[]{:S(2)}) collective-permute-start(f32[2,32,384]{2,1,0:T(8,128)S(1)} %get-tuple-element.65), channel_id=1, source_target_pairs={{0,8},{8,16},{16,24},{24,32},{32,40},{40,48},{48,56},{56,64},{64,7... | collective-permute-start | bytes 294920 | tf_op jit(solution)/shard_map/ppermute | solution.py:663
  102.5 8.0 %collective-permute-start.19 = (f32[2,32,384]{2,1,0:T(8,128)S(1)}, f32[2,32,384]{2,1,0:T(8,128)S(1)}, u32[]{:S(2)}, u32[]{:S(2)}) collective-permute-start(f32[2,32,384]{2,1,0:T(8,128)S(1)} %get-tuple-element.60.refs_4_), channel_id=1, source_target_pairs={{8,0},{16,8},{24,16},{32,24},{40,32},{48,40},{56,48},{64,56},{72,6... | collective-permute-start | bytes 294920 | tf_op jit(solution)/shard_map/ppermute | solution.py:666
  116.0 10.6 %collective-permute-start.20 = (bf16[5,144,256]{2,1,0:T(8,128)(2,1)S(1)}, bf16[5,144,256]{2,1,0:T(8,128)(2,1)S(1)}, u32[]{:S(2)}, u32[]{:S(2)}) collective-permute-start(bf16[5,144,256]{2,1,0:T(8,128)(2,1)S(1)} %get-tuple-element.67), channel_id=1, source_target_pairs={{0,1},{1,2},{2,3},{3,0},{4,5},{5,6},{6,7},{7,4},{8,9},{9,10},{10,1... | collective-permute-start | bytes 1105928 | tf_op jit(solution)/shard_map/ppermute | solution.py:131
  116.0 10.6 %collective-permute-start.21 = (bf16[5,144,256]{2,1,0:T(8,128)(2,1)S(1)}, bf16[5,144,256]{2,1,0:T(8,128)(2,1)S(1)}, u32[]{:S(2)}, u32[]{:S(2)}) collective-permute-start(bf16[5,144,256]{2,1,0:T(8,128)(2,1)S(1)} %get-tuple-element.68), channel_id=1, source_target_pairs={{0,3},{1,0},{2,1},{3,2},{4,7},{5,4},{6,5},{7,6},{8,11},{9,8},{10,9... | collective-permute-start | bytes 1105928 | tf_op jit(solution)/shard_map/ppermute | solution.py:131
  119.3 4.6 %collective-permute-start.22 = (bf16[4,32,384]{2,1,0:T(8,128)(2,1)S(1)}, bf16[4,32,384]{2,1,0:T(8,128)(2,1)S(1)}, u32[]{:S(2)}, u32[]{:S(2)}) collective-permute-start(bf16[4,32,384]{2,1,0:T(8,128)(2,1)S(1)} %get-tuple-element.66.refs_3_), channel_id=1, source_target_pairs={{0,4},{1,5},{2,6},{3,7},{4,0},{5,1},{6,2},{7,3},{8,12},{9,13},{10,... | collective-permute-start | bytes 294920 | tf_op jit(solution)/shard_map/ppermute | solution.py:131
  123.9 5.6 %collective-permute-start.23 = (bf16[32,384]{1,0:T(8,128)(2,1)S(1)}, bf16[32,384]{1,0:T(8,128)(2,1)S(1)}, u32[]{:S(2)}, u32[]{:S(2)}) collective-permute-start(bf16[32,384]{1,0:T(8,128)(2,1)S(1)} %get-tuple-element.71), channel_id=1, source_target_pairs={{0,3},{1,0},{2,1},{3,2},{4,7},{5,4},{6,5},{7,6},{8,11},{9,8},{10,9... | collective-permute-start | bytes 73736 | tf_op jit(solution)/shard_map/ppermute | solution.py:131
  124.0 5.6 %collective-permute-start.24 = (bf16[32,384]{1,0:T(8,128)(2,1)S(1)}, bf16[32,384]{1,0:T(8,128)(2,1)S(1)}, u32[]{:S(2)}, u32[]{:S(2)}) collective-permute-start(bf16[32,384]{1,0:T(8,128)(2,1)S(1)} %get-tuple-element.72), channel_id=1, source_target_pairs={{0,2},{1,3},{2,0},{3,1},{4,6},{5,7},{6,4},{7,5},{8,10},{9,11},{10,... | collective-permute-start | bytes 73736 | tf_op jit(solution)/shard_map/ppermute | solution.py:131
  124.9 5.6 %collective-permute-start.25 = (bf16[32,384]{1,0:T(8,128)(2,1)S(1)}, bf16[32,384]{1,0:T(8,128)(2,1)S(1)}, u32[]{:S(2)}, u32[]{:S(2)}) collective-permute-start(bf16[32,384]{1,0:T(8,128)(2,1)S(1)} %get-tuple-element.73), channel_id=1, source_target_pairs={{0,1},{1,2},{2,3},{3,0},{4,5},{5,6},{6,7},{7,4},{8,9},{9,10},{10,1... | collective-permute-start | bytes 73736 | tf_op jit(solution)/shard_map/ppermute | solution.py:131

commit v7 on v6

--- a/solution.py
+++ b/solution.py
@@ -512,11 +512,12 @@
             value = (total[:, GROUP + h * HEAD : GROUP + (h + 1) * HEAD] * spread).astype(BF16)
             scores = dot_nt(queries[:, cols], head_norm(total[:, cols], floor))
             weights = jnp.where(seen, jnp.exp2(scores * SCALE), 0.0)
-            bottom = jnp.broadcast_to(jnp.sum(weights, axis=1, keepdims=True), (3 * AUD, HEAD))
+            lane = lax.broadcasted_iota(jnp.int32, (3 * AUD, HEAD), 1)
+            bottom = jnp.where(lane == h, jnp.sum(weights, axis=1, keepdims=True), 0.0)
             top = dot(weights.astype(BF16), value)
             for g, ref in enumerate((part_p, part_o, part_n)):
-                ref[0, :, cols] += top[g * AUD : (g + 1) * AUD]
-                ref[1, :, cols] += bottom[g * AUD : (g + 1) * AUD]
+                ref[:, cols] += top[g * AUD : (g + 1) * AUD]
+                ref[:, GROUP:] += bottom[g * AUD : (g + 1) * AUD]
 
     by_thirds(body, (xa, xb, xc))
 
@@ -529,7 +530,7 @@
         [(SMEM, meta)]
         + [(VMEM, a) for a in (*pieces, weights, acc, stat, sums, qkv, from_prev, from_next)],
         extra,
-        [pltpu.VMEM((2, AUD, GROUP), F32)] * 3,
+        [pltpu.VMEM((AUD, GROUP + HEAD), F32)] * 3,
     )
 
 
@@ -537,7 +538,11 @@
     total = own_ref[...] + prev_ref[...] + next_ref[...]
     row = lax.broadcasted_iota(jnp.int32, (AUD, 1), 0)
     valid = row < meta_ref[AT_AUDIO + meta_ref[AT_SHARD]]
-    attended = jnp.where(valid, total[0] / total[1], 0.0).astype(BF16)
+    heads = [
+        total[:, h * HEAD : (h + 1) * HEAD] / total[:, GROUP + h : GROUP + h + 1]
+        for h in range(HEADS_DEV)
+    ]
+    attended = jnp.where(valid, jnp.concatenate(heads, axis=1), 0.0).astype(BF16)
     for j, (dy, dx) in enumerate(OFFSETS):
         product = dot(attended, w_ref[1, :, dest_cols(meta_ref, j)]).astype(BF16)
         (give_ref if dy else keep_ref)[dx] = product

time: 131 us -> 131 us (level)
  no operation moved by 1% of the time
where the time goes in v7:
time: 131 us
  Pallas kernels  39.9 us (30%)
  starting transfers between devices  37.9 us (29%)
  waiting for transfers between devices  28.3 us (22%)
  blocking collectives  20.4 us (16%)
  local copies, waits for them, and re-layouts  3.7 us (3%)
    pallas_call x15, Pallas kernels, call(): pl.pallas_call(run, in_specs=[spec for spec, _ in inputs] + [ANY] * len(e...  39.9 us
    ppermute x22, starting transfers between devices, send(): return lax.ppermute(array, 'tensor', pairs)  24.3 us
    ppermute x22, waiting for transfers between devices, send(): return lax.ppermute(array, 'tensor', pairs)  22 us
    all_to_all x1, blocking collectives, shards(): audio_blocks = lax.all_to_all(audio_copies, 'tensor', 0, 0)  20.4 us
    ppermute x2, starting transfers between devices, to_next(): return lax.ppermute(array, ('tower', 'tm'), up)  11 us
    ppermute x2, waiting for transfers between devices, to_prev(): return lax.ppermute(array, ('tower', 'tm'), down)  3.95 us
  transfers between devices with their start and end apart: 26, of which 11 were waited for; matrix products, arithmetic and copies ran while one was open for 2% of the time, Pallas kernels for 30%

profile of v7, /device:TPU:0, one launch (start us, length us, event | category | flops | bytes accessed | tf_op | source)
XLA Modules:
  0.0 131.1 jit_solution(9373496836182913271)
XLA Ops:
  0.6 2.9 %collective-permute-start.1 = (bf16[1536,384]{1,0:T(8,128)(2,1)}, bf16[1536,384]{1,0:T(8,128)(2,1)S(1)}, u32[]{:S(2)}, u32[]{:S(2)}) collective-permute-start(bf16[1536,384]{1,0:T(8,128)(2,1)} %refs_0_.1), channel_id=1, source_target_pairs={{0,3},{1,0},{2,1},{3,2},{4,7},{5,4},{6,5},{7,6},{8,11},{9,8},{10,9... | collective-permute-start | bytes 3538952 | tf_op jit(solution)/shard_map/ppermute | solution.py:131
  3.5 1.6 %collective-permute-start.2 = (bf16[1536,384]{1,0:T(8,128)(2,1)}, bf16[1536,384]{1,0:T(8,128)(2,1)S(1)}, u32[]{:S(2)}, u32[]{:S(2)}) collective-permute-start(bf16[1536,384]{1,0:T(8,128)(2,1)} %refs_0_.1), channel_id=1, source_target_pairs={{0,4},{1,5},{2,6},{3,7},{4,0},{5,1},{6,2},{7,3},{8,12},{9,13},{10,... | collective-permute-start | bytes 3538952 | tf_op jit(solution)/shard_map/ppermute | solution.py:131
  8.8 6.3 %prefetch.1 = (bf16[8,32,384]{2,1,0:T(8,128)(2,1)S(1)}, bf16[3072,1152]{1,0:T(8,128)(2,1)S(1)}, bf16[2,384,3072]{2,1,0:T(8,128)(2,1)S(1)}, f32[8,1152]{1,0:T(8,128)S(1)}) custom-call(s32[113]{0:T(128)S(1)} %concatenate.3.refs_0_, bf16[32,384]{1,0:T(8,128)(2,1)S(1)} %copy-done, bf16[2,3072,384]{2,1,0:T(8,128)(2,1)} %refs_1_.3, bf16[2,3072,384]{2,1,0:T(8,128)(2,1)} %refs_2_.3, ...), custom_call_target="tpu_custom_call" | custom-call | tf_op jit(solution)/shard_map/prefetch/pallas_call | solution.py:79
  15.1 20.4 %all_to_all.5.refs_3_.refs_0_ = bf16[8,32,384]{2,1,0:T(8,128)(2,1)S(1)} all-to-all(bf16[8,32,384]{2,1,0:T(8,128)(2,1)S(1)} %get-tuple-element.38), channel_id=1, replica_groups=mesh['tower'=2,'tm'=8,'tensor'=8] {'tensor'}, dimensions={0} | all-to-all | bytes 393216 | tf_op jit(solution)/shard_map/all_to_all | solution.py:695
  36.1 3.1 %collective-permute-start.4 = (bf16[1536,384]{1,0:T(8,128)(2,1)S(1)}, bf16[1536,384]{1,0:T(8,128)(2,1)S(1)}, u32[]{:S(2)}, u32[]{:S(2)}) collective-permute-start(bf16[1536,384]{1,0:T(8,128)(2,1)S(1)} %get-tuple-element.40.refs_2_), channel_id=1, source_target_pairs={{0,3},{1,0},{2,1},{3,2},{4,7},{5,4},{6,5},{7,6},{8,11},{9,8},{10,9... | collective-permute-start | bytes 3538952 | tf_op jit(solution)/shard_map/ppermute | solution.py:131
  39.3 3.7 %audio_in.1 = (bf16[96,384]{1,0:T(8,128)(2,1)S(1)}, bf16[48,384]{1,0:T(8,128)(2,1)S(1)}, bf16[48,384]{1,0:T(8,128)(2,1)S(1)}) custom-call(bf16[8,32,384]{2,1,0:T(8,128)(2,1)S(1)} %all_to_all.5.refs_3_.refs_0_, bf16[2,3072,384]{2,1,0:T(8,128)(2,1)} %refs_1_.3, bf16[2,3072,384]{2,1,0:T(8,128)(2,1)} %refs_2_.3, bf16[2,3072,384]{2,1,0:T(8,128)(2,1)} %refs_3_.3, ...), custom_call_target="tpu_custom_call" | custom-call | flops 2000000000 | tf_op jit(solution)/shard_map/audio_in/pallas_call | solution.py:79
  43.0 1.3 collective-permute-start.10
  44.3 6.1 %collective-permute-start.9 = (bf16[48,384]{1,0:T(8,128)(2,1)S(1)}, bf16[48,384]{1,0:T(8,128)(2,1)S(1)}, u32[]{:S(2)}, u32[]{:S(2)}) collective-permute-start(bf16[48,384]{1,0:T(8,128)(2,1)S(1)} %get-tuple-element.44.refs_6_), channel_id=1, source_target_pairs={{0,8},{8,16},{16,24},{24,32},{32,40},{40,48},{48,56},{56,64},{64,7... | collective-permute-start | bytes 110600 | tf_op jit(solution)/shard_map/ppermute | solution.py:668
  50.3 7.9 %first_half.1 = (f32[1536,384]{1,0:T(8,128)S(1)}, f32[1536,768]{1,0:T(8,128)S(1)}, f32[1536,128]{1,0:T(8,128)S(1)}) custom-call(bf16[1536,384]{1,0:T(8,128)(2,1)S(1)} %copy-done.1, bf16[1536,384]{1,0:T(8,128)(2,1)S(1)} %get-tuple-element.41.refs_4_.refs_1_, bf16[1536,384]{1,0:T(8,128)(2,1)S(1)} %get-tuple-element.40.refs_2_, ...), custom_call_target="tpu_custom_call" | custom-call | flops 4000000000 | tf_op jit(solution)/shard_map/first_half/pallas_call | solution.py:79
  58.2 4.3 %collective-permute-done.3.refs_0_.refs_1_ = bf16[1536,384]{1,0:T(8,128)(2,1)S(1)} collective-permute-done((bf16[1536,384]{1,0:T(8,128)(2,1)S(1)}, bf16[1536,384]{1,0:T(8,128)(2,1)S(1)}, u32[]{:S(2)}, u32[]{:S(2)}) %collective-permute-start.3) | collective-permute-done | bytes 1179680 | tf_op jit(solution)/shard_map/ppermute | solution.py:131
  62.6 1.1 collective-permute-start.7
  63.7 3.7 %collective-permute-start.8 = (bf16[512,384]{1,0:T(8,128)(2,1)S(1)}, bf16[512,384]{1,0:T(8,128)(2,1)S(1)}, u32[]{:S(2)}, u32[]{:S(2)}) collective-permute-start(bf16[512,384]{1,0:T(8,128)(2,1)S(1)} %get-tuple-element.48), channel_id=1, source_target_pairs={{0,3},{1,0},{2,1},{3,2},{4,7},{5,4},{6,5},{7,6},{8,11},{9,8},{10,9... | collective-permute-start | bytes 1179656 | tf_op jit(solution)/shard_map/ppermute | solution.py:131
  67.4 1.1 value_out.1
  69.2 3.2 %middle.1 = (f32[1536,384]{1,0:T(8,128)S(1)}, f32[1536,128]{1,0:T(8,128)S(1)}) custom-call(bf16[1536,384]{1,0:T(8,128)(2,1)S(1)} %collective-permute-done.3.refs_0_.refs_1_, bf16[1536,384]{1,0:T(8,128)(2,1)S(1)} %collective-permute-done.4.refs_1_.refs_2_, ...), custom_call_target="tpu_custom_call", output_to_operand_aliasing={{0}: (4, {}), {1}: (5, {})} | custom-call | flops 4000000000 | tf_op jit(solution)/shard_map/middle/pallas_call | solution.py:79
  72.5 1.2 collective-permute-done.7.refs_2_.refs_5_
  73.6 2.8 %collective-permute-done.6.refs_1_.refs_4_ = bf16[512,384]{1,0:T(8,128)(2,1)S(1)} collective-permute-done((bf16[512,384]{1,0:T(8,128)(2,1)S(1)}, bf16[512,384]{1,0:T(8,128)(2,1)S(1)}, u32[]{:S(2)}, u32[]{:S(2)}) %collective-permute-start.6) | collective-permute-done | bytes 393248 | tf_op jit(solution)/shard_map/ppermute | solution.py:131
  76.4 4.8 %queries_out.1 = (bf16[6,144,256]{2,1,0:T(8,128)(2,1)S(1)}, f32[1536,128]{1,0:T(8,128)S(1)}) custom-call(s32[113]{0:T(128)S(1)} %concatenate.3.refs_0_, bf16[512,384]{1,0:T(8,128)(2,1)S(1)} %collective-permute-done.6.refs_1_.refs_4_, bf16[512,384]{1,0:T(8,128)(2,1)S(1)} %collective-permute-done.7.refs_2_.refs_5_, ...), custom_call_target="tpu_custom_call", output_to_operand_aliasing={{1}: (6, {})} | custom-call | flops 2000000000 | tf_op jit(solution)/shard_map/queries_out/pallas_call | solution.py:79
  82.2 1.6 %collective-permute-start.11 = (bf16[6,144,256]{2,1,0:T(8,128)(2,1)S(1)}, bf16[6,144,256]{2,1,0:T(8,128)(2,1)S(1)}, u32[]{:S(2)}, u32[]{:S(2)}) collective-permute-start(bf16[6,144,256]{2,1,0:T(8,128)(2,1)S(1)} %get-tuple-element.56.refs_0_), channel_id=1, source_target_pairs={{0,1},{1,2},{2,3},{3,0},{4,5},{5,6},{6,7},{7,4},{8,9},{9,10},{10,1... | collective-permute-start | bytes 1327112 | tf_op jit(solution)/shard_map/ppermute | solution.py:131
  83.8 8.0 %audio_part.1 = (f32[32,512]{1,0:T(8,128)S(1)}, f32[32,512]{1,0:T(8,128)S(1)}, f32[32,512]{1,0:T(8,128)S(1)}) custom-call(s32[113]{0:T(128)S(1)} %concatenate.3.refs_0_, bf16[1536,384]{1,0:T(8,128)(2,1)S(1)} %collective-permute-done.3.refs_0_.refs_1_, bf16[1536,384]{1,0:T(8,128)(2,1)S(1)} %collective-permute-done.4.refs_1_.refs_2_, ...), custom_call_target="tpu_custom_call" | custom-call | tf_op jit(solution)/shard_map/audio_part/pallas_call | solution.py:79
  91.8 2.9 %collective-permute-done.11.refs_5_.refs_1_ = bf16[6,144,256]{2,1,0:T(8,128)(2,1)S(1)} collective-permute-done((bf16[6,144,256]{2,1,0:T(8,128)(2,1)S(1)}, bf16[6,144,256]{2,1,0:T(8,128)(2,1)S(1)}, u32[]{:S(2)}, u32[]{:S(2)}) %collective-permute-start.11) | collective-permute-done | bytes 442400 | tf_op jit(solution)/shard_map/ppermute | solution.py:131
  95.5 1.7 %collective-permute-start.15 = (bf16[11,144,256]{2,1,0:T(8,128)(2,1)S(1)}, bf16[11,144,256]{2,1,0:T(8,128)(2,1)S(1)}, u32[]{:S(2)}, u32[]{:S(2)}) collective-permute-start(bf16[11,144,256]{2,1,0:T(8,128)(2,1)S(1)} %get-tuple-element.61.refs_5_), channel_id=1, source_target_pairs={{0,1},{1,2},{2,3},{3,0},{4,5},{5,6},{6,7},{7,4},{8,9},{9,10},{10,1... | collective-permute-start | bytes 2433032 | tf_op jit(solution)/shard_map/ppermute | solution.py:131
  97.6 5.0 %collective-permute-start.18 = (f32[32,512]{1,0:T(8,128)S(1)}, f32[32,512]{1,0:T(8,128)S(1)}, u32[]{:S(2)}, u32[]{:S(2)}) collective-permute-start(f32[32,512]{1,0:T(8,128)S(1)} %get-tuple-element.65), channel_id=1, source_target_pairs={{0,8},{8,16},{16,24},{24,32},{32,40},{40,48},{48,56},{56,64},{64,7... | collective-permute-start | bytes 196616 | tf_op jit(solution)/shard_map/ppermute | solution.py:668
  102.5 1.3 collective-permute-start.19
  103.8 2.4 %collective-permute-done.18.refs_2_ = f32[32,512]{1,0:T(8,128)S(1)} collective-permute-done((f32[32,512]{1,0:T(8,128)S(1)}, f32[32,512]{1,0:T(8,128)S(1)}, u32[]{:S(2)}, u32[]{:S(2)}) %collective-permute-start.18) | collective-permute-done | bytes 65568 | tf_op jit(solution)/shard_map/ppermute | solution.py:668
  106.2 4.0 %collective-permute-done.19.refs_3_ = f32[32,512]{1,0:T(8,128)S(1)} collective-permute-done((f32[32,512]{1,0:T(8,128)S(1)}, f32[32,512]{1,0:T(8,128)S(1)}, u32[]{:S(2)}, u32[]{:S(2)}) %collective-permute-start.19) | collective-permute-done | bytes 65568 | tf_op jit(solution)/shard_map/ppermute | solution.py:671
  110.2 1.1 audio_out.1
  111.3 2.2 %collective-permute-done.16.refs_1_.refs_5_ = bf16[11,144,256]{2,1,0:T(8,128)(2,1)S(1)} collective-permute-done((bf16[11,144,256]{2,1,0:T(8,128)(2,1)S(1)}, bf16[11,144,256]{2,1,0:T(8,128)(2,1)S(1)}, u32[]{:S(2)}, u32[]{:S(2)}) %collective-permute-start.16) | collective-permute-done | bytes 811040 | tf_op jit(solution)/shard_map/ppermute | solution.py:131
  113.5 2.5 %collective-permute-done.15.refs_0_.refs_4_ = bf16[11,144,256]{2,1,0:T(8,128)(2,1)S(1)} collective-permute-done((bf16[11,144,256]{2,1,0:T(8,128)(2,1)S(1)}, bf16[11,144,256]{2,1,0:T(8,128)(2,1)S(1)}, u32[]{:S(2)}, u32[]{:S(2)}) %collective-permute-start.15) | collective-permute-done | bytes 811040 | tf_op jit(solution)/shard_map/ppermute | solution.py:131
  116.0 3.2 %collective-permute-start.21 = (bf16[5,144,256]{2,1,0:T(8,128)(2,1)S(1)}, bf16[5,144,256]{2,1,0:T(8,128)(2,1)S(1)}, u32[]{:S(2)}, u32[]{:S(2)}) collective-permute-start(bf16[5,144,256]{2,1,0:T(8,128)(2,1)S(1)} %get-tuple-element.68), channel_id=1, source_target_pairs={{0,3},{1,0},{2,1},{3,2},{4,7},{5,4},{6,5},{7,6},{8,11},{9,8},{10,9... | collective-permute-start | bytes 1105928 | tf_op jit(solution)/shard_map/ppermute | solution.py:131
  119.3 4.6 %collective-permute-done.22.refs_1_ = bf16[4,32,384]{2,1,0:T(8,128)(2,1)S(1)} collective-permute-done((bf16[4,32,384]{2,1,0:T(8,128)(2,1)S(1)}, bf16[4,32,384]{2,1,0:T(8,128)(2,1)S(1)}, u32[]{:S(2)}, u32[]{:S(2)}) %collective-permute-start.22) | collective-permute-done | bytes 98336 | tf_op jit(solution)/shard_map/ppermute | solution.py:131
  124.9 1.1 collective-permute-start.25
  126.6 2.9 %output.1.refs_0_ = bf16[1536,384]{1,0:T(8,128)(2,1)} custom-call(bf16[6,144,256]{2,1,0:T(8,128)(2,1)S(1)} %get-tuple-element.56.refs_0_, bf16[6,144,256]{2,1,0:T(8,128)(2,1)S(1)} %collective-permute-done.11.refs_5_.refs_1_, bf16[6,144,256]{2,1,0:T(8,128)(2,1)S(1)} %collective-permute-done.12.refs_1_.refs_2_, ...), custom_call_target="tpu_custom_call" | custom-call | flops 1000000000 | tf_op jit(solution)/shard_map/output/pallas_call | solution.py:79
  (44 shorter events, 10.5 us)
Async XLA Ops:
  0.6 34.9 %collective-permute-start.1 = (bf16[1536,384]{1,0:T(8,128)(2,1)}, bf16[1536,384]{1,0:T(8,128)(2,1)S(1)}, u32[]{:S(2)}, u32[]{:S(2)}) collective-permute-start(bf16[1536,384]{1,0:T(8,128)(2,1)} %refs_0_.1), channel_id=1, source_target_pairs={{0,3},{1,0},{2,1},{3,2},{4,7},{5,4},{6,5},{7,6},{8,11},{9,8},{10,9... | collective-permute-start | bytes 3538952 | tf_op jit(solution)/shard_map/ppermute | solution.py:131
  3.5 32.0 %collective-permute-start = (bf16[1536,384]{1,0:T(8,128)(2,1)}, bf16[1536,384]{1,0:T(8,128)(2,1)S(1)}, u32[]{:S(2)}, u32[]{:S(2)}) collective-permute-start(bf16[1536,384]{1,0:T(8,128)(2,1)} %refs_0_.1), channel_id=1, source_target_pairs={{0,1},{1,2},{2,3},{3,0},{4,5},{5,6},{6,7},{7,4},{8,9},{9,10},{10,1... | collective-permute-start | bytes 3538952 | tf_op jit(solution)/shard_map/ppermute | solution.py:131
  3.5 32.0 %collective-permute-start.2 = (bf16[1536,384]{1,0:T(8,128)(2,1)}, bf16[1536,384]{1,0:T(8,128)(2,1)S(1)}, u32[]{:S(2)}, u32[]{:S(2)}) collective-permute-start(bf16[1536,384]{1,0:T(8,128)(2,1)} %refs_0_.1), channel_id=1, source_target_pairs={{0,4},{1,5},{2,6},{3,7},{4,0},{5,1},{6,2},{7,3},{8,12},{9,13},{10,... | collective-permute-start | bytes 3538952 | tf_op jit(solution)/shard_map/ppermute | solution.py:131
  8.1 0.7 copy-start
  35.5 27.0 %collective-permute-start.3 = (bf16[1536,384]{1,0:T(8,128)(2,1)S(1)}, bf16[1536,384]{1,0:T(8,128)(2,1)S(1)}, u32[]{:S(2)}, u32[]{:S(2)}) collective-permute-start(bf16[1536,384]{1,0:T(8,128)(2,1)S(1)} %get-tuple-element.39.refs_3_), channel_id=1, source_target_pairs={{0,1},{1,2},{2,3},{3,0},{4,5},{5,6},{6,7},{7,4},{8,9},{9,10},{10,1... | collective-permute-start | bytes 3538952 | tf_op jit(solution)/shard_map/ppermute | solution.py:131
  35.6 26.9 %collective-permute-start.5 = (bf16[1536,384]{1,0:T(8,128)(2,1)S(1)}, bf16[1536,384]{1,0:T(8,128)(2,1)S(1)}, u32[]{:S(2)}, u32[]{:S(2)}) collective-permute-start(bf16[1536,384]{1,0:T(8,128)(2,1)S(1)} %get-tuple-element.40.refs_2_), channel_id=1, source_target_pairs={{0,4},{1,5},{2,6},{3,7},{4,0},{5,1},{6,2},{7,3},{8,12},{9,13},{10,... | collective-permute-start | bytes 3538952 | tf_op jit(solution)/shard_map/ppermute | solution.py:131
  36.1 26.4 %collective-permute-start.4 = (bf16[1536,384]{1,0:T(8,128)(2,1)S(1)}, bf16[1536,384]{1,0:T(8,128)(2,1)S(1)}, u32[]{:S(2)}, u32[]{:S(2)}) collective-permute-start(bf16[1536,384]{1,0:T(8,128)(2,1)S(1)} %get-tuple-element.40.refs_2_), channel_id=1, source_target_pairs={{0,3},{1,0},{2,1},{3,2},{4,7},{5,4},{6,5},{7,6},{8,11},{9,8},{10,9... | collective-permute-start | bytes 3538952 | tf_op jit(solution)/shard_map/ppermute | solution.py:131
  39.3 11.0 %copy-start.1 = (bf16[1536,384]{1,0:T(8,128)(2,1)S(1)}, bf16[1536,384]{1,0:T(8,128)(2,1)}, u32[]{:S(2)}) copy-start(bf16[1536,384]{1,0:T(8,128)(2,1)} %refs_0_.1) | copy-start | bytes 3538948
  43.0 24.5 %collective-permute-start.10 = (bf16[48,384]{1,0:T(8,128)(2,1)S(1)}, bf16[48,384]{1,0:T(8,128)(2,1)S(1)}, u32[]{:S(2)}, u32[]{:S(2)}) collective-permute-start(bf16[48,384]{1,0:T(8,128)(2,1)S(1)} %get-tuple-element.43.refs_5_), channel_id=1, source_target_pairs={{8,0},{16,8},{24,16},{32,24},{40,32},{48,40},{56,48},{64,56},{72,6... | collective-permute-start | bytes 110600 | tf_op jit(solution)/shard_map/ppermute | solution.py:671
  44.3 23.2 %collective-permute-start.9 = (bf16[48,384]{1,0:T(8,128)(2,1)S(1)}, bf16[48,384]{1,0:T(8,128)(2,1)S(1)}, u32[]{:S(2)}, u32[]{:S(2)}) collective-permute-start(bf16[48,384]{1,0:T(8,128)(2,1)S(1)} %get-tuple-element.44.refs_6_), channel_id=1, source_target_pairs={{0,8},{8,16},{16,24},{24,32},{32,40},{40,48},{48,56},{56,64},{64,7... | collective-permute-start | bytes 110600 | tf_op jit(solution)/shard_map/ppermute | solution.py:668
  62.6 11.0 %collective-permute-start.7 = (bf16[512,384]{1,0:T(8,128)(2,1)S(1)}, bf16[512,384]{1,0:T(8,128)(2,1)S(1)}, u32[]{:S(2)}, u32[]{:S(2)}) collective-permute-start(bf16[512,384]{1,0:T(8,128)(2,1)S(1)} %get-tuple-element.47), channel_id=1, source_target_pairs={{0,4},{1,5},{2,6},{3,7},{4,0},{5,1},{6,2},{7,3},{8,12},{9,13},{10,... | collective-permute-start | bytes 1179656 | tf_op jit(solution)/shard_map/ppermute | solution.py:131
  63.7 9.9 %collective-permute-start.8 = (bf16[512,384]{1,0:T(8,128)(2,1)S(1)}, bf16[512,384]{1,0:T(8,128)(2,1)S(1)}, u32[]{:S(2)}, u32[]{:S(2)}) collective-permute-start(bf16[512,384]{1,0:T(8,128)(2,1)S(1)} %get-tuple-element.48), channel_id=1, source_target_pairs={{0,3},{1,0},{2,1},{3,2},{4,7},{5,4},{6,5},{7,6},{8,11},{9,8},{10,9... | collective-permute-start | bytes 1179656 | tf_op jit(solution)/shard_map/ppermute | solution.py:131
  67.4 9.0 %collective-permute-start.6 = (bf16[512,384]{1,0:T(8,128)(2,1)S(1)}, bf16[512,384]{1,0:T(8,128)(2,1)S(1)}, u32[]{:S(2)}, u32[]{:S(2)}) collective-permute-start(bf16[512,384]{1,0:T(8,128)(2,1)S(1)} %get-tuple-element.46.refs_5_), channel_id=1, source_target_pairs={{0,1},{1,2},{2,3},{3,0},{4,5},{5,6},{6,7},{7,4},{8,9},{9,10},{10,1... | collective-permute-start | bytes 1179656 | tf_op jit(solution)/shard_map/ppermute | solution.py:131
  68.5 23.2 %collective-permute-start.14 = (bf16[4,144,384]{2,1,0:T(8,128)(2,1)S(1)}, bf16[4,144,384]{2,1,0:T(8,128)(2,1)S(1)}, u32[]{:S(2)}, u32[]{:S(2)}) collective-permute-start(bf16[4,144,384]{2,1,0:T(8,128)(2,1)S(1)} %get-tuple-element.57), channel_id=1, source_target_pairs={{0,4},{1,5},{2,6},{3,7},{4,0},{5,1},{6,2},{7,3},{8,12},{9,13},{10,... | collective-permute-start | bytes 1327112 | tf_op jit(solution)/shard_map/ppermute | solution.py:131
  81.2 10.5 %collective-permute-start.13 = (bf16[6,144,256]{2,1,0:T(8,128)(2,1)S(1)}, bf16[6,144,256]{2,1,0:T(8,128)(2,1)S(1)}, u32[]{:S(2)}, u32[]{:S(2)}) collective-permute-start(bf16[6,144,256]{2,1,0:T(8,128)(2,1)S(1)} %get-tuple-element.56.refs_0_), channel_id=1, source_target_pairs={{0,4},{1,5},{2,6},{3,7},{4,0},{5,1},{6,2},{7,3},{8,12},{9,13},{10,... | collective-permute-start | bytes 1327112 | tf_op jit(solution)/shard_map/ppermute | solution.py:131
  81.7 10.0 %collective-permute-start.12 = (bf16[6,144,256]{2,1,0:T(8,128)(2,1)S(1)}, bf16[6,144,256]{2,1,0:T(8,128)(2,1)S(1)}, u32[]{:S(2)}, u32[]{:S(2)}) collective-permute-start(bf16[6,144,256]{2,1,0:T(8,128)(2,1)S(1)} %get-tuple-element.56.refs_0_), channel_id=1, source_target_pairs={{0,3},{1,0},{2,1},{3,2},{4,7},{5,4},{6,5},{7,6},{8,11},{9,8},{10,9... | collective-permute-start | bytes 1327112 | tf_op jit(solution)/shard_map/ppermute | solution.py:131
  82.2 12.5 %collective-permute-start.11 = (bf16[6,144,256]{2,1,0:T(8,128)(2,1)S(1)}, bf16[6,144,256]{2,1,0:T(8,128)(2,1)S(1)}, u32[]{:S(2)}, u32[]{:S(2)}) collective-permute-start(bf16[6,144,256]{2,1,0:T(8,128)(2,1)S(1)} %get-tuple-element.56.refs_0_), channel_id=1, source_target_pairs={{0,1},{1,2},{2,3},{3,0},{4,5},{5,6},{6,7},{7,4},{8,9},{9,10},{10,1... | collective-permute-start | bytes 1327112 | tf_op jit(solution)/shard_map/ppermute | solution.py:131
  94.9 18.6 %collective-permute-start.16 = (bf16[11,144,256]{2,1,0:T(8,128)(2,1)S(1)}, bf16[11,144,256]{2,1,0:T(8,128)(2,1)S(1)}, u32[]{:S(2)}, u32[]{:S(2)}) collective-permute-start(bf16[11,144,256]{2,1,0:T(8,128)(2,1)S(1)} %get-tuple-element.62), channel_id=1, source_target_pairs={{0,3},{1,0},{2,1},{3,2},{4,7},{5,4},{6,5},{7,6},{8,11},{9,8},{10,9... | collective-permute-start | bytes 2433032 | tf_op jit(solution)/shard_map/ppermute | solution.py:131
  95.5 20.5 %collective-permute-start.15 = (bf16[11,144,256]{2,1,0:T(8,128)(2,1)S(1)}, bf16[11,144,256]{2,1,0:T(8,128)(2,1)S(1)}, u32[]{:S(2)}, u32[]{:S(2)}) collective-permute-start(bf16[11,144,256]{2,1,0:T(8,128)(2,1)S(1)} %get-tuple-element.61.refs_5_), channel_id=1, source_target_pairs={{0,1},{1,2},{2,3},{3,0},{4,5},{5,6},{6,7},{7,4},{8,9},{9,10},{10,1... | collective-permute-start | bytes 2433032 | tf_op jit(solution)/shard_map/ppermute | solution.py:131
  97.2 14.1 %collective-permute-start.17 = (bf16[6,144,256]{2,1,0:T(8,128)(2,1)S(1)}, bf16[6,144,256]{2,1,0:T(8,128)(2,1)S(1)}, u32[]{:S(2)}, u32[]{:S(2)}) collective-permute-start(bf16[6,144,256]{2,1,0:T(8,128)(2,1)S(1)} %get-tuple-element.63), channel_id=1, source_target_pairs={{0,4},{1,5},{2,6},{3,7},{4,0},{5,1},{6,2},{7,3},{8,12},{9,13},{10,... | collective-permute-start | bytes 1327112 | tf_op jit(solution)/shard_map/ppermute | solution.py:131
  97.6 8.7 %collective-permute-start.18 = (f32[32,512]{1,0:T(8,128)S(1)}, f32[32,512]{1,0:T(8,128)S(1)}, u32[]{:S(2)}, u32[]{:S(2)}) collective-permute-start(f32[32,512]{1,0:T(8,128)S(1)} %get-tuple-element.65), channel_id=1, source_target_pairs={{0,8},{8,16},{16,24},{24,32},{32,40},{40,48},{48,56},{56,64},{64,7... | collective-permute-start | bytes 196616 | tf_op jit(solution)/shard_map/ppermute | solution.py:668
  102.5 7.7 %collective-permute-start.19 = (f32[32,512]{1,0:T(8,128)S(1)}, f32[32,512]{1,0:T(8,128)S(1)}, u32[]{:S(2)}, u32[]{:S(2)}) collective-permute-start(f32[32,512]{1,0:T(8,128)S(1)} %get-tuple-element.60.refs_4_), channel_id=1, source_target_pairs={{8,0},{16,8},{24,16},{32,24},{40,32},{48,40},{56,48},{64,56},{72,6... | collective-permute-start | bytes 196616 | tf_op jit(solution)/shard_map/ppermute | solution.py:671
  116.0 10.6 %collective-permute-start.20 = (bf16[5,144,256]{2,1,0:T(8,128)(2,1)S(1)}, bf16[5,144,256]{2,1,0:T(8,128)(2,1)S(1)}, u32[]{:S(2)}, u32[]{:S(2)}) collective-permute-start(bf16[5,144,256]{2,1,0:T(8,128)(2,1)S(1)} %get-tuple-element.67), channel_id=1, source_target_pairs={{0,1},{1,2},{2,3},{3,0},{4,5},{5,6},{6,7},{7,4},{8,9},{9,10},{10,1... | collective-permute-start | bytes 1105928 | tf_op jit(solution)/shard_map/ppermute | solution.py:131
  116.0 10.6 %collective-permute-start.21 = (bf16[5,144,256]{2,1,0:T(8,128)(2,1)S(1)}, bf16[5,144,256]{2,1,0:T(8,128)(2,1)S(1)}, u32[]{:S(2)}, u32[]{:S(2)}) collective-permute-start(bf16[5,144,256]{2,1,0:T(8,128)(2,1)S(1)} %get-tuple-element.68), channel_id=1, source_target_pairs={{0,3},{1,0},{2,1},{3,2},{4,7},{5,4},{6,5},{7,6},{8,11},{9,8},{10,9... | collective-permute-start | bytes 1105928 | tf_op jit(solution)/shard_map/ppermute | solution.py:131
  119.3 4.6 %collective-permute-start.22 = (bf16[4,32,384]{2,1,0:T(8,128)(2,1)S(1)}, bf16[4,32,384]{2,1,0:T(8,128)(2,1)S(1)}, u32[]{:S(2)}, u32[]{:S(2)}) collective-permute-start(bf16[4,32,384]{2,1,0:T(8,128)(2,1)S(1)} %get-tuple-element.66.refs_3_), channel_id=1, source_target_pairs={{0,4},{1,5},{2,6},{3,7},{4,0},{5,1},{6,2},{7,3},{8,12},{9,13},{10,... | collective-permute-start | bytes 294920 | tf_op jit(solution)/shard_map/ppermute | solution.py:131
  123.9 5.6 %collective-permute-start.23 = (bf16[32,384]{1,0:T(8,128)(2,1)S(1)}, bf16[32,384]{1,0:T(8,128)(2,1)S(1)}, u32[]{:S(2)}, u32[]{:S(2)}) collective-permute-start(bf16[32,384]{1,0:T(8,128)(2,1)S(1)} %get-tuple-element.71), channel_id=1, source_target_pairs={{0,3},{1,0},{2,1},{3,2},{4,7},{5,4},{6,5},{7,6},{8,11},{9,8},{10,9... | collective-permute-start | bytes 73736 | tf_op jit(solution)/shard_map/ppermute | solution.py:131
  124.0 5.6 %collective-permute-start.24 = (bf16[32,384]{1,0:T(8,128)(2,1)S(1)}, bf16[32,384]{1,0:T(8,128)(2,1)S(1)}, u32[]{:S(2)}, u32[]{:S(2)}) collective-permute-start(bf16[32,384]{1,0:T(8,128)(2,1)S(1)} %get-tuple-element.72), channel_id=1, source_target_pairs={{0,2},{1,3},{2,0},{3,1},{4,6},{5,7},{6,4},{7,5},{8,10},{9,11},{10,... | collective-permute-start | bytes 73736 | tf_op jit(solution)/shard_map/ppermute | solution.py:131
  124.9 5.6 %collective-permute-start.25 = (bf16[32,384]{1,0:T(8,128)(2,1)S(1)}, bf16[32,384]{1,0:T(8,128)(2,1)S(1)}, u32[]{:S(2)}, u32[]{:S(2)}) collective-permute-start(bf16[32,384]{1,0:T(8,128)(2,1)S(1)} %get-tuple-element.73), channel_id=1, source_target_pairs={{0,1},{1,2},{2,3},{3,0},{4,5},{5,6},{6,7},{7,4},{8,9},{9,10},{10,1... | collective-permute-start | bytes 73736 | tf_op jit(solution)/shard_map/ppermute | solution.py:131
